TPU v7x, 32 devices: a whole 2x2x4 slice. The times are simulated.
32 devices in a mesh: rows: 16 (over z, y, core), heads: 2 (over x).
Axes of the slice: x: 2, y: 2, z: 4, core: 2. Of those that a mesh axis runs over, the one named last changes fastest.
Arguments:
- tokens: bfloat16 [8192, 1152], P(('rows', 'heads')), may hold values from -6 to 6
- cond: bfloat16 [64, 1152], P('rows'), may hold values from -6 to 6
- image_of: int32 [16, 512], P('rows'), may hold values from 0 to 63, as said below
- grid_row: int32 [16, 512], P('rows'), may hold values from 0 to 63, as said below
- grid_col: int32 [16, 512], P('rows'), may hold values from 0 to 15, as said below
- ada_weight: bfloat16 [2, 1152, 6912], P(None, 'rows', 'heads'), may hold values from -0.1875 to 0.1875
- ada_bias: bfloat16 [2, 6912], P(None, 'heads'), may hold values from -3 to 3
- qkv_weight: bfloat16 [2, 1152, 3456], P(None, 'rows', 'heads'), may hold values from -0.1875 to 0.1875
- qkv_bias: bfloat16 [2, 3456], P(None, 'heads'), may hold values from -3 to 3
- proj_weight: bfloat16 [2, 1152, 1152], P(None, 'heads', 'rows'), may hold values from -2 to 2
- gu_weight: bfloat16 [2, 1152, 2, 3072], P(None, 'rows', None, 'heads'), may hold values from -0.1875 to 0.1875
- down_weight: bfloat16 [2, 3072, 1152], P(None, 'heads', 'rows'), may hold values from -0.109375 to 0.109375
- cotangent: bfloat16 [8192, 1152], P(('rows', 'heads')), may hold values from -6 to 6
Outputs:
- block_out: bfloat16 [8192, 1152], P(('rows', 'heads'))
- tokens_grad: float32 [8192, 1152], P(('rows', 'heads'))
- cond_grad: float32 [64, 1152], P('rows')
- ada_grad: float32 [2, 1152, 6912], P(None, 'rows', 'heads')
- ada_bias_grad: float32 [2, 6912], P(None, 'heads')
- qkv_grad: float32 [2, 1152, 3456], P(None, 'rows', 'heads')
- qkv_bias_grad: float32 [2, 3456], P(None, 'heads')
- proj_grad: float32 [2, 1152, 1152], P(None, 'heads', 'rows')
- gu_grad: float32 [2, 1152, 2, 3072], P(None, 'rows', None, 'heads')
- down_grad: float32 [2, 3072, 1152], P(None, 'heads', 'rows')
Inputs may be any that keep to these rules, and one draw needn't show every extreme that they name: `image_of`: packed row r holds 4 images numbered 4 * r to 4 * r + 3 in increasing order, each a run of consecutive tokens; every row has one image of 256 tokens and one of 64 tokens, and its other images lie between these lengths. `grid_row`: the token's place within its image divided by the image's width, rounded down; each image has one width from 4 to 16, and in every row the image of 256 tokens is 4 wide. `grid_col`: the token's place within its image modulo the image's width; in every row the image of 64 tokens is 16 wide.
All inputs are finite; a program needn't handle non-finite values.
Results may differ from a plain program's by a relative error of at most 0.03.
Values may be sent and summed in bfloat16 or wider, within the bound.
A program may use at most 256 MiB of HBM per device.

v0:
```python
import jax
import jax.numpy as jnp
from jax import lax
from jax.sharding import PartitionSpec as P

HD = 72


epsilon = 1e-06
theta_base = 10000.0
highest = lax.Precision.HIGHEST


def normalize(values):
    center = values - jnp.mean(values, axis=-1, keepdims=True)
    inverse = lax.rsqrt(jnp.mean(center * center, axis=-1, keepdims=True) + epsilon)
    return (center * inverse, inverse)


def norm_back(incoming, normed, inverse):
    return inverse * (
        incoming
        - jnp.mean(incoming, axis=-1, keepdims=True)
        - normed * jnp.mean(incoming * normed, axis=-1, keepdims=True)
    )


def lead_dot(operand, other):
    return lax.dot_general(
        operand, other, (((0,), (0,)), ((), ())), preferred_element_type=jnp.float32
    )


def tail_dot(operand, other):
    return lax.dot_general(
        operand, other, (((1,), (1,)), ((), ())), preferred_element_type=jnp.float32
    )


def angles(coords, quarter):
    frequency = theta_base ** (-jnp.arange(quarter, dtype=jnp.float32) / quarter)
    return coords.astype(jnp.float32)[..., None] * frequency


def rotate_pair(section, angle):
    half_width = section.shape[-1] // 2
    lower_half = section[..., :half_width]
    upper_half = section[..., half_width:]
    cosine = jnp.cos(angle)
    sine_term = jnp.sin(angle)
    return jnp.concatenate(
        [
            lower_half * cosine - upper_half * sine_term,
            upper_half * cosine + lower_half * sine_term,
        ],
        axis=-1,
    )


def rotary(vectors, row_angle, col_angle):
    half_width = vectors.shape[-1] // 2
    return jnp.concatenate(
        [
            rotate_pair(vectors[..., :half_width], row_angle[:, :, None, :]),
            rotate_pair(vectors[..., half_width:], col_angle[:, :, None, :]),
        ],
        axis=-1,
    )


def masked_scores(queries, key_rows, image_ids):
    score_scale = queries.shape[-1] ** (-0.5)
    scores = (
        jnp.einsum("qhe,khe->hqk", queries, key_rows, preferred_element_type=jnp.float32)
        * score_scale
    )
    same_image = image_ids[:, None] == image_ids[None, :]
    return jnp.where(same_image[None], scores, -1e30)


def attend(row_data):
    queries, key_rows, value_rows, image_ids = row_data
    scores = masked_scores(queries, key_rows, image_ids)
    maximum = jnp.max(scores, axis=-1, keepdims=True)
    scaled_exp = jnp.exp(scores - maximum)
    denominator = jnp.sum(scaled_exp, axis=-1, keepdims=True)
    weights = (scaled_exp / denominator).astype(jnp.bfloat16)
    attended = jnp.einsum("hqk,khe->qhe", weights, value_rows, preferred_element_type=jnp.float32)
    return (attended.astype(jnp.bfloat16), (maximum + jnp.log(denominator))[..., 0])


def attend_back(row_data):
    queries, key_rows, value_rows, image_ids, logsum, grad_attended = row_data
    score_scale = queries.shape[-1] ** (-0.5)
    probs = jnp.exp(masked_scores(queries, key_rows, image_ids) - logsum[..., None])
    weights = probs.astype(jnp.bfloat16)
    grad_value = jnp.einsum(
        "hqk,qhe->khe", weights, grad_attended, preferred_element_type=jnp.float32
    )
    grad_probs = jnp.einsum(
        "qhe,khe->hqk", grad_attended, value_rows, preferred_element_type=jnp.float32
    )
    inner_sum = jnp.sum(probs * grad_probs, axis=-1, keepdims=True)
    grad_scores = (probs * (grad_probs - inner_sum)).astype(jnp.bfloat16)
    grad_query = (
        jnp.einsum("hqk,khe->qhe", grad_scores, key_rows, preferred_element_type=jnp.float32)
        * score_scale
    )
    grad_key = (
        jnp.einsum("hqk,qhe->khe", grad_scores, queries, preferred_element_type=jnp.float32)
        * score_scale
    )
    return (grad_query, grad_key, grad_value)


def spread(values):
    return lax.all_gather(values, "heads", axis=0, tiled=True)


def spread_grad(values):
    return lax.all_gather(values, "heads", axis=0, tiled=True)


def collect(operand, other, own_rows):

    def partial_sum(begin_at, length):
        return jnp.dot(operand, other, preferred_element_type=jnp.float32)

    return lax.psum_scatter(
        partial_sum(jnp.int32(0), lax.axis_size("heads") * own_rows),
        "heads",
        scatter_dimension=0,
        tiled=True,
    )


def collect_back(operand, other, own_rows):

    def partial_sum(begin_at, length):
        return tail_dot(operand, other)

    return lax.psum_scatter(
        partial_sum(jnp.int32(0), own_rows * lax.axis_size("heads")).astype(jnp.bfloat16),
        "heads",
        scatter_dimension=0,
        tiled=True,
    ).astype(jnp.float32)


def block_forward(residual, token_mods, qkv_full, qkv_b, proj_full, gu_full, down_full, geometry):
    image_ids, row_angle, col_angle = geometry
    shift_attn, scale_attn, gate_attn, shift_mlp, scale_mlp, gate_mlp = jnp.split(
        token_mods, 6, axis=1
    )
    own_rows = residual.shape[0]
    count_rows, row_len = image_ids.shape
    normed_attn, inverse_attn = normalize(residual)
    input_attn = spread((normed_attn * (1.0 + scale_attn) + shift_attn).astype(jnp.bfloat16))
    packed = jnp.dot(input_attn, qkv_full, preferred_element_type=jnp.float32) + qkv_b
    heads_here = packed.shape[1] // (3 * HD)
    packed = packed.reshape(count_rows, row_len, heads_here, 3, HD)
    queries = rotary(packed[:, :, :, 0], row_angle, col_angle).astype(jnp.bfloat16)
    key_rows = rotary(packed[:, :, :, 1], row_angle, col_angle).astype(jnp.bfloat16)
    value_rows = packed[:, :, :, 2].astype(jnp.bfloat16)
    attended, logsum = lax.map(attend, (queries, key_rows, value_rows, image_ids))
    attended = attended.reshape(count_rows * row_len, heads_here * HD)
    branch = collect(attended, proj_full, own_rows)
    middle = residual + gate_attn * branch
    normed_mlp, inverse_mlp = normalize(middle)
    input_mlp = spread((normed_mlp * (1.0 + scale_mlp) + shift_mlp).astype(jnp.bfloat16))
    hidden_width = gu_full.shape[2]
    gate_up = jnp.dot(
        input_mlp,
        gu_full.reshape(gu_full.shape[0], 2 * hidden_width),
        preferred_element_type=jnp.float32,
    )
    gate_part = gate_up[:, :hidden_width]
    up_part = gate_up[:, hidden_width:]
    hidden = (jax.nn.silu(gate_part) * up_part).astype(jnp.bfloat16)
    mlp_out = collect(hidden, down_full, own_rows)
    result = middle + gate_mlp * mlp_out
    stored = (
        normed_attn,
        inverse_attn,
        input_attn,
        queries,
        key_rows,
        value_rows,
        logsum,
        attended,
        branch,
        normed_mlp,
        inverse_mlp,
        input_mlp,
        gate_part,
        up_part,
        hidden,
        mlp_out,
    )
    return (result, stored)


def block_backward(incoming, token_mods, stored, qkv_full, proj_full, gu_full, down_full, geometry):
    image_ids, row_angle, col_angle = geometry
    shift_attn, scale_attn, gate_attn, shift_mlp, scale_mlp, gate_mlp = jnp.split(
        token_mods, 6, axis=1
    )
    (
        normed_attn,
        inverse_attn,
        input_attn,
        queries,
        key_rows,
        value_rows,
        logsum,
        attended,
        branch,
        normed_mlp,
        inverse_mlp,
        input_mlp,
        gate_part,
        up_part,
        hidden,
        mlp_out,
    ) = stored
    own_rows = incoming.shape[0]
    count_rows, row_len = image_ids.shape
    grad_mlp = (gate_mlp * incoming).astype(jnp.bfloat16)
    grad_gate_mlp = incoming * mlp_out
    gathered_mlp = spread_grad(grad_mlp)
    down_grad = lead_dot(hidden, gathered_mlp)
    grad_hidden = tail_dot(gathered_mlp, down_full)
    logistic = jax.nn.sigmoid(gate_part)
    grad_gate_part = grad_hidden * up_part * logistic * (1.0 + gate_part * (1.0 - logistic))
    grad_up_part = grad_hidden * gate_part * logistic
    grad_gate_up = jnp.concatenate([grad_gate_part, grad_up_part], axis=1).astype(jnp.bfloat16)
    gu_flat = gu_full.reshape(gu_full.shape[0], -1)
    gu_grad = lead_dot(input_mlp, grad_gate_up).reshape(gu_full.shape)
    grad_input_mlp = collect_back(grad_gate_up, gu_flat, own_rows)
    grad_middle = incoming + norm_back(grad_input_mlp * (1.0 + scale_mlp), normed_mlp, inverse_mlp)
    grad_branch = (gate_attn * grad_middle).astype(jnp.bfloat16)
    grad_gate_attn = grad_middle * branch
    heads_here = queries.shape[2]
    gathered_branch = spread_grad(grad_branch)
    proj_grad = lead_dot(attended, gathered_branch)
    grad_attended = tail_dot(gathered_branch, proj_full).astype(jnp.bfloat16)
    grad_attended = grad_attended.reshape(count_rows, row_len, heads_here, HD)
    grad_query, grad_key, grad_value = lax.map(
        attend_back, (queries, key_rows, value_rows, image_ids, logsum, grad_attended)
    )
    grad_query = rotary(grad_query, -row_angle, -col_angle)
    grad_key = rotary(grad_key, -row_angle, -col_angle)
    grad_packed = (
        jnp.stack([grad_query, grad_key, grad_value], axis=3)
        .reshape(count_rows * row_len, heads_here * 3 * HD)
        .astype(jnp.bfloat16)
    )
    qkv_bias_grad = jnp.sum(grad_packed, axis=0, dtype=jnp.float32)
    qkv_grad = lead_dot(input_attn, grad_packed)
    grad_input_attn = collect_back(grad_packed, qkv_full, own_rows)
    grad_input = grad_middle + norm_back(
        grad_input_attn * (1.0 + scale_attn), normed_attn, inverse_attn
    )
    grad_mods = jnp.concatenate(
        [
            grad_input_attn,
            grad_input_attn * normed_attn,
            grad_gate_attn,
            grad_input_mlp,
            grad_input_mlp * normed_mlp,
            grad_gate_mlp,
        ],
        axis=1,
    )
    return (grad_input, grad_mods, (qkv_grad, qkv_bias_grad, proj_grad, gu_grad, down_grad))


def shards(
    tokens,
    cond,
    image_of,
    grid_row,
    grid_col,
    ada_weight,
    ada_bias,
    qkv_weight,
    qkv_bias,
    proj_weight,
    gu_weight,
    down_weight,
    cotangent,
):
    own_rows = tokens.shape[0]
    image_count = cond.shape[0]
    block_count = qkv_weight.shape[0]
    image_ids = image_of - lax.axis_index("rows") * image_count
    quarter = HD // 4
    geometry = (image_ids, angles(grid_row, quarter), angles(grid_col, quarter))
    own_images = lax.dynamic_slice_in_dim(
        image_ids.reshape(-1), lax.axis_index("heads") * own_rows, own_rows
    )
    picker = (own_images[:, None] == jnp.arange(image_count, dtype=jnp.int32)[None, :]).astype(
        jnp.float32
    )
    gathered = (
        lax.all_gather(ada_weight, "rows", axis=1, tiled=True),
        lax.all_gather(qkv_weight, "rows", axis=1, tiled=True),
        lax.all_gather(proj_weight, "rows", axis=2, tiled=True),
        lax.all_gather(gu_weight, "rows", axis=1, tiled=True),
        lax.all_gather(down_weight, "rows", axis=2, tiled=True),
    )
    ada_full, qkv_full, proj_full, gu_full, down_full = gathered
    cond_wide = cond.astype(jnp.float32)
    cond_act = jax.nn.silu(cond_wide).astype(jnp.bfloat16)
    mod_local = (
        jnp.einsum("id,bdc->bic", cond_act, ada_full, preferred_element_type=jnp.float32)
        + ada_bias.astype(jnp.float32)[:, None, :]
    )
    modulation = lax.all_gather(mod_local, "heads", axis=2, tiled=True)
    token_mods = [
        jnp.dot(picker, modulation[block_index], precision=highest)
        for block_index in range(block_count)
    ]
    residual = tokens.astype(jnp.float32)
    stored_all = []
    for block_index in range(block_count):
        residual, stored = block_forward(
            residual,
            token_mods[block_index],
            qkv_full[block_index],
            qkv_bias[block_index].astype(jnp.float32),
            proj_full[block_index],
            gu_full[block_index],
            down_full[block_index],
            geometry,
        )
        stored_all.append(stored)
    block_out = residual.astype(jnp.bfloat16)
    regathered = (
        lax.all_gather(ada_weight, "rows", axis=1, tiled=True),
        lax.all_gather(qkv_weight, "rows", axis=1, tiled=True),
        lax.all_gather(proj_weight, "rows", axis=2, tiled=True),
        lax.all_gather(gu_weight, "rows", axis=1, tiled=True),
        lax.all_gather(down_weight, "rows", axis=2, tiled=True),
    )
    ada_full, qkv_full, proj_full, gu_full, down_full = regathered
    incoming = cotangent.astype(jnp.float32)
    mod_grads = [None] * block_count
    block_grads = [None] * block_count
    for block_index in reversed(range(block_count)):
        incoming, grad_mods, gradients = block_backward(
            incoming,
            token_mods[block_index],
            stored_all[block_index],
            qkv_full[block_index],
            proj_full[block_index],
            gu_full[block_index],
            down_full[block_index],
            geometry,
        )
        mod_grads[block_index] = lax.dot_general(
            picker, grad_mods, (((0,), (0,)), ((), ())), precision=highest
        )
        block_grads[block_index] = gradients
    image_grads = lax.psum_scatter(
        jnp.stack(mod_grads).astype(jnp.bfloat16), "heads", scatter_dimension=2, tiled=True
    )
    ada_grad = jnp.einsum("id,bic->bdc", cond_act, image_grads, preferred_element_type=jnp.float32)
    ada_bias_grad = jnp.sum(image_grads, axis=1, dtype=jnp.float32)
    cond_partial = jnp.einsum(
        "bic,bdc->id", image_grads, ada_full, preferred_element_type=jnp.float32
    )
    cond_total = lax.psum(cond_partial.astype(jnp.bfloat16), "heads").astype(jnp.float32)
    logistic = jax.nn.sigmoid(cond_wide)
    cond_grad = cond_total * logistic * (1.0 + cond_wide * (1.0 - logistic))
    qkv_grads = jnp.stack([item[0] for item in block_grads])
    qkv_bias_grads = jnp.stack([item[1] for item in block_grads])
    proj_grads = jnp.stack([item[2] for item in block_grads])
    gu_grads = jnp.stack([item[3] for item in block_grads])
    down_grads = jnp.stack([item[4] for item in block_grads])
    summed = (
        lax.psum_scatter(
            ada_grad.astype(jnp.bfloat16), "rows", scatter_dimension=1, tiled=True
        ).astype(jnp.float32),
        lax.psum_scatter(
            qkv_grads.astype(jnp.bfloat16), "rows", scatter_dimension=1, tiled=True
        ).astype(jnp.float32),
        lax.psum_scatter(
            proj_grads.astype(jnp.bfloat16), "rows", scatter_dimension=2, tiled=True
        ).astype(jnp.float32),
        lax.psum_scatter(
            gu_grads.astype(jnp.bfloat16), "rows", scatter_dimension=1, tiled=True
        ).astype(jnp.float32),
        lax.psum_scatter(
            down_grads.astype(jnp.bfloat16), "rows", scatter_dimension=2, tiled=True
        ).astype(jnp.float32),
    )
    bias_sums = lax.psum((ada_bias_grad, qkv_bias_grads), "rows")
    return (
        block_out,
        incoming,
        cond_grad,
        summed[0],
        bias_sums[0],
        summed[1],
        bias_sums[1],
        summed[2],
        summed[3],
        summed[4],
    )


def solution(mesh):
    in_specs = (
        P(("rows", "heads"), None),
        P("rows", None),
        P("rows", None),
        P("rows", None),
        P("rows", None),
        P(None, "rows", "heads"),
        P(None, "heads"),
        P(None, "rows", "heads"),
        P(None, "heads"),
        P(None, "heads", "rows"),
        P(None, "rows", None, "heads"),
        P(None, "heads", "rows"),
        P(("rows", "heads"), None),
    )
    out_specs = (
        P(("rows", "heads"), None),
        P(("rows", "heads"), None),
        P("rows", None),
        P(None, "rows", "heads"),
        P(None, "heads"),
        P(None, "rows", "heads"),
        P(None, "heads"),
        P(None, "heads", "rows"),
        P(None, "rows", None, "heads"),
        P(None, "heads", "rows"),
    )
    return jax.shard_map(shards, mesh=mesh, in_specs=in_specs, out_specs=out_specs, check_vma=False)
```

profile of v0, /device:TPU:0, one launch (start us, length us, event | category | flops | bytes accessed | tf_op | source)
XLA Modules:
  0.0 1829.2 jit_solution(16813667854142064118)
XLA Ops:
  10.0 124.5 %all-gather.14.cloned.1.call-done = bf16[2,1152,3456]{2,1,0:T(8,128)(2,1)} async-done(((bf16[2,72,3456]{2,1,0:T(8,128)(2,1)}), bf16[2,1152,3456]{2,1,0:T(8,128)(2,1)}) %all-gather.14.cloned.1.call-update) | async-done | bytes 15925264 | tf_op jit(solution)/shard_map/all_gather | solution.py:306
  158.1 50.9 %all-gather.18.cloned.1.call-done = bf16[2,1152,1728]{2,1,0:T(8,128)(2,1)} async-done(((bf16[2,72,1728]{2,1,0:T(8,128)(2,1)}), bf16[2,1152,1728]{2,1,0:T(8,128)(2,1)}) %all-gather.18.cloned.1.call-update) | async-done | bytes 7962640 | tf_op jit(solution)/shard_map/all_gather | solution.py:307
  209.0 23.2 %all-gather.16.cloned.1.call-done = bf16[512,1152]{1,0:T(8,128)(2,1)} async-done(((bf16[256,1152]{1,0:T(8,128)(2,1)}), bf16[512,1152]{1,0:T(8,128)(2,1)}) %all-gather.16.cloned.1.call-update) | async-done | bytes 1179664 | tf_op jit(solution)/shard_map/all_gather | solution.py:117
  245.5 33.6 %all-gather.20.cloned.1.call-done = bf16[2,576,1152]{1,2,0:T(8,128)(2,1)} async-done(((bf16[2,576,72]{1,2,0:T(8,128)(2,1)}), bf16[2,576,1152]{1,2,0:T(8,128)(2,1)}) %all-gather.20.cloned.1.call-update) | async-done | bytes 2654224 | tf_op jit(solution)/shard_map/all_gather | solution.py:308
  283.6 32.6 %reduce-scatter.16.cloned.1.call-done = f32[256,1152]{1,0:T(8,128)} async-done(((f32[512,1152]{1,0:T(8,128)}), f32[256,1152]{1,0:T(8,128)}) %reduce-scatter.16.cloned.1.call-update) | async-done | bytes 1179664 | tf_op jit(solution)/shard_map/reduce_scatter | solution.py:129
  322.1 107.2 %all-gather.24.cloned.1.call-done = bf16[2,1152,2,1536]{3,2,1,0:T(2,128)(2,1)} async-done(((bf16[2,72,2,1536]{3,2,1,0:T(2,128)(2,1)}), bf16[2,1152,2,1536]{3,2,1,0:T(2,128)(2,1)}) %all-gather.24.cloned.1.call-update) | async-done | bytes 14155792 | tf_op jit(solution)/shard_map/all_gather | solution.py:309
  429.3 12.3 fusion.132
  462.9 58.8 %all-gather.26.cloned.1.call-done = bf16[2,1536,1152]{1,2,0:T(8,128)(2,1)} async-done(((bf16[2,1536,72]{1,2,0:T(8,128)(2,1)}), bf16[2,1536,1152]{1,2,0:T(8,128)(2,1)}) %all-gather.26.cloned.1.call-update) | async-done | bytes 7077904 | tf_op jit(solution)/shard_map/all_gather | solution.py:310
  532.6 28.1 %reduce-scatter.18.cloned.1.call-done = f32[256,1152]{1,0:T(8,128)} async-done(((f32[512,1152]{1,0:T(8,128)}), f32[256,1152]{1,0:T(8,128)}) %reduce-scatter.18.cloned.1.call-update) | async-done | bytes 1179664 | tf_op jit(solution)/shard_map/reduce_scatter | solution.py:129
  565.9 22.7 %all-gather.28.cloned.1.call-done = bf16[512,1152]{1,0:T(8,128)(2,1)} async-done(((bf16[256,1152]{1,0:T(8,128)(2,1)}), bf16[512,1152]{1,0:T(8,128)(2,1)}) %all-gather.28.cloned.1.call-update) | async-done | bytes 1179664 | tf_op jit(solution)/shard_map/all_gather | solution.py:117
  606.2 34.8 %reduce-scatter.20.cloned.1.call-done = f32[256,1152]{1,0:T(8,128)} async-done(((f32[512,1152]{1,0:T(8,128)}), f32[256,1152]{1,0:T(8,128)}) %reduce-scatter.20.cloned.1.call-update) | async-done | bytes 1179664 | tf_op jit(solution)/shard_map/reduce_scatter | solution.py:129
  656.2 14.0 all-gather.30.cloned.1.call-done
  670.2 10.3 fusion.138
  680.5 14.7 all-gather.32.cloned.1.call-done
  717.3 15.5 reduce-scatter.24.cloned.1.call-done
  734.6 35.0 %reduce-scatter.22.cloned.1.call-done = f32[256,1152]{1,0:T(8,128)} async-done(((f32[512,1152]{1,0:T(8,128)}), f32[256,1152]{1,0:T(8,128)}) %reduce-scatter.22.cloned.1.call-update) | async-done | bytes 1179664 | tf_op jit(solution)/shard_map/reduce_scatter | solution.py:129
  775.2 22.1 %all-gather.34.cloned.1.call-done = bf16[512,1152]{1,0:T(8,128)(2,1)} async-done(((bf16[256,1152]{1,0:T(8,128)(2,1)}), bf16[512,1152]{1,0:T(8,128)(2,1)}) %all-gather.34.cloned.1.call-update) | async-done | bytes 1179664 | tf_op jit(solution)/shard_map/all_gather | solution.py:121
  822.6 21.6 %reduce-scatter.26.cloned.1.call-done = bf16[256,1152]{1,0:T(8,128)(2,1)} async-done(((bf16[512,1152]{1,0:T(8,128)(2,1)}), bf16[256,1152]{1,0:T(8,128)(2,1)}) %reduce-scatter.26.cloned.1.call-update) | async-done | bytes 589840 | tf_op jit(solution)/shard_map/reduce_scatter | solution.py:142
  852.5 22.9 %all-gather.36.cloned.1.call-done = bf16[512,1152]{1,0:T(8,128)(2,1)} async-done(((bf16[256,1152]{1,0:T(8,128)(2,1)}), bf16[512,1152]{1,0:T(8,128)(2,1)}) %all-gather.36.cloned.1.call-update) | async-done | bytes 1179664 | tf_op jit(solution)/shard_map/all_gather | solution.py:121
  892.8 21.8 %reduce-scatter.28.cloned.1.call-done = bf16[256,1152]{1,0:T(8,128)(2,1)} async-done(((bf16[512,1152]{1,0:T(8,128)(2,1)}), bf16[256,1152]{1,0:T(8,128)(2,1)}) %reduce-scatter.28.cloned.1.call-update) | async-done | bytes 589840 | tf_op jit(solution)/shard_map/reduce_scatter | solution.py:142
  928.0 14.9 all-gather.38.cloned.1.call-done
  1017.4 18.4 %copy.79 = bf16[2,1536,1152]{1,0,2:T(2,128)(2,1)} copy(bf16[2,1536,1152]{2,1,0:T(8,128)(2,1)} %pad_maximum_fusion.2) | data formatting | bytes 14155776 | tf_op jit(solution)/shard_map/stack | solution.py:380
  1049.4 23.1 %copy.75 = bf16[2,1152,1728]{2,0,1:T(2,128)(2,1)} copy(bf16[2,1152,1728]{1,2,0:T(8,128)(2,1)} %pad_maximum_fusion.1) | data formatting | bytes 15925248 | tf_op jit(solution)/shard_map/stack | solution.py:376
  1094.8 41.1 %copy.74 = bf16[2,1152,3456]{2,0,1:T(2,128)(2,1)} copy(bf16[2,1152,3456]{1,2,0:T(8,128)(2,1)} %fusion) | data formatting | bytes 31850496 | tf_op jit(solution)/shard_map/convert_element_type | solution.py:383
  1144.8 16.9 stack_reshape.9
  1168.9 16.6 stack_reshape.8
  1185.5 17.0 copy_bitcast_fusion
  1202.5 22.6 %reshape.716 = bf16[1152,6144]{1,0:T(8,128)(2,1)} reshape(bf16[1152,2,2,1536]{3,2,1,0:T(2,128)(2,1)} %copy_bitcast_fusion) | data formatting | bytes 28311552
  1229.7 10.0 fusion.34
  1244.8 64.7 %all-reduce.4 = (f32[2,3456]{1,0:T(2,128)}, f32[2,1728]{1,0:T(2,128)}) all-reduce(f32[2,3456]{1,0:T(2,128)S(1)} %convert_reduce_fusion.3, f32[2,1728]{1,0:T(2,128)S(1)} %pad_maximum_fusion.15), channel_id=1, replica_groups=mesh['rows'=16,'heads'=2] {'rows'}, use_global_device_ids=true, to_apply=%region_34.35 | all-reduce | flops 10368 | bytes 82944 | tf_op jit(solution)/shard_map/psum | solution.py:398
  1310.1 357.6 %all-reduce.11.cloned.1.call-done = (bf16[2,1152,3456]{2,0,1:T(2,128)(2,1)}, bf16[2,1152,1728]{2,0,1:T(2,128)(2,1)}, bf16[2,576,1152]{1,0,2:T(2,128)(2,1)}) async-done(((bf16[2,1152,3456]{2,0,1:T(2,128)(2,1)}, bf16[2,1152,1728]{2,0,1:T(2,128)(2,1)}, bf16[2,576,1152]{1,0,2:T(2,128)(2,1)}), (bf16[2,1152,3456]{2,0,1:T(2,128)(2,1)}, bf16[2,1152,1728]{2,0,1:T(2,128)(2,1)}, ...) | async-done | bytes 26542096
  1675.3 142.3 %reduce-scatter.34.cloned.1.call-done = bf16[72,6144]{1,0:T(8,128)(2,1)} async-done(((bf16[1152,6144]{1,0:T(8,128)(2,1)}), bf16[72,6144]{1,0:T(8,128)(2,1)}) %reduce-scatter.34.cloned.1.call-update) | async-done | bytes 884752
  (469 shorter events, 360.3 us)
Async XLA Ops:
  7.2 127.3 %copy-start.75 = (bf16[4,1152]{1,0:T(4,128)(2,1)S(1)}, bf16[4,1152]{1,0:T(4,128)(2,1)}, u32[]{:S(2)}) copy-start(bf16[4,1152]{1,0:T(4,128)(2,1)} %param.14) | copy-start | bytes 27652
  7.2 127.3 %all-gather.14.cloned.1.call-start = ((), (), s32[]{:S(2)}) async-start(), calls=%async_computation.10 | async-start | bytes 16920576 | tf_op jit(solution)/shard_map/all_gather | solution.py:306
  7.9 201.0 %all-gather.18.cloned.1.call-start = ((), (), s32[]{:S(2)}) async-start(), calls=%async_computation.12 | async-start | bytes 8773632 | tf_op jit(solution)/shard_map/all_gather | solution.py:307
  8.7 223.5 %all-gather.16.cloned.1.call-start = ((), (), s32[]{:S(2)}) async-start(), calls=%async_computation.11 | async-start | bytes 1769472 | tf_op jit(solution)/shard_map/all_gather | solution.py:117
  9.5 517.9 %copy-start.73 = (s32[1,256]{1,0:T(1,128)}, s32[1,256]{1,0:T(1,128)S(1)}, u32[]{:S(2)}) copy-start(s32[1,256]{1,0:T(1,128)S(1)} %constant_dynamic-slice_fusion) | copy-start | bytes 3076
  9.7 141.4 %copy-start.94 = (f32[256]{0:T(256)}, f32[256]{0:T(256)S(1)}, u32[]{:S(2)}) copy-start(f32[256]{0:T(256)S(1)} %broadcast_multiply_fusion.11) | copy-start | bytes 3076
  10.0 141.1 %copy-start.98 = (f32[256]{0:T(256)}, f32[256]{0:T(256)S(1)}, u32[]{:S(2)}) copy-start(f32[256]{0:T(256)S(1)} %add_rsqrt_fusion.3) | copy-start | bytes 3076
  155.2 123.8 %all-gather.20.cloned.1.call-start = ((), (), s32[]{:S(2)}) async-start(), calls=%async_computation.13 | async-start | bytes 3133440 | tf_op jit(solution)/shard_map/all_gather | solution.py:308
  155.8 160.4 %reduce-scatter.16.cloned.1.call-start = ((), (), s32[]{:S(2)}) async-start(), calls=%async_computation.14 | async-start | bytes 3538944 | tf_op jit(solution)/shard_map/reduce_scatter | solution.py:129
  283.0 146.3 %all-gather.24.cloned.1.call-start = ((), (), s32[]{:S(2)}) async-start(), calls=%async_computation.16 | async-start | bytes 15040512 | tf_op jit(solution)/shard_map/all_gather | solution.py:309
  283.6 168.9 %all-gather.22.cloned.1.call-start = ((), (), s32[]{:S(2)}) async-start(), calls=%async_computation.15 | async-start | bytes 1769472 | tf_op jit(solution)/shard_map/all_gather | solution.py:117
  321.1 200.6 %all-gather.26.cloned.1.call-start = ((), (), s32[]{:S(2)}) async-start(), calls=%async_computation.17 | async-start | bytes 7520256 | tf_op jit(solution)/shard_map/all_gather | solution.py:310
  321.9 238.8 %reduce-scatter.18.cloned.1.call-start = ((), (), s32[]{:S(2)}) async-start(), calls=%async_computation.18 | async-start | bytes 3538944 | tf_op jit(solution)/shard_map/reduce_scatter | solution.py:129
  462.9 64.5 %copy-start.30 = (bf16[512,1536]{1,0:T(8,128)(2,1)}, bf16[512,1536]{1,0:T(8,128)(2,1)S(1)}, u32[]{:S(2)}) copy-start(bf16[512,1536]{1,0:T(8,128)(2,1)S(1)} %multiply_convert_fusion.7) | copy-start | bytes 4718596
  527.4 61.2 %all-gather.28.cloned.1.call-start = ((), (), s32[]{:S(2)}) async-start(), calls=%async_computation.19 | async-start | bytes 1769472 | tf_op jit(solution)/shard_map/all_gather | solution.py:117
  565.7 75.3 %reduce-scatter.20.cloned.1.call-start = ((), (), s32[]{:S(2)}) async-start(), calls=%async_computation.20 | async-start | bytes 3538944 | tf_op jit(solution)/shard_map/reduce_scatter | solution.py:129
  606.1 64.1 %all-gather.30.cloned.1.call-start = ((), (), s32[]{:S(2)}) async-start(), calls=%async_computation.21 | async-start | bytes 1769472 | tf_op jit(solution)/shard_map/all_gather | solution.py:117
  642.9 126.7 %copy-start.85 = (f32[256]{0:T(256)}, f32[256]{0:T(256)S(1)}, u32[]{:S(2)}) copy-start(f32[256]{0:T(256)S(1)} %broadcast_multiply_fusion.8) | copy-start | bytes 3076
  643.9 125.7 %copy-start.91 = (f32[256]{0:T(256)}, f32[256]{0:T(256)S(1)}, u32[]{:S(2)}) copy-start(f32[256]{0:T(256)S(1)} %add_rsqrt_fusion) | copy-start | bytes 3076
  647.2 47.9 %all-gather.32.cloned.1.call-start = ((), (), s32[]{:S(2)}) async-start(), calls=%async_computation.23 | async-start | bytes 1769472 | tf_op jit(solution)/shard_map/all_gather | solution.py:121
  648.0 84.8 %reduce-scatter.24.cloned.1.call-start = ((), (), s32[]{:S(2)}) async-start(), calls=%async_computation.24 | async-start | bytes 1769472 | tf_op jit(solution)/shard_map/reduce_scatter | solution.py:142
  710.9 58.7 %reduce-scatter.22.cloned.1.call-start = ((), (), s32[]{:S(2)}) async-start(), calls=%async_computation.22 | async-start | bytes 3538944 | tf_op jit(solution)/shard_map/reduce_scatter | solution.py:129
  717.0 80.3 %all-gather.34.cloned.1.call-start = ((), (), s32[]{:S(2)}) async-start(), calls=%async_computation.25 | async-start | bytes 1769472 | tf_op jit(solution)/shard_map/all_gather | solution.py:121
  774.4 69.8 %reduce-scatter.26.cloned.1.call-start = ((), (), s32[]{:S(2)}) async-start(), calls=%async_computation.26 | async-start | bytes 1769472 | tf_op jit(solution)/shard_map/reduce_scatter | solution.py:142
  822.3 53.1 %all-gather.36.cloned.1.call-start = ((), (), s32[]{:S(2)}) async-start(), calls=%async_computation.27 | async-start | bytes 1769472 | tf_op jit(solution)/shard_map/all_gather | solution.py:121
  852.5 62.2 %reduce-scatter.28.cloned.1.call-start = ((), (), s32[]{:S(2)}) async-start(), calls=%async_computation.28 | async-start | bytes 1769472 | tf_op jit(solution)/shard_map/reduce_scatter | solution.py:142
  892.7 50.2 %all-gather.38.cloned.1.call-start = ((), (), s32[]{:S(2)}) async-start(), calls=%async_computation.29 | async-start | bytes 1769472 | tf_op jit(solution)/shard_map/all_gather | solution.py:121
  920.0 69.6 %reduce-scatter.30.cloned.1.call-start = ((), (), s32[]{:S(2)}) async-start(), calls=%async_computation.30 | async-start | bytes 1769472 | tf_op jit(solution)/shard_map/reduce_scatter | solution.py:142
  967.7 113.7 %reduce-scatter.32.cloned.1.call-start = ((), (), s32[]{:S(2)}) async-start(), calls=%async_computation.31 | async-start | bytes 2654208
  1010.6 216.7 %all-reduce.9.cloned.1.call-start = ((), (), s32[]{:S(2)}) async-start(), calls=%async_computation.33 | async-start | bytes 14155776
  1035.8 631.9 %all-reduce.11.cloned.1.call-start = ((), (), s32[]{:S(2)}) async-start(), calls=%async_computation.34 | async-start | bytes 54263808
  1135.9 681.7 %reduce-scatter.34.cloned.1.call-start = ((), (), s32[]{:S(2)}) async-start(), calls=%async_computation.32 | async-start | bytes 15040512
  (122 other events, 549.5 us)
Sparse Core Ops, SparseCore 0:
  10.2 124.2 all-gather.13
  136.7 72.2 all-gather.17
  211.1 21.0 all-gather.15
  234.2 44.7 all-gather.19
  283.1 33.0 reduce-scatter.15
  318.6 110.6 all-gather.23
  431.5 20.9 all-gather.21
  455.0 66.6 all-gather.25
  527.5 33.1 reduce-scatter.17
  565.8 22.7 all-gather.27
  606.2 34.7 reduce-scatter.19
  647.4 22.7 all-gather.29
  672.4 22.7 all-gather.31
  711.0 21.7 reduce-scatter.23
  734.9 34.7 reduce-scatter.21
  774.5 22.7 all-gather.33
  822.4 21.7 reduce-scatter.25
  852.6 22.7 all-gather.35
  892.8 21.7 reduce-scatter.27
  920.1 22.7 all-gather.37
  967.8 21.7 reduce-scatter.29
  1010.7 28.2 reduce-scatter.31
  1043.1 150.3 all-reduce.8
  1198.8 468.8 all-reduce.10
  1671.9 145.6 reduce-scatter.33
where the time goes:
time: 1840 us; the launch traced here: 1830 us
  waiting for transfers between devices  1220 us (66%)
  local copies, waits for them, and re-layouts  221 us (12%)
  matrix products  195 us (11%)
  other arithmetic  101 us (5%)
  blocking collectives  75.7 us (4%)
    unnamed x29, waiting for transfers between devices  504 us
    reduce_scatter x4, waiting for transfers between devices, collect(): lax.psum_scatter(partial_sum(jnp.int32(0), lax.axis_size('heads') * own_r...  130 us
    all_gather x1, waiting for transfers between devices, shards(): lax.all_gather(ada_weight, 'rows', axis=1, tiled=True)  124 us
    all_gather x1, waiting for transfers between devices, shards(): lax.all_gather(gu_weight, 'rows', axis=1, tiled=True)  107 us
    unnamed x273, local copies, waits for them, and re-layouts  84.7 us
    all_gather x4, waiting for transfers between devices, spread_grad(): return lax.all_gather(values, 'heads', axis=0, tiled=True)  74.6 us
    all_gather x4, waiting for transfers between devices, spread(): return lax.all_gather(values, 'heads', axis=0, tiled=True)  66.1 us
    reduce_scatter x4, waiting for transfers between devices, collect_back(): lax.psum_scatter(partial_sum(jnp.int32(0), own_rows * lax.axis_size('head...  65.6 us
  transfers between devices with their start and end apart: 25, of which 23 were waited for; matrix products, arithmetic and copies ran while one was open for 19% of the time, Pallas kernels for 0%

commit v1 on v0

v1 whole, which is shorter than its diff:
```python
import jax
import jax.numpy as jnp
from jax import lax
from jax.sharding import PartitionSpec as P

HD = 72


epsilon = 1e-06
theta_base = 10000.0
highest = lax.Precision.HIGHEST


def normalize(values):
    center = values - jnp.mean(values, axis=-1, keepdims=True)
    inverse = lax.rsqrt(jnp.mean(center * center, axis=-1, keepdims=True) + epsilon)
    return (center * inverse, inverse)


def norm_back(incoming, normed, inverse):
    return inverse * (
        incoming
        - jnp.mean(incoming, axis=-1, keepdims=True)
        - normed * jnp.mean(incoming * normed, axis=-1, keepdims=True)
    )


def lead_dot(operand, other):
    return lax.dot_general(
        operand, other, (((0,), (0,)), ((), ())), preferred_element_type=jnp.float32
    )


def tail_dot(operand, other):
    return lax.dot_general(
        operand, other, (((1,), (1,)), ((), ())), preferred_element_type=jnp.float32
    )


def angles(coords, quarter):
    frequency = theta_base ** (-jnp.arange(quarter, dtype=jnp.float32) / quarter)
    return coords.astype(jnp.float32)[..., None] * frequency


def row_factors():
    size = lax.axis_size("rows")
    return (4, size // 8, 2)


def row_place():
    sizes = row_factors()
    index = lax.axis_index("rows")
    return (index // (sizes[1] * sizes[2]), (index // sizes[2]) % sizes[1], index % sizes[2])


def row_move(value, dim, step):
    sizes = row_factors()
    pairs = []
    for target in range(lax.axis_size("rows")):
        place = [target // (sizes[1] * sizes[2]), (target // sizes[2]) % sizes[1], target % sizes[2]]
        place[dim] = (place[dim] + step) % sizes[dim]
        pairs.append(((place[0] * sizes[1] + place[1]) * sizes[2] + place[2], target))
    return lax.ppermute(value, "rows", pairs)


def head_move(value, flip):
    size = lax.axis_size("heads")
    return lax.ppermute(value, "heads", [(index, index ^ flip) for index in range(size)])


def in_order(chunks, mine, axis):
    count = len(chunks)
    placed = []
    for slot in range(count):
        value = chunks[0]
        for step in range(1, count):
            value = jnp.where(mine == (slot - step) % count, chunks[step], value)
        placed.append(value)
    return jnp.stack(placed, axis=axis)


def gather_rows(shard):
    sizes = row_factors()
    place = row_place()
    value = shard
    for dim in range(3):
        chunks = [value] + [row_move(value, dim, step) for step in range(1, sizes[dim])]
        value = in_order(chunks, place[dim], dim)
    return value.reshape(-1, shard.shape[-1])


def scatter_rows(parts):
    sizes = row_factors()
    place = row_place()
    pieces = [part.reshape(sizes + (-1, part.shape[-1])) for part in parts]
    for dim in (2, 1, 0):
        count = sizes[dim]

        def pick(step):
            taken = [
                lax.dynamic_index_in_dim(piece, (place[dim] + step) % count, dim, keepdims=False)
                for piece in pieces
            ]
            return taken[0] if len(taken) == 1 else jnp.concatenate(taken, axis=-1)

        arrived = [row_move(pick(step), dim, count - step) for step in range(1, count)]
        total = pick(0).astype(jnp.float32)
        for item in arrived:
            total = total + item.astype(jnp.float32)
        pieces = [total.astype(jnp.bfloat16) if dim else total]
    return pieces[0]


def rope_parts(coords):
    angle = angles(coords, HD // 4)
    return jnp.cos(angle), jnp.sin(angle)


def turn(vectors, geometry, sign):
    row_cos, row_sin, col_cos, col_sin = [item[:, :, None, :] for item in geometry]
    quarter = HD // 4
    a, b, c, d = [vectors[..., quarter * i : quarter * (i + 1)] for i in range(4)]
    return jnp.concatenate(
        [
            a * row_cos - b * (sign * row_sin),
            b * row_cos + a * (sign * row_sin),
            c * col_cos - d * (sign * col_sin),
            d * col_cos + c * (sign * col_sin),
        ],
        axis=-1,
    )


def masked_scores(queries, key_rows, image_ids):
    scores = jnp.einsum(
        "rqhe,rkhe->rhqk", queries, key_rows, preferred_element_type=jnp.float32
    ) * HD ** (-0.5)
    same_image = image_ids[:, :, None] == image_ids[:, None, :]
    return jnp.where(same_image[:, None], scores, -1e30)


def attend(queries, key_rows, value_rows, image_ids):
    scores = masked_scores(queries, key_rows, image_ids)
    maximum = jnp.max(scores, axis=-1, keepdims=True)
    scaled_exp = jnp.exp(scores - maximum)
    denominator = jnp.sum(scaled_exp, axis=-1, keepdims=True)
    weights = (scaled_exp / denominator).astype(jnp.bfloat16)
    attended = jnp.einsum("rhqk,rkhe->rqhe", weights, value_rows, preferred_element_type=jnp.float32)
    return (attended.astype(jnp.bfloat16), (maximum + jnp.log(denominator))[..., 0])


def attend_back(queries, key_rows, value_rows, image_ids, logsum, grad_attended):
    score_scale = HD ** (-0.5)
    probs = jnp.exp(masked_scores(queries, key_rows, image_ids) - logsum[..., None])
    weights = probs.astype(jnp.bfloat16)
    grad_value = jnp.einsum(
        "rhqk,rqhe->rkhe", weights, grad_attended, preferred_element_type=jnp.float32
    )
    grad_probs = jnp.einsum(
        "rqhe,rkhe->rhqk", grad_attended, value_rows, preferred_element_type=jnp.float32
    )
    inner_sum = jnp.sum(probs * grad_probs, axis=-1, keepdims=True)
    grad_scores = (probs * (grad_probs - inner_sum)).astype(jnp.bfloat16)
    grad_query = (
        jnp.einsum("rhqk,rkhe->rqhe", grad_scores, key_rows, preferred_element_type=jnp.float32)
        * score_scale
    )
    grad_key = (
        jnp.einsum("rhqk,rqhe->rkhe", grad_scores, queries, preferred_element_type=jnp.float32)
        * score_scale
    )
    return (grad_query, grad_key, grad_value)


def spread(values):
    return jnp.concatenate(
        [values] + [head_move(values, flip) for flip in range(1, lax.axis_size("heads"))], axis=0
    )


def collect(operand, product, own_rows):
    total = None
    arrived = []
    for flip in range(1, lax.axis_size("heads")):
        partial = product(operand[flip * own_rows : (flip + 1) * own_rows])
        arrived.append(head_move(partial.astype(jnp.bfloat16), flip))
    total = product(operand[:own_rows])
    for item in arrived:
        total = total + item.astype(jnp.float32)
    return total


def plain_dot(operand, other):
    return jnp.dot(operand, other, preferred_element_type=jnp.float32)


def piece_of(mods, picks, index):
    width = mods.shape[1] // 6
    value = mods[:, index * width : (index + 1) * width]
    total = jnp.zeros((picks.shape[0], width), jnp.float32)
    for image in range(mods.shape[0]):
        total = jnp.where(picks[:, None] == image, value[image][None, :], total)
    return total


def block_forward(residual, pieces, qkv_full, qkv_b, proj_t, gu_full, down_t, image_ids, geometry):
    shift_attn, scale_attn, gate_attn, shift_mlp, scale_mlp, gate_mlp = pieces
    own_rows = residual.shape[0]
    count_rows, row_len = image_ids.shape
    normed_attn, inverse_attn = normalize(residual)
    input_attn = spread((normed_attn * (1.0 + scale_attn) + shift_attn).astype(jnp.bfloat16))
    packed = plain_dot(input_attn, qkv_full) + qkv_b
    heads_here = packed.shape[1] // (3 * HD)
    packed = packed.reshape(count_rows, row_len, heads_here, 3, HD)
    queries = turn(packed[:, :, :, 0], geometry, 1.0).astype(jnp.bfloat16)
    key_rows = turn(packed[:, :, :, 1], geometry, 1.0).astype(jnp.bfloat16)
    value_rows = packed[:, :, :, 2].astype(jnp.bfloat16)
    attended, logsum = attend(queries, key_rows, value_rows, image_ids)
    attended = attended.reshape(count_rows * row_len, heads_here * HD)
    branch = collect(attended, lambda rows: tail_dot(rows, proj_t), own_rows)
    middle = residual + gate_attn * branch
    normed_mlp, inverse_mlp = normalize(middle)
    input_mlp = spread((normed_mlp * (1.0 + scale_mlp) + shift_mlp).astype(jnp.bfloat16))
    gate_up = plain_dot(input_mlp, gu_full)
    hidden_width = gate_up.shape[1] // 2
    gate_part = gate_up[:, :hidden_width]
    up_part = gate_up[:, hidden_width:]
    hidden = (jax.nn.silu(gate_part) * up_part).astype(jnp.bfloat16)
    mlp_out = collect(hidden, lambda rows: tail_dot(rows, down_t), own_rows)
    result = middle + gate_mlp * mlp_out
    stored = (
        normed_attn,
        inverse_attn,
        input_attn,
        queries,
        key_rows,
        value_rows,
        logsum,
        attended,
        branch,
        normed_mlp,
        inverse_mlp,
        input_mlp,
        gate_part,
        up_part,
        hidden,
        mlp_out,
    )
    return (result, stored)


def block_backward(incoming, pieces, stored, qkv_full, proj_t, gu_full, down_t, image_ids, geometry):
    shift_attn, scale_attn, gate_attn, shift_mlp, scale_mlp, gate_mlp = pieces
    (
        normed_attn,
        inverse_attn,
        input_attn,
        queries,
        key_rows,
        value_rows,
        logsum,
        attended,
        branch,
        normed_mlp,
        inverse_mlp,
        input_mlp,
        gate_part,
        up_part,
        hidden,
        mlp_out,
    ) = stored
    own_rows = incoming.shape[0]
    count_rows, row_len = image_ids.shape
    grad_mlp = (gate_mlp * incoming).astype(jnp.bfloat16)
    grad_gate_mlp = incoming * mlp_out
    gathered_mlp = spread(grad_mlp)
    down_grad = lead_dot(gathered_mlp, hidden).astype(jnp.bfloat16)
    grad_hidden = plain_dot(gathered_mlp, down_t)
    logistic = jax.nn.sigmoid(gate_part)
    grad_gate_part = grad_hidden * up_part * logistic * (1.0 + gate_part * (1.0 - logistic))
    grad_up_part = grad_hidden * gate_part * logistic
    grad_gate_up = jnp.concatenate([grad_gate_part, grad_up_part], axis=1).astype(jnp.bfloat16)
    gu_grad = lead_dot(input_mlp, grad_gate_up).astype(jnp.bfloat16)
    gu_out = lax.psum_scatter(gu_grad, "rows", scatter_dimension=0, tiled=True).astype(jnp.float32)
    grad_input_mlp = collect(grad_gate_up, lambda rows: tail_dot(rows, gu_full), own_rows)
    grad_middle = incoming + norm_back(grad_input_mlp * (1.0 + scale_mlp), normed_mlp, inverse_mlp)
    grad_branch = (gate_attn * grad_middle).astype(jnp.bfloat16)
    grad_gate_attn = grad_middle * branch
    heads_here = queries.shape[2]
    gathered_branch = spread(grad_branch)
    proj_grad = lead_dot(gathered_branch, attended).astype(jnp.bfloat16)
    side = scatter_rows([down_grad, proj_grad])
    down_out, proj_out = side[:, : hidden.shape[1]], side[:, hidden.shape[1] :]
    grad_attended = plain_dot(gathered_branch, proj_t).astype(jnp.bfloat16)
    grad_attended = grad_attended.reshape(count_rows, row_len, heads_here, HD)
    grad_query, grad_key, grad_value = attend_back(
        queries, key_rows, value_rows, image_ids, logsum, grad_attended
    )
    grad_query = turn(grad_query, geometry, -1.0)
    grad_key = turn(grad_key, geometry, -1.0)
    grad_packed = (
        jnp.stack([grad_query, grad_key, grad_value], axis=3)
        .reshape(count_rows * row_len, heads_here * 3 * HD)
        .astype(jnp.bfloat16)
    )
    qkv_bias_grad = jnp.sum(grad_packed, axis=0, dtype=jnp.float32)
    qkv_grad = lead_dot(input_attn, grad_packed).astype(jnp.bfloat16)
    qkv_out = scatter_rows([qkv_grad])
    grad_input_attn = collect(grad_packed, lambda rows: tail_dot(rows, qkv_full), own_rows)
    grad_input = grad_middle + norm_back(
        grad_input_attn * (1.0 + scale_attn), normed_attn, inverse_attn
    )
    grad_mods = jnp.concatenate(
        [
            grad_input_attn,
            grad_input_attn * normed_attn,
            grad_gate_attn,
            grad_input_mlp,
            grad_input_mlp * normed_mlp,
            grad_gate_mlp,
        ],
        axis=1,
    )
    return (grad_input, grad_mods, (qkv_out, qkv_bias_grad, proj_out, gu_out, down_out))


def heads_in_order(value):
    index = lax.axis_index("heads")
    count = lax.axis_size("heads")
    chunks = [value] + [head_move(value, flip) for flip in range(1, count)]
    placed = []
    for slot in range(count):
        item = chunks[0]
        for flip in range(1, count):
            item = jnp.where(index == slot ^ flip, chunks[flip], item)
        placed.append(item)
    return jnp.stack(placed)


def heads_share(value):
    index = lax.axis_index("heads")
    count = lax.axis_size("heads")
    width = value.shape[-1] // count

    def part(flip):
        return lax.dynamic_slice_in_dim(value, (index ^ flip) * width, width, value.ndim - 1)

    arrived = [head_move(part(flip), flip) for flip in range(1, count)]
    total = part(0)
    for item in arrived:
        total = total + item
    return total


def shards(
    tokens,
    cond,
    image_of,
    grid_row,
    grid_col,
    ada_weight,
    ada_bias,
    qkv_weight,
    qkv_bias,
    proj_weight,
    gu_weight,
    down_weight,
    cotangent,
):
    own_rows = tokens.shape[0]
    image_count = cond.shape[0]
    block_count = qkv_weight.shape[0]
    row_size = lax.axis_size("rows")
    head_size = lax.axis_size("heads")
    head_index = lax.axis_index("heads")

    def device_order(values):
        parts = values.reshape(head_size, own_rows)
        picked = [
            lax.dynamic_index_in_dim(parts, head_index ^ flip, 0, keepdims=False)
            for flip in range(head_size)
        ]
        return jnp.concatenate(picked).reshape(values.shape)

    image_ids = device_order(image_of - lax.axis_index("rows") * image_count)
    own_images = image_ids.reshape(-1)[:own_rows]
    picker = (own_images[:, None] == jnp.arange(image_count, dtype=jnp.int32)[None, :]).astype(
        jnp.float32
    )
    geometry = lax.optimization_barrier(
        rope_parts(device_order(grid_row)) + rope_parts(device_order(grid_col))
    )
    qkv_full = [None] * block_count
    gu_full = [None] * block_count
    down_t = [None] * block_count
    proj_t = [None] * block_count
    shard_rows = qkv_weight.shape[1]
    for b in range(block_count):
        if b == 0:
            qkv_full[b] = lax.all_gather(qkv_weight[b], "rows", axis=0, tiled=True)
        else:
            qkv_full[b] = gather_rows(qkv_weight[b])
        gu_full[b] = lax.all_gather(
            gu_weight[b].reshape(shard_rows, -1), "rows", axis=0, tiled=True
        )
        side = gather_rows(jnp.concatenate([down_weight[b].T, proj_weight[b].T], axis=1))
        down_t[b] = side[:, : down_weight.shape[1]]
        proj_t[b] = side[:, down_weight.shape[1] :]
    cond_wide = cond.astype(jnp.float32)
    cond_act = jax.nn.silu(cond_wide).astype(jnp.bfloat16)
    cond_mine = lax.all_to_all(
        cond_act.reshape(image_count, row_size, -1).transpose(1, 0, 2), "rows", 0, 0
    ).reshape(row_size * image_count, -1)
    mod_partial = jnp.stack([plain_dot(cond_mine, ada_weight[b]) for b in range(block_count)], axis=1)
    mod_arrived = lax.all_to_all(
        mod_partial.reshape(row_size, image_count, block_count, -1), "rows", 0, 0
    )
    mod_local = jnp.sum(mod_arrived, axis=0) + ada_bias.astype(jnp.float32)[None]
    mod_all = heads_in_order(mod_local)
    modulation = [
        jnp.concatenate([mod_all[index, :, b] for index in range(head_size)], axis=1)
        for b in range(block_count)
    ]
    pieces = [
        [piece_of(modulation[b], own_images, index) for index in range(6)] for b in range(block_count)
    ]
    residual = tokens.astype(jnp.float32)
    stored_all = []
    for b in range(block_count):
        residual, stored = block_forward(
            residual,
            pieces[b],
            qkv_full[b],
            qkv_bias[b].astype(jnp.float32),
            proj_t[b],
            gu_full[b],
            down_t[b],
            image_ids,
            geometry,
        )
        stored_all.append(stored)
    block_out = residual.astype(jnp.bfloat16)
    incoming = cotangent.astype(jnp.float32)
    block_grads = [None] * block_count
    ada_grads = [None] * block_count
    ada_bias_grads = [None] * block_count
    cond_partial = 0.0
    for b in reversed(range(block_count)):
        incoming, grad_mods, gradients = block_backward(
            incoming,
            pieces[b],
            stored_all[b],
            qkv_full[b],
            proj_t[b],
            gu_full[b],
            down_t[b],
            image_ids,
            geometry,
        )
        image_sums = lax.dot_general(
            picker, grad_mods, (((0,), (0,)), ((), ())), precision=highest
        )
        image_grads = heads_share(image_sums).astype(jnp.bfloat16)
        all_grads = lax.all_gather(image_grads, "rows", axis=0, tiled=True)
        ada_grads[b] = lead_dot(cond_mine, all_grads)
        ada_bias_grads[b] = jnp.sum(all_grads, axis=0, dtype=jnp.float32)
        cond_partial = cond_partial + tail_dot(all_grads, ada_weight[b])
        block_grads[b] = gradients
    cond_parts = lax.all_to_all(
        cond_partial.astype(jnp.bfloat16).reshape(row_size, image_count, -1), "rows", 0, 0
    )
    cond_rows = cond_parts.transpose(1, 0, 2).reshape(image_count, -1).astype(jnp.float32)
    cond_total = cond_rows
    for flip in range(1, head_size):
        cond_total = cond_total + head_move(cond_rows.astype(jnp.bfloat16), flip).astype(jnp.float32)
    logistic = jax.nn.sigmoid(cond_wide)
    cond_grad = cond_total * logistic * (1.0 + cond_wide * (1.0 - logistic))
    qkv_bias_out = lax.psum(jnp.stack([item[1] for item in block_grads]), "rows")
    return (
        block_out,
        incoming,
        cond_grad,
        jnp.stack(ada_grads),
        jnp.stack(ada_bias_grads),
        jnp.stack([item[0] for item in block_grads]),
        qkv_bias_out,
        jnp.stack([item[2].T for item in block_grads]),
        jnp.stack([item[3].reshape(gu_weight.shape[1:]) for item in block_grads]),
        jnp.stack([item[4].T for item in block_grads]),
    )


def solution(mesh):
    in_specs = (
        P(("rows", "heads"), None),
        P("rows", None),
        P("rows", None),
        P("rows", None),
        P("rows", None),
        P(None, "rows", "heads"),
        P(None, "heads"),
        P(None, "rows", "heads"),
        P(None, "heads"),
        P(None, "heads", "rows"),
        P(None, "rows", None, "heads"),
        P(None, "heads", "rows"),
        P(("rows", "heads"), None),
    )
    out_specs = (
        P(("rows", "heads"), None),
        P(("rows", "heads"), None),
        P("rows", None),
        P(None, "rows", "heads"),
        P(None, "heads"),
        P(None, "rows", "heads"),
        P(None, "heads"),
        P(None, "heads", "rows"),
        P(None, "rows", None, "heads"),
        P(None, "heads", "rows"),
    )
    return jax.shard_map(shards, mesh=mesh, in_specs=in_specs, out_specs=out_specs, check_vma=False)
```

time: 1840 us -> 928 us (0.50)
  waiting for transfers between devices: 1220 us -> 335 us
  local copies, waits for them, and re-layouts: 221 us -> 89.8 us
  starting transfers between devices: 3.35 us -> 80.4 us
  blocking collectives: 75.7 us -> 138 us
  matrix products: 195 us -> 166 us
    all_gather x13 -> x3, waiting for transfers between devices: 516 us -> 0.02 us  [the longest x2 0.02 us: shards(): lax.all_gather(gu_weight[b].reshape(shard_rows, -1), 'rows', axis=0, tile...]
    unnamed x29 -> x5, waiting for transfers between devices: 504 us -> 0.08 us
    ppermute x0 -> x55, waiting for transfers between devices: none -> 287 us  [the longest x35 206 us: row_move(): return lax.ppermute(value, 'rows', pairs)]
    reduce_scatter x8 -> x2, waiting for transfers between devices: 196 us -> 0.02 us  [block_backward(): lax.psum_scatter(gu_grad, 'rows', scatter_dimension=0, tiled=True)]
    all_gather x1 -> x2, blocking collectives: 5.9 us -> 78.6 us  [shards(): all_grads = lax.all_gather(image_grads, 'rows', axis=0, tiled=True)]
    another operation x7 -> x14, local copies, waits for them, and re-layouts: 82.5 us -> 10.5 us  [the longest x3 3.18 us: in_order(): return jnp.stack(placed, axis=axis)]
    ppermute x0 -> x55, starting transfers between devices: none -> 61.9 us  [the longest x35 38.3 us: row_move(): return lax.ppermute(value, 'rows', pairs)]
    unnamed x273 -> x585, local copies, waits for them, and re-layouts: 84.7 us -> 29.6 us
  transfers between devices with their start and end apart: 25 -> 63, of which waited for: 23 -> 25; matrix products, arithmetic and copies ran while one was open for 19% -> 34% of each run, Pallas kernels for 0% -> 0%
where the time goes in v1:
time: 928 us; the launch traced here: 921 us
  waiting for transfers between devices  335 us (36%)
  matrix products  166 us (18%)
  blocking collectives  138 us (15%)
  other arithmetic  94.9 us (10%)
  local copies, waits for them, and re-layouts  89.8 us (10%)
  starting transfers between devices  80.4 us (9%)
  between operations  18.2 us (2%)
    ppermute x35, waiting for transfers between devices, row_move(): return lax.ppermute(value, 'rows', pairs)  206 us
    ppermute x20, waiting for transfers between devices, head_move(): lax.ppermute(value, 'heads', [(index, index ^ flip) for index in range(si...  81.3 us
    all_gather x2, blocking collectives, shards(): all_grads = lax.all_gather(image_grads, 'rows', axis=0, tiled=True)  78.6 us
    psum x1, blocking collectives, shards(): lax.psum(jnp.stack([item[1] for item in block_grads]), 'rows')  58.9 us
    dot_general x18, matrix products, tail_dot(): lax.dot_general(operand, other, (((1,), (1,)), ((), ())), preferred_eleme...  48.2 us
    all_to_all x1, waiting for transfers between devices, shards(): lax.all_to_all(cond_act.reshape(image_count, row_size, -1).transpose(1, 0...  44.6 us
    dot_general x10, matrix products, plain_dot(): return jnp.dot(operand, other, preferred_element_type=jnp.float32)  42.3 us
    dot_general x10, matrix products, lead_dot(): lax.dot_general(operand, other, (((0,), (0,)), ((), ())), preferred_eleme...  39.4 us
  transfers between devices with their start and end apart: 63, of which 25 were waited for; matrix products, arithmetic and copies ran while one was open for 34% of the time, Pallas kernels for 0%

profile of v1, /device:TPU:0, one launch (start us, length us, event | category | flops | bytes accessed | tf_op | source)
XLA Modules:
  0.0 921.1 jit_solution(1348667803906579301)
XLA Ops:
  33.1 44.6 %all-to-all-done = bf16[16,4,72]{2,1,0:T(4,128)(2,1)S(1)} async-done(((bf16[16,4,72]{2,1,0:T(4,128)(2,1)}), bf16[16,4,72]{2,1,0:T(4,128)(2,1)S(1)}, u32[]{:S(2)}, u32[]{:S(2)}) %all-to-all-start) | async-done | bytes 9248 | tf_op jit(solution)/shard_map/all_to_all | solution.py:411
  82.4 10.7 %all-to-all-start.1 = ((f32[16,4,2,3456]{3,1,2,0:T(4,128)}), f32[16,4,2,3456]{3,1,2,0:T(4,128)}, u32[]{:S(2)}, u32[]{:S(2)}) async-start(f32[16,4,2,3456]{3,1,2,0:T(4,128)} %copy.168), calls=%async_computation.1 | async-start | bytes 3538944 | tf_op jit(solution)/shard_map/all_to_all | solution.py:415
  101.4 46.7 %collective-permute-done.2 = bf16[72,2112]{1,0:T(8,128)(2,1)S(1)} collective-permute-done((bf16[72,2112]{1,0:T(8,128)(2,1)}, bf16[72,2112]{1,0:T(8,128)(2,1)S(1)}, u32[]{:S(2)}, u32[]{:S(2)}) %collective-permute-start.2) | collective-permute-done | bytes 304160 | tf_op jit(solution)/shard_map/ppermute | solution.py:63
  156.0 55.3 %collective-permute-done.17 = bf16[72,2112]{1,0:T(8,128)(2,1)S(1)} collective-permute-done((bf16[72,2112]{1,0:T(8,128)(2,1)}, bf16[72,2112]{1,0:T(8,128)(2,1)S(1)}, u32[]{:S(2)}, u32[]{:S(2)}) %collective-permute-start.17) | collective-permute-done | bytes 304160 | tf_op jit(solution)/shard_map/ppermute | solution.py:63
  230.4 8.9 collective-permute-done.1
  260.3 7.8 collective-permute-done.7
  277.5 7.0 collective-permute-done.8
  284.5 6.8 fusion.108
  319.2 6.0 collective-permute-done.10
  341.3 8.5 collective-permute-done.21
  360.0 11.6 %collective-permute-done.22 = bf16[256,1152]{1,0:T(8,128)(2,1)} collective-permute-done((bf16[256,1152]{1,0:T(8,128)(2,1)}, bf16[256,1152]{1,0:T(8,128)(2,1)}, u32[]{:S(2)}, u32[]{:S(2)}) %collective-permute-start.22) | collective-permute-done | bytes 589856 | tf_op jit(solution)/shard_map/ppermute | solution.py:68
  371.7 7.1 fusion.107
  378.8 5.7 multiply_convert_fusion.4
  397.2 9.4 %collective-permute-done.25 = bf16[256,1152]{1,0:T(8,128)(2,1)S(1)} collective-permute-done((bf16[256,1152]{1,0:T(8,128)(2,1)S(1)}, bf16[256,1152]{1,0:T(8,128)(2,1)S(1)}, u32[]{:S(2)}, u32[]{:S(2)}) %collective-permute-start.25) | collective-permute-done | bytes 589856 | tf_op jit(solution)/shard_map/ppermute | solution.py:68
  413.6 7.3 convolution_convert_fusion
  425.5 5.8 fusion.64
  466.6 6.7 copy.195
  496.4 54.2 %all-gather.1 = bf16[16,4,3456]{2,1,0:T(4,128)(2,1)S(1)} all-gather(bf16[1,4,3456]{2,1,0:T(4,128)(2,1)S(1)} %fusion.160), channel_id=1, replica_groups=mesh['rows'=16,'heads'=2] {'rows'}, dimensions={0}, use_global_device_ids=true | all-gather | bytes 470016 | tf_op jit(solution)/shard_map/all_gather | solution.py:464
  553.5 7.5 multiply_convert_fusion.2
  566.3 7.4 convolution_convert_fusion.1
  581.9 7.9 fusion.197
  595.8 11.4 %collective-permute-done.30 = bf16[256,1152]{1,0:T(8,128)(2,1)S(1)} collective-permute-done((bf16[256,1152]{1,0:T(8,128)(2,1)S(1)}, bf16[256,1152]{1,0:T(8,128)(2,1)S(1)}, u32[]{:S(2)}, u32[]{:S(2)}) %collective-permute-start.30) | collective-permute-done | bytes 589856 | tf_op jit(solution)/shard_map/ppermute | solution.py:68
  641.4 5.6 convolution_convert_fusion.3
  647.0 6.4 copy.193
  657.2 58.9 %psum.7 = f32[2,1728]{1,0:T(2,128)} all-reduce(f32[2,1728]{1,0:T(2,128)} %pad_maximum_fusion.51), channel_id=1, replica_groups=mesh['rows'=16,'heads'=2] {'rows'}, use_global_device_ids=true, to_apply=%region_27.28 | all-reduce | flops 3456 | bytes 27648 | tf_op jit(solution)/shard_map/psum | solution.py:478
  735.4 24.4 %all-gather.2 = bf16[16,4,3456]{2,1,0:T(4,128)(2,1)S(1)} all-gather(bf16[1,4,3456]{2,1,0:T(4,128)(2,1)S(1)} %fusion.161), channel_id=1, replica_groups=mesh['rows'=16,'heads'=2] {'rows'}, dimensions={0}, use_global_device_ids=true | all-gather | bytes 470016 | tf_op jit(solution)/shard_map/all_gather | solution.py:464
  789.7 21.3 %collective-permute-done.43 = bf16[72,1728]{1,0:T(8,128)(2,1)S(1)} collective-permute-done((bf16[72,1728]{1,0:T(8,128)(2,1)}, bf16[72,1728]{1,0:T(8,128)(2,1)S(1)}, u32[]{:S(2)}, u32[]{:S(2)}) %collective-permute-start.43) | collective-permute-done | bytes 248864 | tf_op jit(solution)/shard_map/ppermute | solution.py:63
  812.1 10.6 %collective-permute-done.53 = bf16[72,2112]{1,0:T(8,128)(2,1)S(1)} collective-permute-done((bf16[72,2112]{1,0:T(8,128)(2,1)S(1)}, bf16[72,2112]{1,0:T(8,128)(2,1)S(1)}, u32[]{:S(2)}, u32[]{:S(2)}) %collective-permute-start.53) | collective-permute-done | bytes 304160 | tf_op jit(solution)/shard_map/ppermute | solution.py:63
  829.8 21.2 %collective-permute-done.36 = bf16[4,72,1728]{2,1,0:T(8,128)(2,1)S(1)} collective-permute-done((bf16[4,72,1728]{2,1,0:T(8,128)(2,1)S(1)}, bf16[4,72,1728]{2,1,0:T(8,128)(2,1)S(1)}, u32[]{:S(2)}, u32[]{:S(2)}) %collective-permute-start.36) | collective-permute-done | bytes 995360 | tf_op jit(solution)/shard_map/ppermute | solution.py:63
  855.2 20.0 %collective-permute-done.46 = bf16[4,72,2112]{2,1,0:T(8,128)(2,1)S(1)} collective-permute-done((bf16[4,72,2112]{2,1,0:T(8,128)(2,1)S(1)}, bf16[4,72,2112]{2,1,0:T(8,128)(2,1)S(1)}, u32[]{:S(2)}, u32[]{:S(2)}) %collective-permute-start.46) | collective-permute-done | bytes 1216544 | tf_op jit(solution)/shard_map/ppermute | solution.py:63
  882.1 6.6 collective-permute-done.47
  892.5 14.8 %collective-permute-done.48 = bf16[72,2112]{1,0:T(8,128)(2,1)S(1)} collective-permute-done((bf16[72,2112]{1,0:T(8,128)(2,1)S(1)}, bf16[72,2112]{1,0:T(8,128)(2,1)S(1)}, u32[]{:S(2)}, u32[]{:S(2)}) %collective-permute-start.48) | collective-permute-done | bytes 304160 | tf_op jit(solution)/shard_map/ppermute | solution.py:63
  (941 shorter events, 368.8 us)
Async XLA Ops:
  7.2 232.1 %all-gather.11.cloned.1.call-start = ((), (), s32[]{:S(2)}) async-start(), calls=%async_computation.9 | async-start | bytes 4386816 | tf_op jit(solution)/shard_map/all_gather | solution.py:400
  9.2 275.3 %all-gather.7.cloned.1.call-start = ((), (), s32[]{:S(2)}) async-start(), calls=%async_computation.5 | async-start | bytes 7520256 | tf_op jit(solution)/shard_map/all_gather | solution.py:403
  11.9 87.4 %collective-permute-start.4 = (bf16[72,2112]{1,0:T(8,128)(2,1)}, bf16[72,2112]{1,0:T(8,128)(2,1)}, u32[]{:S(2)}, u32[]{:S(2)}) collective-permute-start(bf16[72,2112]{1,0:T(8,128)(2,1)} %pad_maximum_fusion.48), channel_id=1, source_target_pairs={{8,0},{10,2},{12,4},{14,6},{16,8},{18,10},{20,12},{22,14},{24,16},... | collective-permute-start | bytes 912392 | tf_op jit(solution)/shard_map/ppermute | solution.py:63
  16.9 84.5 %collective-permute-start.3 = (bf16[72,2112]{1,0:T(8,128)(2,1)}, bf16[72,2112]{1,0:T(8,128)(2,1)}, u32[]{:S(2)}, u32[]{:S(2)}) collective-permute-start(bf16[72,2112]{1,0:T(8,128)(2,1)} %pad_maximum_fusion.48), channel_id=1, source_target_pairs={{16,0},{18,2},{20,4},{22,6},{24,8},{26,10},{28,12},{30,14},{0,16},... | collective-permute-start | bytes 912392 | tf_op jit(solution)/shard_map/ppermute | solution.py:63
  16.9 76.2 %collective-permute-start.13 = (bf16[72,1728]{1,0:T(8,128)(2,1)}, bf16[72,1728]{1,0:T(8,128)(2,1)S(1)}, u32[]{:S(2)}, u32[]{:S(2)}) collective-permute-start(bf16[72,1728]{1,0:T(8,128)(2,1)} %get-tuple-element.216), channel_id=1, source_target_pairs={{8,0},{10,2},{12,4},{14,6},{16,8},{18,10},{20,12},{22,14},{24,16},... | collective-permute-start | bytes 746504 | tf_op jit(solution)/shard_map/ppermute | solution.py:63
  17.4 77.7 %collective-permute-start.12 = (bf16[72,1728]{1,0:T(8,128)(2,1)}, bf16[72,1728]{1,0:T(8,128)(2,1)}, u32[]{:S(2)}, u32[]{:S(2)}) collective-permute-start(bf16[72,1728]{1,0:T(8,128)(2,1)} %get-tuple-element.216), channel_id=1, source_target_pairs={{16,0},{18,2},{20,4},{22,6},{24,8},{26,10},{28,12},{30,14},{0,16},... | collective-permute-start | bytes 746504 | tf_op jit(solution)/shard_map/ppermute | solution.py:63
  19.9 77.2 %collective-permute-start.11 = (bf16[72,1728]{1,0:T(8,128)(2,1)}, bf16[72,1728]{1,0:T(8,128)(2,1)}, u32[]{:S(2)}, u32[]{:S(2)}) collective-permute-start(bf16[72,1728]{1,0:T(8,128)(2,1)} %get-tuple-element.216), channel_id=1, source_target_pairs={{24,0},{26,2},{28,4},{30,6},{0,8},{2,10},{4,12},{6,14},{8,16},{10,... | collective-permute-start | bytes 746504 | tf_op jit(solution)/shard_map/ppermute | solution.py:63
  22.6 55.1 %all-to-all-start = ((bf16[16,4,72]{2,1,0:T(4,128)(2,1)}), bf16[16,4,72]{2,1,0:T(4,128)(2,1)S(1)}, u32[]{:S(2)}, u32[]{:S(2)}) async-start(bf16[16,4,72]{2,1,0:T(4,128)(2,1)} %copy.165), calls=%async_computation | async-start | bytes 32768 | tf_op jit(solution)/shard_map/all_to_all | solution.py:411
  26.8 333.3 %all-gather.9.cloned.1.call-start = ((), (), s32[]{:S(2)}) async-start(), calls=%async_computation.6 | async-start | bytes 7520256 | tf_op jit(solution)/shard_map/all_gather | solution.py:403
  82.4 132.7 %all-to-all-start.1 = ((f32[16,4,2,3456]{3,1,2,0:T(4,128)}), f32[16,4,2,3456]{3,1,2,0:T(4,128)}, u32[]{:S(2)}, u32[]{:S(2)}) async-start(f32[16,4,2,3456]{3,1,2,0:T(4,128)} %copy.168), calls=%async_computation.1 | async-start | bytes 3538944 | tf_op jit(solution)/shard_map/all_to_all | solution.py:415
  93.1 816.2 %reduce-scatter.5.cloned.1.call-start = ((), (), s32[]{:S(2)}) async-start(), calls=%async_computation.8 | async-start | bytes 7520256 | tf_op jit(solution)/shard_map/reduce_scatter | solution.py:284
  93.2 54.9 %collective-permute-start.2 = (bf16[72,2112]{1,0:T(8,128)(2,1)}, bf16[72,2112]{1,0:T(8,128)(2,1)S(1)}, u32[]{:S(2)}, u32[]{:S(2)}) collective-permute-start(bf16[72,2112]{1,0:T(8,128)(2,1)} %pad_maximum_fusion.48), channel_id=1, source_target_pairs={{24,0},{26,2},{28,4},{30,6},{0,8},{2,10},{4,12},{6,14},{8,16},{10,... | collective-permute-start | bytes 912392 | tf_op jit(solution)/shard_map/ppermute | solution.py:63
  95.1 61.0 %collective-permute-start.18 = (bf16[72,2112]{1,0:T(8,128)(2,1)}, bf16[72,2112]{1,0:T(8,128)(2,1)S(1)}, u32[]{:S(2)}, u32[]{:S(2)}) collective-permute-start(bf16[72,2112]{1,0:T(8,128)(2,1)} %pad_maximum_fusion.49), channel_id=1, source_target_pairs={{8,0},{10,2},{12,4},{14,6},{16,8},{18,10},{20,12},{22,14},{24,16},... | collective-permute-start | bytes 912392 | tf_op jit(solution)/shard_map/ppermute | solution.py:63
  97.1 114.3 %collective-permute-start.17 = (bf16[72,2112]{1,0:T(8,128)(2,1)}, bf16[72,2112]{1,0:T(8,128)(2,1)S(1)}, u32[]{:S(2)}, u32[]{:S(2)}) collective-permute-start(bf16[72,2112]{1,0:T(8,128)(2,1)} %pad_maximum_fusion.49), channel_id=1, source_target_pairs={{16,0},{18,2},{20,4},{22,6},{24,8},{26,10},{28,12},{30,14},{0,16},... | collective-permute-start | bytes 912392 | tf_op jit(solution)/shard_map/ppermute | solution.py:63
  99.3 112.0 %collective-permute-start.16 = (bf16[72,2112]{1,0:T(8,128)(2,1)}, bf16[72,2112]{1,0:T(8,128)(2,1)S(1)}, u32[]{:S(2)}, u32[]{:S(2)}) collective-permute-start(bf16[72,2112]{1,0:T(8,128)(2,1)} %pad_maximum_fusion.49), channel_id=1, source_target_pairs={{24,0},{26,2},{28,4},{30,6},{0,8},{2,10},{4,12},{6,14},{8,16},{10,... | collective-permute-start | bytes 912392 | tf_op jit(solution)/shard_map/ppermute | solution.py:63
  149.7 65.0 %collective-permute-start.5 = (bf16[4,72,2112]{2,1,0:T(8,128)(2,1)S(1)}, bf16[4,72,2112]{2,1,0:T(8,128)(2,1)S(1)}, u32[]{:S(2)}, u32[]{:S(2)}) collective-permute-start(bf16[4,72,2112]{2,1,0:T(8,128)(2,1)S(1)} %pad_maximum_fusion.14), channel_id=1, source_target_pairs={{4,0},{6,2},{0,4},{2,6},{12,8},{14,10},{8,12},{10,14},{20,16},{22,... | collective-permute-start | bytes 3649544 | tf_op jit(solution)/shard_map/ppermute | solution.py:63
  152.4 104.0 %collective-permute-start.14 = (bf16[4,72,1728]{2,1,0:T(8,128)(2,1)}, bf16[4,72,1728]{2,1,0:T(8,128)(2,1)}, u32[]{:S(2)}, u32[]{:S(2)}) collective-permute-start(bf16[4,72,1728]{2,1,0:T(8,128)(2,1)} %pad_maximum_fusion.24), channel_id=1, source_target_pairs={{4,0},{6,2},{0,4},{2,6},{12,8},{14,10},{8,12},{10,14},{20,16},{22,... | collective-permute-start | bytes 2985992 | tf_op jit(solution)/shard_map/ppermute | solution.py:63
  213.2 60.3 %collective-permute-start.19 = (bf16[4,72,2112]{2,1,0:T(8,128)(2,1)}, bf16[4,72,2112]{2,1,0:T(8,128)(2,1)}, u32[]{:S(2)}, u32[]{:S(2)}) collective-permute-start(bf16[4,72,2112]{2,1,0:T(8,128)(2,1)} %pad_maximum_fusion.15), channel_id=1, source_target_pairs={{4,0},{6,2},{0,4},{2,6},{12,8},{14,10},{8,12},{10,14},{20,16},{22,... | collective-permute-start | bytes 3649544 | tf_op jit(solution)/shard_map/ppermute | solution.py:63
  259.5 40.4 %collective-permute-start.15 = (bf16[4,2,72,1728]{3,2,0,1:T(8,128)(2,1)}, bf16[4,2,72,1728]{3,2,0,1:T(8,128)(2,1)}, u32[]{:S(2)}, u32[]{:S(2)}) collective-permute-start(bf16[4,2,72,1728]{3,2,0,1:T(8,128)(2,1)} %pad_maximum_fusion.11), channel_id=1, source_target_pairs={{2,0},{0,2},{6,4},{4,6},{10,8},{8,10},{14,12},{12,14},{18,16},{16,... | collective-permute-start | bytes 5971976 | tf_op jit(solution)/shard_map/ppermute | solution.py:63
  277.5 38.6 %collective-permute-start.20 = (bf16[4,2,72,2112]{3,2,0,1:T(8,128)(2,1)}, bf16[4,2,72,2112]{3,2,0,1:T(8,128)(2,1)}, u32[]{:S(2)}, u32[]{:S(2)}) collective-permute-start(bf16[4,2,72,2112]{3,2,0,1:T(8,128)(2,1)} %pad_maximum_fusion.8), channel_id=1, source_target_pairs={{2,0},{0,2},{6,4},{4,6},{10,8},{8,10},{14,12},{12,14},{18,16},{16,... | collective-permute-start | bytes 7299080 | tf_op jit(solution)/shard_map/ppermute | solution.py:63
  386.6 96.4 %collective-permute-start.23 = (bf16[256,1152]{1,0:T(8,128)(2,1)}, bf16[256,1152]{1,0:T(8,128)(2,1)}, u32[]{:S(2)}, u32[]{:S(2)}) collective-permute-start(bf16[256,1152]{1,0:T(8,128)(2,1)} %fusion.38), channel_id=1, source_target_pairs={{0,1},{1,0},{2,3},{3,2},{4,5},{5,4},{6,7},{7,6},{8,9},{9,8},{10,11... | collective-permute-start | bytes 1769480 | tf_op jit(solution)/shard_map/ppermute | solution.py:68
  420.9 489.8 %reduce-scatter.3.cloned.1.call-start = ((), (), s32[]{:S(2)}) async-start(), calls=%async_computation.7 | async-start | bytes 7520256 | tf_op jit(solution)/shard_map/reduce_scatter | solution.py:284
  460.9 255.2 %collective-permute-start.50 = (bf16[4,2,72,2112]{3,2,0,1:T(8,128)(2,1)}, bf16[4,2,72,2112]{3,2,0,1:T(8,128)(2,1)}, u32[]{:S(2)}, u32[]{:S(2)}) collective-permute-start(bf16[4,2,72,2112]{3,2,0,1:T(8,128)(2,1)} %pad_maximum_fusion.10), channel_id=1, source_target_pairs={{2,0},{0,2},{6,4},{4,6},{10,8},{8,10},{14,12},{12,14},{18,16},{16,... | collective-permute-start | bytes 7299080 | tf_op jit(solution)/shard_map/ppermute | solution.py:63
  495.1 96.9 %collective-permute-start.40 = (bf16[4,2,72,1728]{3,2,0,1:T(8,128)(2,1)}, bf16[4,2,72,1728]{3,2,0,1:T(8,128)(2,1)}, u32[]{:S(2)}, u32[]{:S(2)}) collective-permute-start(bf16[4,2,72,1728]{3,2,0,1:T(8,128)(2,1)} %bitcast.409), channel_id=1, source_target_pairs={{2,0},{0,2},{6,4},{4,6},{10,8},{8,10},{14,12},{12,14},{18,16},{16,... | collective-permute-start | bytes 5971976 | tf_op jit(solution)/shard_map/ppermute | solution.py:63
  495.1 58.4 %collective-permute-start.28 = (bf16[256,1152]{1,0:T(8,128)(2,1)}, bf16[256,1152]{1,0:T(8,128)(2,1)}, u32[]{:S(2)}, u32[]{:S(2)}) collective-permute-start(bf16[256,1152]{1,0:T(8,128)(2,1)} %get-tuple-element.84), channel_id=1, source_target_pairs={{0,1},{1,0},{2,3},{3,2},{4,5},{5,4},{6,7},{7,6},{8,9},{9,8},{10,11... | collective-permute-start | bytes 1769480 | tf_op jit(solution)/shard_map/ppermute | solution.py:68
  595.8 137.2 %collective-permute-start.41 = (bf16[4,72,1728]{2,1,0:T(8,128)(2,1)}, bf16[4,72,1728]{2,1,0:T(8,128)(2,1)}, u32[]{:S(2)}, u32[]{:S(2)}) collective-permute-start(bf16[4,72,1728]{2,1,0:T(8,128)(2,1)} %dynamic-slice_bitcast_fusion.3), channel_id=1, source_target_pairs={{4,0},{6,2},{0,4},{2,6},{12,8},{14,10},{8,12},{10,14},{20,16},{22,... | collective-permute-start | bytes 2985992 | tf_op jit(solution)/shard_map/ppermute | solution.py:63
  629.2 196.6 %collective-permute-start.45 = (bf16[4,2,72,2112]{3,2,0,1:T(8,128)(2,1)}, bf16[4,2,72,2112]{3,2,0,1:T(8,128)(2,1)}, u32[]{:S(2)}, u32[]{:S(2)}) collective-permute-start(bf16[4,2,72,2112]{3,2,0,1:T(8,128)(2,1)} %pad_maximum_fusion.9), channel_id=1, source_target_pairs={{2,0},{0,2},{6,4},{4,6},{10,8},{8,10},{14,12},{12,14},{18,16},{16,... | collective-permute-start | bytes 7299080 | tf_op jit(solution)/shard_map/ppermute | solution.py:63
  640.1 80.6 %collective-permute-start.31 = (bf16[256,1152]{1,0:T(8,128)(2,1)}, bf16[256,1152]{1,0:T(8,128)(2,1)S(1)}, u32[]{:S(2)}, u32[]{:S(2)}) collective-permute-start(bf16[256,1152]{1,0:T(8,128)(2,1)} %fusion.41), channel_id=1, source_target_pairs={{0,1},{1,0},{2,3},{3,2},{4,5},{5,4},{6,7},{7,6},{8,9},{9,8},{10,11... | collective-permute-start | bytes 1769480 | tf_op jit(solution)/shard_map/ppermute | solution.py:68
  656.6 166.3 %collective-permute-start.35 = (bf16[4,2,72,1728]{3,2,1,0:T(8,128)(2,1)}, bf16[4,2,72,1728]{3,2,1,0:T(8,128)(2,1)}, u32[]{:S(2)}, u32[]{:S(2)}) collective-permute-start(bf16[4,2,72,1728]{3,2,1,0:T(8,128)(2,1)} %dynamic-slice_bitcast_fusion), channel_id=1, source_target_pairs={{2,0},{0,2},{6,4},{4,6},{10,8},{8,10},{14,12},{12,14},{18,16},{16,... | collective-permute-start | bytes 5971976 | tf_op jit(solution)/shard_map/ppermute | solution.py:63
  720.7 58.9 %collective-permute-start.51 = (bf16[4,72,2112]{2,1,0:T(8,128)(2,1)}, bf16[4,72,2112]{2,1,0:T(8,128)(2,1)}, u32[]{:S(2)}, u32[]{:S(2)}) collective-permute-start(bf16[4,72,2112]{2,1,0:T(8,128)(2,1)} %dynamic-slice_bitcast_fusion.1), channel_id=1, source_target_pairs={{4,0},{6,2},{0,4},{2,6},{12,8},{14,10},{8,12},{10,14},{20,16},{22,... | collective-permute-start | bytes 3649544 | tf_op jit(solution)/shard_map/ppermute | solution.py:63
  735.4 46.9 %collective-permute-start.42 = (bf16[72,1728]{1,0:T(8,128)(2,1)}, bf16[72,1728]{1,0:T(8,128)(2,1)}, u32[]{:S(2)}, u32[]{:S(2)}) collective-permute-start(bf16[72,1728]{1,0:T(8,128)(2,1)} %get-tuple-element.207), channel_id=1, source_target_pairs={{24,0},{26,2},{28,4},{30,6},{0,8},{2,10},{4,12},{6,14},{8,16},{10,... | collective-permute-start | bytes 746504 | tf_op jit(solution)/shard_map/ppermute | solution.py:63
  828.9 46.3 %collective-permute-start.46 = (bf16[4,72,2112]{2,1,0:T(8,128)(2,1)S(1)}, bf16[4,72,2112]{2,1,0:T(8,128)(2,1)S(1)}, u32[]{:S(2)}, u32[]{:S(2)}) collective-permute-start(bf16[4,72,2112]{2,1,0:T(8,128)(2,1)S(1)} %dynamic-slice_bitcast_fusion.2), channel_id=1, source_target_pairs={{4,0},{6,2},{0,4},{2,6},{12,8},{14,10},{8,12},{10,14},{20,16},{22,... | collective-permute-start | bytes 3649544 | tf_op jit(solution)/shard_map/ppermute | solution.py:63
  (319 other events, 4721.2 us)
Sparse Core Ops, SparseCore 0:
  10.9 75.2 all-gather.10
  89.0 118.0 all-gather.6
  209.4 86.5 all-gather.8
  421.0 123.8 reduce-scatter.4
  580.7 95.9 reduce-scatter.2

commit v2 on v1

--- a/solution.py
+++ b/solution.py
@@ -1,6 +1,10 @@
+import functools
+
 import jax
 import jax.numpy as jnp
 from jax import lax
+from jax.experimental import pallas as pl
+from jax.experimental.pallas import tpu as pltpu
 from jax.sharding import PartitionSpec as P
 
 HD = 72
@@ -42,73 +46,447 @@
     return coords.astype(jnp.float32)[..., None] * frequency
 
 
-def row_factors():
-    size = lax.axis_size("rows")
-    return (4, size // 8, 2)
-
-
-def row_place():
-    sizes = row_factors()
-    index = lax.axis_index("rows")
-    return (index // (sizes[1] * sizes[2]), (index // sizes[2]) % sizes[1], index % sizes[2])
-
-
-def row_move(value, dim, step):
-    sizes = row_factors()
-    pairs = []
-    for target in range(lax.axis_size("rows")):
-        place = [target // (sizes[1] * sizes[2]), (target // sizes[2]) % sizes[1], target % sizes[2]]
-        place[dim] = (place[dim] + step) % sizes[dim]
-        pairs.append(((place[0] * sizes[1] + place[1]) * sizes[2] + place[2], target))
-    return lax.ppermute(value, "rows", pairs)
-
-
 def head_move(value, flip):
     size = lax.axis_size("heads")
     return lax.ppermute(value, "heads", [(index, index ^ flip) for index in range(size)])
 
 
-def in_order(chunks, mine, axis):
-    count = len(chunks)
-    placed = []
-    for slot in range(count):
-        value = chunks[0]
-        for step in range(1, count):
-            value = jnp.where(mine == (slot - step) % count, chunks[step], value)
-        placed.append(value)
-    return jnp.stack(placed, axis=axis)
-
-
-def gather_rows(shard):
-    sizes = row_factors()
-    place = row_place()
-    value = shard
-    for dim in range(3):
-        chunks = [value] + [row_move(value, dim, step) for step in range(1, sizes[dim])]
-        value = in_order(chunks, place[dim], dim)
-    return value.reshape(-1, shard.shape[-1])
-
-
-def scatter_rows(parts):
-    sizes = row_factors()
-    place = row_place()
-    pieces = [part.reshape(sizes + (-1, part.shape[-1])) for part in parts]
-    for dim in (2, 1, 0):
-        count = sizes[dim]
-
-        def pick(step):
-            taken = [
-                lax.dynamic_index_in_dim(piece, (place[dim] + step) % count, dim, keepdims=False)
-                for piece in pieces
-            ]
-            return taken[0] if len(taken) == 1 else jnp.concatenate(taken, axis=-1)
-
-        arrived = [row_move(pick(step), dim, count - step) for step in range(1, count)]
-        total = pick(0).astype(jnp.float32)
-        for item in arrived:
-            total = total + item.astype(jnp.float32)
-        pieces = [total.astype(jnp.bfloat16) if dim else total]
-    return pieces[0]
+MESH = pl.DeviceIdType.MESH
+
+
+class Place:
+    def __init__(self, row_size, head_size):
+        self.sizes = (4, row_size // 8, 2)
+        index = lax.axis_index("rows")
+        a, b, c = self.sizes
+        self.mine = (index // (b * c), (index // c) % b, index % c)
+        self.heads = head_size
+        self.head = lax.axis_index("heads")
+
+    def step(self, dim, by):
+        return (self.mine[dim] + by + self.sizes[dim]) % self.sizes[dim]
+
+    def row(self, a, b, c):
+        return (a * self.sizes[1] + b) * self.sizes[2] + c
+
+    def near(self, dim, by):
+        at = list(self.mine)
+        at[dim] = self.step(dim, by)
+        return {"rows": self.row(*at)}
+
+    def flip(self, by):
+        return {"heads": self.head ^ by}
+
+    def partners(self, with_heads):
+        found = [self.near(dim, by) for dim in range(3) for by in range(1, self.sizes[dim])]
+        if with_heads:
+            found += [self.flip(by) for by in range(1, self.heads)]
+        return found
+
+    def greet(self, with_heads):
+        barrier = pltpu.get_barrier_semaphore()
+        found = self.partners(with_heads)
+        for partner in found:
+            pl.semaphore_signal(barrier, inc=1, device_id=partner, device_id_type=MESH)
+        pl.semaphore_wait(barrier, len(found))
+
+
+def gather_count(row_size):
+    a, b, c = 4, row_size // 8, 2
+    return 2 * (a - 1) + (2 * a - 1) * (2 * b - 1)
+
+
+class Gather:
+    def __init__(self, place, shard, out, send, recv, local):
+        self.place, self.shard, self.out = place, shard, out
+        self.send, self.recv = send, recv
+        self.used = 0
+        self.keep = pltpu.make_async_copy(shard, out.at[place.row(*place.mine)], local)
+        a, b, _ = place.sizes
+        self.hops, self.along_b, self.along_c = {}, {}, {}
+        names = [(0, 0)] + [(way, k) for k in range(1, a) for way in (1, -1)]
+        for way, k in names:
+            if k:
+                self.hops[way, k] = self.copy(way, k - 1, 0, place.near(0, way))
+        for way, k in names:
+            for j in range(1, b):
+                self.along_b[way, k, j] = self.copy(way, k, 0, place.near(1, j))
+        for way, k in names:
+            for j in range(b):
+                self.along_c[way, k, j] = self.copy(way, k, j, place.near(2, 1))
+
+    def copy(self, way, k, j, device):
+        place, slot = self.place, self.used
+        self.used += 1
+        index = place.row(place.step(0, -way * k), place.step(1, -j), place.mine[2])
+        return pltpu.make_async_remote_copy(
+            src_ref=self.shard if k == 0 and j == 0 else self.out.at[index],
+            dst_ref=self.out.at[index],
+            send_sem=self.send.at[slot],
+            recv_sem=self.recv.at[slot],
+            device_id=device,
+            device_id_type=MESH,
+        )
+
+    def holds(self, way, k):
+        at = self.place.mine[0]
+        return at >= k if way > 0 else at < self.place.sizes[0] - k
+
+    def hop(self, way, k):
+        at = self.place.mine[0]
+        last = self.place.sizes[0] - 1
+        return (at < last) & (at >= k - 1) if way > 0 else (at > 0) & (at <= last - (k - 1))
+
+    def begin(self):
+        self.keep.start()
+        for way in (1, -1):
+            pl.when(self.hop(way, 1))(self.hops[way, 1].start)
+        self.pass_on(0, 0)
+
+    def pass_on(self, way, k):
+        for j in range(1, self.place.sizes[1]):
+            self.along_b[way, k, j].start()
+        self.along_c[way, k, 0].start()
+
+    def first(self, k):
+        for way in (1, -1):
+
+            @pl.when(self.holds(way, k))
+            def _():
+                self.hops[way, k].wait_recv()
+                if k + 1 < self.place.sizes[0]:
+                    pl.when(self.hop(way, k + 1))(self.hops[way, k + 1].start)
+                self.pass_on(way, k)
+
+    def each(self, way, k, action):
+        if k:
+            pl.when(self.holds(way, k))(action)
+        else:
+            action()
+
+    def second(self):
+        for way, k, j in self.along_b:
+
+            def action():
+                self.along_b[way, k, j].wait_recv()
+                self.along_c[way, k, j].start()
+
+            self.each(way, k, action)
+
+    def finish(self):
+        for way, k, j in self.along_c:
+
+            def action():
+                self.along_c[way, k, j].wait_recv()
+                self.along_c[way, k, j].wait_send()
+
+            self.each(way, k, action)
+        for way, k, j in self.along_b:
+            self.each(way, k, self.along_b[way, k, j].wait_send)
+        for way, k in self.hops:
+            pl.when(self.hop(way, k))(self.hops[way, k].wait_send)
+        self.keep.wait()
+
+
+def gather_all(items):
+    count = len(items)
+    items[0].begin()
+    for step in range(count + 1):
+        if step < count:
+            items[step].first(1)
+            if step + 1 < count:
+                items[step + 1].begin()
+            for k in range(2, items[step].place.sizes[0]):
+                items[step].first(k)
+        if step >= 1:
+            items[step - 1].second()
+    for item in items:
+        item.finish()
+
+
+def scatter_count(row_size):
+    a, b, c = 4, row_size // 8, 2
+    return a * b + a * (b - 1) + (a - 1)
+
+
+class Scatter:
+    def __init__(self, place, source, out, held, met, side, far, send, recv, load):
+        self.place, self.source, self.out = place, source, out
+        self.held, self.met, self.side, self.far = held, met, side, far
+        self.send, self.recv, self.load = send, recv, load
+
+    def remote(self, source, target, slot, device):
+        return pltpu.make_async_remote_copy(
+            src_ref=source,
+            dst_ref=target,
+            send_sem=self.send.at[slot],
+            recv_sem=self.recv.at[slot],
+            device_id=device,
+            device_id_type=MESH,
+        )
+
+    def across(self, k, j):
+        place = self.place
+        a, b = place.step(0, k), place.step(1, j)
+        other = place.step(2, 1)
+        return self.remote(
+            self.source.at[place.row(a, b, other)],
+            self.met.at[a, b],
+            k * place.sizes[1] + j,
+            place.near(2, 1),
+        )
+
+    def fetch(self, k, j):
+        place = self.place
+        a, b = place.step(0, k), place.step(1, j)
+        return pltpu.make_async_copy(
+            self.source.at[place.row(a, b, place.mine[2])],
+            self.held.at[a, b],
+            self.load.at[k * place.sizes[1] + j],
+        )
+
+    def along_b(self, k, j):
+        place = self.place
+        a, b = place.step(0, k), place.step(1, j)
+        base = place.sizes[0] * place.sizes[1]
+        return self.remote(
+            self.held.at[a, b],
+            self.side.at[j - 1, a],
+            base + (j - 1) * place.sizes[0] + k,
+            place.near(1, j),
+        )
+
+    def along_a(self, k):
+        place = self.place
+        base = place.sizes[0] * (2 * place.sizes[1] - 1)
+        return self.remote(
+            self.held.at[place.step(0, k), place.mine[1]],
+            self.far.at[k - 1],
+            base + k - 1,
+            place.near(0, k),
+        )
+
+    def order(self):
+        a, b, _ = self.place.sizes
+        return [(k, j) for j in list(range(1, b)) + [0] for k in list(range(1, a)) + [0]]
+
+    def begin(self):
+        for k, j in self.order():
+            self.fetch(k, j).start()
+            self.across(k, j).start()
+
+    def first(self):
+        place = self.place
+        a, b, _ = place.sizes
+        for j in range(1, b):
+            for k in list(range(1, a)) + [0]:
+                self.fetch(k, j).wait()
+                self.across(k, j).wait_recv()
+                at = (place.step(0, k), place.step(1, j))
+                self.held[at] = (
+                    self.held[at].astype(jnp.float32) + self.met[at].astype(jnp.float32)
+                ).astype(self.held.dtype)
+                self.along_b(k, j).start()
+
+    def total(self, k):
+        place = self.place
+        a, b = place.step(0, k), place.mine[1]
+        value = self.held[a, b].astype(jnp.float32) + self.met[a, b].astype(jnp.float32)
+        for j in range(1, place.sizes[1]):
+            value = value + self.side[j - 1, a].astype(jnp.float32)
+        return value
+
+    def second(self):
+        place = self.place
+        a, b, _ = place.sizes
+        for k in list(range(1, a)) + [0]:
+            self.fetch(k, 0).wait()
+            self.across(k, 0).wait_recv()
+            for j in range(1, b):
+                self.along_b(k, j).wait_recv()
+            if k:
+                self.held[place.step(0, k), place.mine[1]] = self.total(k).astype(self.held.dtype)
+                self.along_a(k).start()
+            else:
+                self.out[...] = self.total(0)
+
+    def finish(self):
+        place = self.place
+        a, b, _ = place.sizes
+        for k in range(1, a):
+            self.along_a(k).wait_recv()
+            self.out[...] = self.out[...] + self.far[k - 1].astype(jnp.float32)
+        for k, j in self.order():
+            self.across(k, j).wait_send()
+            if j:
+                self.along_b(k, j).wait_send()
+        for k in range(1, a):
+            self.along_a(k).wait_send()
+
+
+def scatter_all(items):
+    count = len(items)
+    for item in items:
+        item.begin()
+    for step in range(count + 2):
+        if step < count:
+            items[step].first()
+        if 1 <= step <= count:
+            items[step - 1].second()
+        if step >= 2:
+            items[step - 2].finish()
+
+
+def start_kernel(row_size, head_size, images, blocks, weights, *refs):
+    cond, ada, bias = refs[:3]
+    shards = refs[3 : 3 + weights]
+    outs = refs[3 + weights : 3 + 2 * weights]
+    mods = refs[3 + 2 * weights]
+    (conds, part, held, met, side, far, total, every, sends, recvs, keeps, mod_send, mod_recv, mod_load, head_send, head_recv) = refs[4 + 2 * weights :]
+    place = Place(row_size, head_size)
+    place.greet(True)
+    items = [
+        Gather(place, shard, out, sends.at[i], recvs.at[i], keeps.at[i])
+        for i, (shard, out) in enumerate(zip((cond,) + shards, (conds,) + outs))
+    ]
+    lead, bulk = items[0], items[1:]
+    lead.begin()
+    bulk[0].begin()
+    hops = range(1, place.sizes[0])
+    for k in hops:
+        lead.first(k)
+    lead.second()
+    lead.finish()
+    width = cond.shape[1]
+    share = ada.shape[1]
+    pad = cond.shape[0]
+    lane = lax.broadcasted_iota(jnp.int32, (width, share), 0)
+    slot = lax.broadcasted_iota(jnp.int32, (width, share), 1)
+    pick = jnp.where(lane == lax.axis_index("rows") * share + slot, 1.0, 0.0).astype(jnp.bfloat16)
+    mine = jnp.dot(
+        conds[...].reshape(row_size * pad, width), pick, preferred_element_type=jnp.float32
+    ).astype(jnp.bfloat16)
+    for b in range(blocks):
+        value = jnp.dot(mine, ada[b], preferred_element_type=jnp.float32)
+        part[:, b * images : (b + 1) * images, :] = value.reshape(row_size, pad, -1)[:, :images]
+    sums = Scatter(place, part, total, held, met, side, far, mod_send, mod_recv, mod_load)
+    sums.begin()
+    bulk[0].first(1)
+    for item in bulk[1:]:
+        item.begin()
+    sums.first()
+    for k in hops[1:]:
+        bulk[0].first(k)
+    sums.second()
+    for item in bulk[1:]:
+        for k in hops:
+            item.first(k)
+    sums.finish()
+    every[place.head] = total[...] + bias[...]
+    across = [
+        pltpu.make_async_remote_copy(
+            src_ref=every.at[place.head],
+            dst_ref=every.at[place.head],
+            send_sem=head_send.at[by - 1],
+            recv_sem=head_recv.at[by - 1],
+            device_id=place.flip(by),
+            device_id_type=MESH,
+        )
+        for by in range(1, head_size)
+    ]
+    for copy in across:
+        copy.start()
+    for item in bulk:
+        item.second()
+    for copy in across:
+        copy.wait()
+    mods[...] = every[...]
+    for item in bulk:
+        item.finish()
+
+
+def start_call(row_size, head_size, cond, ada, bias, shards):
+    images = bias.shape[0] // ada.shape[0]
+    blocks = ada.shape[0]
+    count = len(shards)
+    a, b = 4, row_size // 8
+    chunk = bias.shape
+    copies = gather_count(row_size)
+    anywhere = pl.BlockSpec(memory_space=pl.ANY)
+    vmem = pl.BlockSpec(memory_space=pltpu.VMEM)
+    f32 = jnp.float32
+    return pl.pallas_call(
+        functools.partial(start_kernel, row_size, head_size, images, blocks, count),
+        out_shape=[jax.ShapeDtypeStruct((row_size,) + item.shape, item.dtype) for item in shards]
+        + [jax.ShapeDtypeStruct((head_size,) + chunk, f32)],
+        in_specs=[vmem] * 3 + [anywhere] * count,
+        out_specs=[anywhere] * count + [vmem],
+        scratch_shapes=[
+            pltpu.VMEM((row_size,) + cond.shape, cond.dtype),
+            pltpu.VMEM((row_size,) + chunk, f32),
+            pltpu.VMEM((a, b) + chunk, f32),
+            pltpu.VMEM((a, b) + chunk, f32),
+            pltpu.VMEM((b - 1, a) + chunk, f32),
+            pltpu.VMEM((a - 1,) + chunk, f32),
+            pltpu.VMEM(chunk, f32),
+            pltpu.VMEM((head_size,) + chunk, f32),
+            pltpu.SemaphoreType.DMA((count + 1, copies)),
+            pltpu.SemaphoreType.DMA((count + 1, copies)),
+            pltpu.SemaphoreType.DMA((count + 1,)),
+            pltpu.SemaphoreType.DMA((scatter_count(row_size),)),
+            pltpu.SemaphoreType.DMA((scatter_count(row_size),)),
+            pltpu.SemaphoreType.DMA((a * b,)),
+            pltpu.SemaphoreType.DMA((head_size - 1,)),
+            pltpu.SemaphoreType.DMA((head_size - 1,)),
+        ],
+        compiler_params=pltpu.CompilerParams(
+            collective_id=1, has_side_effects=True, vmem_limit_bytes=48 * 2**20
+        ),
+        name="start",
+    )(cond, ada, bias, *shards)
+
+
+def scatter_kernel(row_size, head_size, count, *refs):
+    ins, outs = refs[:count], refs[count : 2 * count]
+    scratch = refs[2 * count : 6 * count]
+    send, recv, load = refs[6 * count :]
+    place = Place(row_size, head_size)
+    place.greet(False)
+    scatter_all(
+        [
+            Scatter(
+                place, ins[i], outs[i], *scratch[4 * i : 4 * i + 4], send.at[i], recv.at[i], load.at[i]
+            )
+            for i in range(count)
+        ]
+    )
+
+
+def scatter_call(row_size, head_size, grads):
+    count = len(grads)
+    copies = scatter_count(row_size)
+    a, b = 4, row_size // 8
+    scratch = []
+    for grad in grads:
+        chunk = grad.shape[1:]
+        for lead in ((a, b), (a, b), (b - 1, a), (a - 1,)):
+            scratch.append(pltpu.VMEM(lead + chunk, grad.dtype))
+    return pl.pallas_call(
+        functools.partial(scatter_kernel, row_size, head_size, count),
+        out_shape=[jax.ShapeDtypeStruct(grad.shape[1:], jnp.float32) for grad in grads],
+        in_specs=[pl.BlockSpec(memory_space=pl.ANY)] * count,
+        out_specs=[pl.BlockSpec(memory_space=pltpu.VMEM)] * count,
+        scratch_shapes=scratch
+        + [
+            pltpu.SemaphoreType.DMA((count, copies)),
+            pltpu.SemaphoreType.DMA((count, copies)),
+            pltpu.SemaphoreType.DMA((count, a * b)),
+        ],
+        compiler_params=pltpu.CompilerParams(
+            collective_id=2, has_side_effects=True, vmem_limit_bytes=56 * 2**20
+        ),
+        name="sum_rows",
+    )(*grads)
 
 
 def rope_parts(coords):
@@ -172,22 +550,23 @@
     return (grad_query, grad_key, grad_value)
 
 
-def spread(values):
-    return jnp.concatenate(
-        [values] + [head_move(values, flip) for flip in range(1, lax.axis_size("heads"))], axis=0
-    )
-
-
-def collect(operand, product, own_rows):
+def spread(values, beside=()):
+    arrived = [head_move(values, flip) for flip in range(1, lax.axis_size("heads"))]
+    arrived, beside = lax.optimization_barrier((arrived, beside))
+    return jnp.concatenate([values] + arrived, axis=0), beside
+
+
+def collect(operand, product, own_rows, beside=()):
     total = None
     arrived = []
     for flip in range(1, lax.axis_size("heads")):
         partial = product(operand[flip * own_rows : (flip + 1) * own_rows])
         arrived.append(head_move(partial.astype(jnp.bfloat16), flip))
     total = product(operand[:own_rows])
+    total, arrived, beside = lax.optimization_barrier((total, arrived, beside))
     for item in arrived:
         total = total + item.astype(jnp.float32)
-    return total
+    return total, beside
 
 
 def plain_dot(operand, other):
@@ -208,7 +587,7 @@
     own_rows = residual.shape[0]
     count_rows, row_len = image_ids.shape
     normed_attn, inverse_attn = normalize(residual)
-    input_attn = spread((normed_attn * (1.0 + scale_attn) + shift_attn).astype(jnp.bfloat16))
+    input_attn, _ = spread((normed_attn * (1.0 + scale_attn) + shift_attn).astype(jnp.bfloat16))
     packed = plain_dot(input_attn, qkv_full) + qkv_b
     heads_here = packed.shape[1] // (3 * HD)
     packed = packed.reshape(count_rows, row_len, heads_here, 3, HD)
@@ -217,16 +596,16 @@
     value_rows = packed[:, :, :, 2].astype(jnp.bfloat16)
     attended, logsum = attend(queries, key_rows, value_rows, image_ids)
     attended = attended.reshape(count_rows * row_len, heads_here * HD)
-    branch = collect(attended, lambda rows: tail_dot(rows, proj_t), own_rows)
+    branch, _ = collect(attended, lambda rows: tail_dot(rows, proj_t), own_rows)
     middle = residual + gate_attn * branch
     normed_mlp, inverse_mlp = normalize(middle)
-    input_mlp = spread((normed_mlp * (1.0 + scale_mlp) + shift_mlp).astype(jnp.bfloat16))
+    input_mlp, _ = spread((normed_mlp * (1.0 + scale_mlp) + shift_mlp).astype(jnp.bfloat16))
     gate_up = plain_dot(input_mlp, gu_full)
     hidden_width = gate_up.shape[1] // 2
     gate_part = gate_up[:, :hidden_width]
     up_part = gate_up[:, hidden_width:]
     hidden = (jax.nn.silu(gate_part) * up_part).astype(jnp.bfloat16)
-    mlp_out = collect(hidden, lambda rows: tail_dot(rows, down_t), own_rows)
+    mlp_out, _ = collect(hidden, lambda rows: tail_dot(rows, down_t), own_rows)
     result = middle + gate_mlp * mlp_out
     stored = (
         normed_attn,
@@ -273,7 +652,7 @@
     count_rows, row_len = image_ids.shape
     grad_mlp = (gate_mlp * incoming).astype(jnp.bfloat16)
     grad_gate_mlp = incoming * mlp_out
-    gathered_mlp = spread(grad_mlp)
+    gathered_mlp, _ = spread(grad_mlp)
     down_grad = lead_dot(gathered_mlp, hidden).astype(jnp.bfloat16)
     grad_hidden = plain_dot(gathered_mlp, down_t)
     logistic = jax.nn.sigmoid(gate_part)
@@ -281,16 +660,16 @@
     grad_up_part = grad_hidden * gate_part * logistic
     grad_gate_up = jnp.concatenate([grad_gate_part, grad_up_part], axis=1).astype(jnp.bfloat16)
     gu_grad = lead_dot(input_mlp, grad_gate_up).astype(jnp.bfloat16)
+    grad_input_mlp, gu_grad = collect(
+        grad_gate_up, lambda rows: tail_dot(rows, gu_full), own_rows, gu_grad
+    )
     gu_out = lax.psum_scatter(gu_grad, "rows", scatter_dimension=0, tiled=True).astype(jnp.float32)
-    grad_input_mlp = collect(grad_gate_up, lambda rows: tail_dot(rows, gu_full), own_rows)
     grad_middle = incoming + norm_back(grad_input_mlp * (1.0 + scale_mlp), normed_mlp, inverse_mlp)
     grad_branch = (gate_attn * grad_middle).astype(jnp.bfloat16)
     grad_gate_attn = grad_middle * branch
     heads_here = queries.shape[2]
-    gathered_branch = spread(grad_branch)
+    gathered_branch, down_grad = spread(grad_branch, down_grad)
     proj_grad = lead_dot(gathered_branch, attended).astype(jnp.bfloat16)
-    side = scatter_rows([down_grad, proj_grad])
-    down_out, proj_out = side[:, : hidden.shape[1]], side[:, hidden.shape[1] :]
     grad_attended = plain_dot(gathered_branch, proj_t).astype(jnp.bfloat16)
     grad_attended = grad_attended.reshape(count_rows, row_len, heads_here, HD)
     grad_query, grad_key, grad_value = attend_back(
@@ -305,8 +684,9 @@
     )
     qkv_bias_grad = jnp.sum(grad_packed, axis=0, dtype=jnp.float32)
     qkv_grad = lead_dot(input_attn, grad_packed).astype(jnp.bfloat16)
-    qkv_out = scatter_rows([qkv_grad])
-    grad_input_attn = collect(grad_packed, lambda rows: tail_dot(rows, qkv_full), own_rows)
+    grad_input_attn, (qkv_grad, proj_grad) = collect(
+        grad_packed, lambda rows: tail_dot(rows, qkv_full), own_rows, (qkv_grad, proj_grad)
+    )
     grad_input = grad_middle + norm_back(
         grad_input_attn * (1.0 + scale_attn), normed_attn, inverse_attn
     )
@@ -321,7 +701,7 @@
         ],
         axis=1,
     )
-    return (grad_input, grad_mods, (qkv_out, qkv_bias_grad, proj_out, gu_out, down_out))
+    return (grad_input, grad_mods, (qkv_grad, qkv_bias_grad, proj_grad, gu_out, down_grad))
 
 
 def heads_in_order(value):
@@ -390,35 +770,39 @@
     geometry = lax.optimization_barrier(
         rope_parts(device_order(grid_row)) + rope_parts(device_order(grid_col))
     )
-    qkv_full = [None] * block_count
-    gu_full = [None] * block_count
-    down_t = [None] * block_count
-    proj_t = [None] * block_count
     shard_rows = qkv_weight.shape[1]
+
+    def gathered(shard):
+        return lax.all_gather(shard, "rows", axis=0, tiled=True)
+
+    cond_wide = cond.astype(jnp.float32)
+    cond_act = jax.nn.silu(cond_wide).astype(jnp.bfloat16)
+    pad = -image_count % 16
+    bias_rows = jnp.repeat(ada_bias.astype(jnp.float32), image_count, axis=0)
+    first_qkv, first_proj, mods = start_call(
+        row_size,
+        head_size,
+        jnp.pad(cond_act, ((0, pad), (0, 0))),
+        ada_weight,
+        bias_rows,
+        [qkv_weight[0], proj_weight[0].T],
+    )
+    qkv_full, gu_full, down_t, proj_t = [], [], [], []
     for b in range(block_count):
         if b == 0:
-            qkv_full[b] = lax.all_gather(qkv_weight[b], "rows", axis=0, tiled=True)
+            qkv_full.append(first_qkv.reshape(-1, first_qkv.shape[-1]))
+            proj_t.append(first_proj.reshape(-1, first_proj.shape[-1]))
         else:
-            qkv_full[b] = gather_rows(qkv_weight[b])
-        gu_full[b] = lax.all_gather(
-            gu_weight[b].reshape(shard_rows, -1), "rows", axis=0, tiled=True
-        )
-        side = gather_rows(jnp.concatenate([down_weight[b].T, proj_weight[b].T], axis=1))
-        down_t[b] = side[:, : down_weight.shape[1]]
-        proj_t[b] = side[:, down_weight.shape[1] :]
-    cond_wide = cond.astype(jnp.float32)
-    cond_act = jax.nn.silu(cond_wide).astype(jnp.bfloat16)
+            qkv_full.append(gathered(qkv_weight[b]))
+            proj_t.append(gathered(proj_weight[b].T))
+        gu_full.append(gathered(gu_weight[b].reshape(shard_rows, -1)))
+        down_t.append(gathered(down_weight[b].T))
+    mod_all = mods.reshape(head_size, block_count, image_count, -1)
     cond_mine = lax.all_to_all(
         cond_act.reshape(image_count, row_size, -1).transpose(1, 0, 2), "rows", 0, 0
     ).reshape(row_size * image_count, -1)
-    mod_partial = jnp.stack([plain_dot(cond_mine, ada_weight[b]) for b in range(block_count)], axis=1)
-    mod_arrived = lax.all_to_all(
-        mod_partial.reshape(row_size, image_count, block_count, -1), "rows", 0, 0
-    )
-    mod_local = jnp.sum(mod_arrived, axis=0) + ada_bias.astype(jnp.float32)[None]
-    mod_all = heads_in_order(mod_local)
     modulation = [
-        jnp.concatenate([mod_all[index, :, b] for index in range(head_size)], axis=1)
+        jnp.concatenate([mod_all[index, b] for index in range(head_size)], axis=1)
         for b in range(block_count)
     ]
     pieces = [
@@ -442,9 +826,7 @@
     block_out = residual.astype(jnp.bfloat16)
     incoming = cotangent.astype(jnp.float32)
     block_grads = [None] * block_count
-    ada_grads = [None] * block_count
-    ada_bias_grads = [None] * block_count
-    cond_partial = 0.0
+    image_sums = [None] * block_count
     for b in reversed(range(block_count)):
         incoming, grad_mods, gradients = block_backward(
             incoming,
@@ -457,15 +839,37 @@
             image_ids,
             geometry,
         )
-        image_sums = lax.dot_general(
+        image_sums[b] = lax.dot_general(
             picker, grad_mods, (((0,), (0,)), ((), ())), precision=highest
         )
-        image_grads = heads_share(image_sums).astype(jnp.bfloat16)
-        all_grads = lax.all_gather(image_grads, "rows", axis=0, tiled=True)
-        ada_grads[b] = lead_dot(cond_mine, all_grads)
-        ada_bias_grads[b] = jnp.sum(all_grads, axis=0, dtype=jnp.float32)
-        cond_partial = cond_partial + tail_dot(all_grads, ada_weight[b])
         block_grads[b] = gradients
+    image_grads = heads_share(jnp.stack(image_sums)).astype(jnp.bfloat16)
+    bias_sums = jnp.stack([item[1] for item in block_grads])
+    bias_high = bias_sums.astype(jnp.bfloat16)
+    bias_rest = bias_sums - bias_high.astype(jnp.float32)
+    bias_middle = bias_rest.astype(jnp.bfloat16)
+    bias_low = (bias_rest - bias_middle.astype(jnp.float32)).astype(jnp.bfloat16)
+    small = jnp.concatenate(
+        [
+            image_grads.reshape(1, -1),
+            bias_high.reshape(1, -1),
+            bias_middle.reshape(1, -1),
+            bias_low.reshape(1, -1),
+        ],
+        axis=1,
+    )
+    small = lax.all_gather(small, "rows", axis=0, tiled=True)
+    split = image_grads.size
+    all_grads = small[:, :split].reshape((row_size,) + image_grads.shape)
+    bias_all = small[:, split:].reshape((row_size, 3) + bias_sums.shape).astype(jnp.float32)
+    qkv_bias_out = jnp.sum(bias_all, axis=(0, 1))
+    ada_grads = []
+    cond_partial = 0.0
+    for b in range(block_count):
+        block_grads_all = all_grads[:, b].reshape(row_size * image_count, -1)
+        ada_grads.append(lead_dot(cond_mine, block_grads_all))
+        cond_partial = cond_partial + tail_dot(block_grads_all, ada_weight[b])
+    ada_bias_grads = jnp.sum(all_grads, axis=(0, 2), dtype=jnp.float32)
     cond_parts = lax.all_to_all(
         cond_partial.astype(jnp.bfloat16).reshape(row_size, image_count, -1), "rows", 0, 0
     )
@@ -475,18 +879,24 @@
         cond_total = cond_total + head_move(cond_rows.astype(jnp.bfloat16), flip).astype(jnp.float32)
     logistic = jax.nn.sigmoid(cond_wide)
     cond_grad = cond_total * logistic * (1.0 + cond_wide * (1.0 - logistic))
-    qkv_bias_out = lax.psum(jnp.stack([item[1] for item in block_grads]), "rows")
+    parts = []
+    for b in reversed(range(block_count)):
+        parts += [block_grads[b][4], block_grads[b][2], block_grads[b][0]]
+    sums = scatter_call(
+        row_size, head_size, [part.reshape(row_size, shard_rows, -1) for part in parts]
+    )
+    sums = [sums[3 * b : 3 * b + 3] for b in reversed(range(block_count))]
     return (
         block_out,
         incoming,
         cond_grad,
         jnp.stack(ada_grads),
-        jnp.stack(ada_bias_grads),
-        jnp.stack([item[0] for item in block_grads]),
+        ada_bias_grads,
+        jnp.stack([item[2] for item in sums]),
         qkv_bias_out,
-        jnp.stack([item[2].T for item in block_grads]),
+        jnp.stack([item[1].T for item in sums]),
         jnp.stack([item[3].reshape(gu_weight.shape[1:]) for item in block_grads]),
-        jnp.stack([item[4].T for item in block_grads]),
+        jnp.stack([item[0].T for item in sums]),
     )
 
 

time: 928 us -> 853 us (0.919)
  Pallas kernels: 0 us -> 235 us
  blocking collectives: 138 us -> 0 us
  waiting for transfers between devices: 335 us -> 277 us
  starting transfers between devices: 80.4 us -> 35.9 us
  other arithmetic: 94.9 us -> 58.9 us
  local copies, waits for them, and re-layouts: 89.8 us -> 69.9 us
  matrix products: 166 us -> 154 us
    pallas_call x0 -> x2, Pallas kernels: none -> 235 us  [the longest x1 147 us: scatter_call(): pl.pallas_call(functools.partial(scatter_kernel, row_size, head_size, cou...]
    ppermute x35 -> x0, waiting for transfers between devices: 206 us -> none  [row_move(): return lax.ppermute(value, 'rows', pairs)]
    all_gather x2 -> x0, blocking collectives: 78.6 us -> none  [shards(): all_grads = lax.all_gather(image_grads, 'rows', axis=0, tiled=True)]
    all_gather x3 -> x7, waiting for transfers between devices: 0.02 us -> 75 us  [the longest x6 75 us: gathered(): return lax.all_gather(shard, 'rows', axis=0, tiled=True)]
    reduce_scatter x2, waiting for transfers between devices: 0.02 us -> 71 us  [block_backward(): lax.psum_scatter(gu_grad, 'rows', scatter_dimension=0, tiled=True)]
    psum x1 -> x0, blocking collectives: 58.9 us -> none  [shards(): lax.psum(jnp.stack([item[1] for item in block_grads]), 'rows')]
    all_to_all x1, waiting for transfers between devices: 44.6 us -> 0.01 us  [shards(): lax.all_to_all(cond_act.reshape(image_count, row_size, -1).transpose(1, 0...]
    ppermute x20 -> x18, waiting for transfers between devices: 81.3 us -> 125 us  [head_move(): lax.ppermute(value, 'heads', [(index, index ^ flip) for index in range(si...]
  transfers between devices with their start and end apart: 63 -> 29, of which waited for: 25 -> 22; matrix products, arithmetic and copies ran while one was open for 34% -> 21% of each run, Pallas kernels for 0% -> 28%
where the time goes in v2:
time: 853 us; the launch traced here: 848 us
  waiting for transfers between devices  277 us (32%)
  Pallas kernels  235 us (28%)
  matrix products  154 us (18%)
  local copies, waits for them, and re-layouts  69.9 us (8%)
  other arithmetic  58.9 us (7%)
  starting transfers between devices  35.9 us (4%)
  between operations  17.8 us (2%)
    pallas_call x1, Pallas kernels, scatter_call(): pl.pallas_call(functools.partial(scatter_kernel, row_size, head_size, cou...  147 us
    ppermute x18, waiting for transfers between devices, head_move(): lax.ppermute(value, 'heads', [(index, index ^ flip) for index in range(si...  125 us
    pallas_call x1, Pallas kernels, start_call(): pl.pallas_call(functools.partial(start_kernel, row_size, head_size, image...  88.9 us
    all_gather x6, waiting for transfers between devices, gathered(): return lax.all_gather(shard, 'rows', axis=0, tiled=True)  75 us
    reduce_scatter x2, waiting for transfers between devices, block_backward(): lax.psum_scatter(gu_grad, 'rows', scatter_dimension=0, tiled=True)  71 us
    dot_general x18, matrix products, tail_dot(): lax.dot_general(operand, other, (((1,), (1,)), ((), ())), preferred_eleme...  50.5 us
    dot_general x8, matrix products, plain_dot(): return jnp.dot(operand, other, preferred_element_type=jnp.float32)  39.6 us
    dot_general x10, matrix products, lead_dot(): lax.dot_general(operand, other, (((0,), (0,)), ((), ())), preferred_eleme...  37.3 us
  transfers between devices with their start and end apart: 29, of which 22 were waited for; matrix products, arithmetic and copies ran while one was open for 21% of the time, Pallas kernels for 28%

profile of v2, /device:TPU:0, one launch (start us, length us, event | category | flops | bytes accessed | tf_op | source)
XLA Modules:
  0.0 848.3 jit_solution(53690937174510083)
XLA Ops:
  14.4 88.9 %start.1 = (bf16[16,72,1728]{2,1,0:T(8,128)(2,1)}, bf16[16,72,576]{2,1,0:T(8,128)(2,1)S(1)}, f32[2,8,3456]{2,1,0:T(8,128)S(1)}) custom-call(bf16[16,1152]{1,0:T(8,128)(2,1)S(1)} %pad.4.refs_0_, bf16[2,72,3456]{2,1,0:T(8,128)(2,1)S(1)} %copy-done.2, f32[8,3456]{1,0:T(8,128)S(1)} %reshape.938.refs_2_, bf16[72,1728]{1,0:T(8,128)(2,1)S(1)} %get-tuple-element.243.refs_3_, ...), custom_call_target="tpu_custom_call" | custom-call | tf_op jit(solution)/shard_map/start/pallas_call | solution.py:418
  112.8 10.9 %collective-permute-done = bf16[256,1152]{1,0:T(8,128)(2,1)} collective-permute-done((bf16[256,1152]{1,0:T(8,128)(2,1)S(1)}, bf16[256,1152]{1,0:T(8,128)(2,1)}, u32[]{:S(2)}, u32[]{:S(2)}) %collective-permute-start) | collective-permute-done | bytes 589856 | tf_op jit(solution)/shard_map/ppermute | solution.py:51
  141.1 12.3 %collective-permute-done.1 = bf16[256,1152]{1,0:T(8,128)(2,1)S(1)} collective-permute-done((bf16[256,1152]{1,0:T(8,128)(2,1)S(1)}, bf16[256,1152]{1,0:T(8,128)(2,1)S(1)}, u32[]{:S(2)}, u32[]{:S(2)}) %collective-permute-start.1) | collective-permute-done | bytes 589856 | tf_op jit(solution)/shard_map/ppermute | solution.py:51
  157.8 12.5 %collective-permute-done.2 = bf16[256,1152]{1,0:T(8,128)(2,1)} collective-permute-done((bf16[256,1152]{1,0:T(8,128)(2,1)S(1)}, bf16[256,1152]{1,0:T(8,128)(2,1)}, u32[]{:S(2)}, u32[]{:S(2)}) %collective-permute-start.2) | collective-permute-done | bytes 589856 | tf_op jit(solution)/shard_map/ppermute | solution.py:51
  170.3 6.6 fusion.76
  189.5 9.2 %collective-permute-done.3 = bf16[256,1152]{1,0:T(8,128)(2,1)S(1)} collective-permute-done((bf16[256,1152]{1,0:T(8,128)(2,1)S(1)}, bf16[256,1152]{1,0:T(8,128)(2,1)S(1)}, u32[]{:S(2)}, u32[]{:S(2)}) %collective-permute-start.3) | collective-permute-done | bytes 589856 | tf_op jit(solution)/shard_map/ppermute | solution.py:51
  204.9 10.4 %collective-permute-done.4 = bf16[256,1152]{1,0:T(8,128)(2,1)S(1)} collective-permute-done((bf16[256,1152]{1,0:T(8,128)(2,1)S(1)}, bf16[256,1152]{1,0:T(8,128)(2,1)S(1)}, u32[]{:S(2)}, u32[]{:S(2)}) %collective-permute-start.4) | collective-permute-done | bytes 589856 | tf_op jit(solution)/shard_map/ppermute | solution.py:51
  215.3 4.9 fusion.18
  230.7 12.7 %all-gather.14.cloned.1.call-done = bf16[1152,576]{1,0:T(8,128)(2,1)} async-done(((bf16[72,576]{1,0:T(8,128)(2,1)}), bf16[1152,576]{1,0:T(8,128)(2,1)}) %all-gather.14.cloned.1.call-update) | async-done | bytes 1327120 | tf_op jit(solution)/shard_map/all_gather | solution.py:776
  250.3 12.5 %collective-permute-done.5 = bf16[256,1152]{1,0:T(8,128)(2,1)S(1)} collective-permute-done((bf16[256,1152]{1,0:T(8,128)(2,1)}, bf16[256,1152]{1,0:T(8,128)(2,1)S(1)}, u32[]{:S(2)}, u32[]{:S(2)}) %collective-permute-start.5) | collective-permute-done | bytes 589856 | tf_op jit(solution)/shard_map/ppermute | solution.py:51
  268.5 7.0 collective-permute-done.8
  276.3 11.3 %collective-permute-done.6 = bf16[256,1152]{1,0:T(8,128)(2,1)} collective-permute-done((bf16[256,1152]{1,0:T(8,128)(2,1)S(1)}, bf16[256,1152]{1,0:T(8,128)(2,1)}, u32[]{:S(2)}, u32[]{:S(2)}) %collective-permute-start.6) | collective-permute-done | bytes 589856 | tf_op jit(solution)/shard_map/ppermute | solution.py:51
  287.6 24.1 %all-gather.16.cloned.1.call-done = bf16[1152,3072]{1,0:T(8,128)(2,1)} async-done(((bf16[72,3072]{1,0:T(8,128)(2,1)}), bf16[1152,3072]{1,0:T(8,128)(2,1)}) %all-gather.16.cloned.1.call-update) | async-done | bytes 7077904 | tf_op jit(solution)/shard_map/all_gather | solution.py:776
  311.6 10.2 %fusion.75 = f32[512,3072]{1,0:T(8,128)} fusion(bf16[1152,3072]{1,0:T(8,128)(2,1)} %all-gather.16.cloned.1.call-done, bf16[256,1152]{1,0:T(8,128)(2,1)} %collective-permute-done.6, bf16[256,1152]{1,0:T(8,128)(2,1)S(1)} %add_convert_fusion.1), kind=kOutput, calls=%fused_computation.194 | convolution fusion | flops 3626237952 | bytes 14548992 | tf_op jit(solution)/shard_map/dot_general | solution.py:573
  321.9 38.2 %all-gather.18.cloned.1.call-done = bf16[1152,1536]{1,0:T(8,128)(2,1)} async-done(((bf16[72,1536]{1,0:T(8,128)(2,1)}), bf16[1152,1536]{1,0:T(8,128)(2,1)}) %all-gather.18.cloned.1.call-update) | async-done | bytes 3538960 | tf_op jit(solution)/shard_map/all_gather | solution.py:776
  360.0 7.4 multiply_convert_fusion.4
  371.3 7.5 convolution_convert_fusion.1
  378.8 5.9 convolution_convert_fusion.12
  385.4 5.2 fusion.30
  390.7 9.3 %collective-permute-done.9 = bf16[256,1152]{1,0:T(8,128)(2,1)S(1)} collective-permute-done((bf16[256,1152]{1,0:T(8,128)(2,1)S(1)}, bf16[256,1152]{1,0:T(8,128)(2,1)S(1)}, u32[]{:S(2)}, u32[]{:S(2)}) %collective-permute-start.9) | collective-permute-done | bytes 589856 | tf_op jit(solution)/shard_map/ppermute | solution.py:51
  410.0 7.6 collective-permute-done.10
  464.8 5.0 collective-permute-done.12
  474.7 7.6 convolution_convert_fusion
  482.3 5.6 convolution_convert_fusion.11
  488.6 5.6 fusion.25
  494.3 5.4 collective-permute-done.13
  537.5 5.5 convolution_convert_fusion.2
  566.8 6.6 copy.118
  575.0 6.4 copy.120
  581.4 146.5 %sum_rows.1 = (f32[72,1536]{1,0:T(8,128)}, f32[72,576]{1,0:T(8,128)}, f32[72,1728]{1,0:T(8,128)}, f32[72,1536]{1,0:T(8,128)}, f32[72,576]{1,0:T(8,128)}, /*index=5*/f32[72,1728]{1,0:T(8,128)}) custom-call(bf16[16,72,1536]{2,1,0:T(8,128)(2,1)} %bitcast.309, bf16[16,72,576]{2,1,0:T(8,128)(2,1)} %bitcast.285, bf16[16,72,1728]{2,1,0:T(8,128)(2,1)} %bitcast.274, ...), custom_call_target="tpu_custom_call" | custom-call | tf_op jit(solution)/shard_map/sum_rows/pallas_call | solution.py:474
  743.2 11.3 %all-to-all-start = ((bf16[16,4,72]{2,1,0:T(4,128)(2,1)}), bf16[16,4,72]{2,1,0:T(4,128)(2,1)S(1)}, u32[]{:S(2)}, u32[]{:S(2)}) async-start(bf16[16,4,72]{2,1,0:T(4,128)(2,1)} %bitcast.97), calls=%async_computation | async-start | bytes 32768 | tf_op jit(solution)/shard_map/all_to_all | solution.py:873
  766.8 71.0 %reduce-scatter.3.cloned.1.call-done = bf16[72,3072]{1,0:T(8,128)(2,1)} async-done(((bf16[1152,3072]{1,0:T(8,128)(2,1)}), bf16[72,3072]{1,0:T(8,128)(2,1)}) %reduce-scatter.3.cloned.1.call-update) | async-done | bytes 442384 | tf_op jit(solution)/shard_map/reduce_scatter | solution.py:666
  (785 shorter events, 239.3 us)
Async XLA Ops:
  7.2 163.1 %all-gather.10.cloned.1.call-start = ((), (), s32[]{:S(2)}) async-start(), calls=%async_computation.4 | async-start | bytes 7520256 | tf_op jit(solution)/shard_map/all_gather | solution.py:776
  9.9 171.7 %all-gather.12.cloned.1.call-start = ((), (), s32[]{:S(2)}) async-start(), calls=%async_computation.5 | async-start | bytes 3760128 | tf_op jit(solution)/shard_map/all_gather | solution.py:776
  10.8 204.5 %all-gather.20.cloned.1.call-start = ((), (), s32[]{:S(2)}) async-start(), calls=%async_computation.11 | async-start | bytes 4386816 | tf_op jit(solution)/shard_map/all_gather | solution.py:776
  11.6 231.9 %all-gather.14.cloned.1.call-start = ((), (), s32[]{:S(2)}) async-start(), calls=%async_computation.6 | async-start | bytes 1566720 | tf_op jit(solution)/shard_map/all_gather | solution.py:776
  12.3 299.3 %all-gather.16.cloned.1.call-start = ((), (), s32[]{:S(2)}) async-start(), calls=%async_computation.7 | async-start | bytes 7520256 | tf_op jit(solution)/shard_map/all_gather | solution.py:776
  13.3 346.8 %all-gather.18.cloned.1.call-start = ((), (), s32[]{:S(2)}) async-start(), calls=%async_computation.8 | async-start | bytes 3760128 | tf_op jit(solution)/shard_map/all_gather | solution.py:776
  13.9 250.1 %copy-start.114 = (pred[256]{0:T(512)(128)(4,1)}, pred[256]{0:T(512)(128)(4,1)S(1)}, u32[]{:S(2)}) copy-start(pred[256]{0:T(512)(128)(4,1)S(1)} %get-tuple-element.267) | copy-start | bytes 772
  13.9 250.1 %copy-start.119 = (pred[256]{0:T(512)(128)(4,1)}, pred[256]{0:T(512)(128)(4,1)S(1)}, u32[]{:S(2)}) copy-start(pred[256]{0:T(512)(128)(4,1)S(1)} %get-tuple-element.268) | copy-start | bytes 772
  13.9 250.1 %copy-start.124 = (pred[256]{0:T(512)(128)(4,1)}, pred[256]{0:T(512)(128)(4,1)S(1)}, u32[]{:S(2)}) copy-start(pred[256]{0:T(512)(128)(4,1)S(1)} %get-tuple-element.269) | copy-start | bytes 772
  107.9 15.8 %collective-permute-start = (bf16[256,1152]{1,0:T(8,128)(2,1)S(1)}, bf16[256,1152]{1,0:T(8,128)(2,1)}, u32[]{:S(2)}, u32[]{:S(2)}) collective-permute-start(bf16[256,1152]{1,0:T(8,128)(2,1)S(1)} %fusion.53), channel_id=1, source_target_pairs={{0,1},{1,0},{2,3},{3,2},{4,5},{5,4},{6,7},{7,6},{8,9},{9,8},{10,11... | collective-permute-start | bytes 1769480 | tf_op jit(solution)/shard_map/ppermute | solution.py:51
  138.7 14.8 %collective-permute-start.1 = (bf16[256,1152]{1,0:T(8,128)(2,1)S(1)}, bf16[256,1152]{1,0:T(8,128)(2,1)S(1)}, u32[]{:S(2)}, u32[]{:S(2)}) collective-permute-start(bf16[256,1152]{1,0:T(8,128)(2,1)S(1)} %convolution_convert_fusion.14), channel_id=1, source_target_pairs={{0,1},{1,0},{2,3},{3,2},{4,5},{5,4},{6,7},{7,6},{8,9},{9,8},{10,11... | collective-permute-start | bytes 1769480 | tf_op jit(solution)/shard_map/ppermute | solution.py:51
  156.3 14.0 %collective-permute-start.2 = (bf16[256,1152]{1,0:T(8,128)(2,1)S(1)}, bf16[256,1152]{1,0:T(8,128)(2,1)}, u32[]{:S(2)}, u32[]{:S(2)}) collective-permute-start(bf16[256,1152]{1,0:T(8,128)(2,1)S(1)} %add_convert_fusion.3), channel_id=1, source_target_pairs={{0,1},{1,0},{2,3},{3,2},{4,5},{5,4},{6,7},{7,6},{8,9},{9,8},{10,11... | collective-permute-start | bytes 1769480 | tf_op jit(solution)/shard_map/ppermute | solution.py:51
  185.2 13.4 %collective-permute-start.3 = (bf16[256,1152]{1,0:T(8,128)(2,1)S(1)}, bf16[256,1152]{1,0:T(8,128)(2,1)S(1)}, u32[]{:S(2)}, u32[]{:S(2)}) collective-permute-start(bf16[256,1152]{1,0:T(8,128)(2,1)S(1)} %convolution_convert_fusion.9), channel_id=1, source_target_pairs={{0,1},{1,0},{2,3},{3,2},{4,5},{5,4},{6,7},{7,6},{8,9},{9,8},{10,11... | collective-permute-start | bytes 1769480 | tf_op jit(solution)/shard_map/ppermute | solution.py:51
  202.8 12.5 %collective-permute-start.4 = (bf16[256,1152]{1,0:T(8,128)(2,1)S(1)}, bf16[256,1152]{1,0:T(8,128)(2,1)S(1)}, u32[]{:S(2)}, u32[]{:S(2)}) collective-permute-start(bf16[256,1152]{1,0:T(8,128)(2,1)S(1)} %add_convert_fusion.2), channel_id=1, source_target_pairs={{0,1},{1,0},{2,3},{3,2},{4,5},{5,4},{6,7},{7,6},{8,9},{9,8},{10,11... | collective-permute-start | bytes 1769480 | tf_op jit(solution)/shard_map/ppermute | solution.py:51
  204.4 528.6 %all-gather.22.cloned.1.call-start = ((), (), s32[]{:S(2)}) async-start(), calls=%async_computation.12 | async-start | bytes 2585088 | tf_op jit(solution)/shard_map/all_gather | solution.py:861
  246.5 16.4 %collective-permute-start.5 = (bf16[256,1152]{1,0:T(8,128)(2,1)}, bf16[256,1152]{1,0:T(8,128)(2,1)S(1)}, u32[]{:S(2)}, u32[]{:S(2)}) collective-permute-start(bf16[256,1152]{1,0:T(8,128)(2,1)} %convolution_convert_fusion.13), channel_id=1, source_target_pairs={{0,1},{1,0},{2,3},{3,2},{4,5},{5,4},{6,7},{7,6},{8,9},{9,8},{10,11... | collective-permute-start | bytes 1769480 | tf_op jit(solution)/shard_map/ppermute | solution.py:51
  248.0 27.5 %collective-permute-start.8 = (bf16[256,1152]{1,0:T(8,128)(2,1)}, bf16[256,1152]{1,0:T(8,128)(2,1)S(1)}, u32[]{:S(2)}, u32[]{:S(2)}) collective-permute-start(bf16[256,1152]{1,0:T(8,128)(2,1)} %get-tuple-element.259), channel_id=1, source_target_pairs={{0,1},{1,0},{2,3},{3,2},{4,5},{5,4},{6,7},{7,6},{8,9},{9,8},{10,11... | collective-permute-start | bytes 1769480 | tf_op jit(solution)/shard_map/ppermute | solution.py:51
  266.3 21.2 %collective-permute-start.6 = (bf16[256,1152]{1,0:T(8,128)(2,1)S(1)}, bf16[256,1152]{1,0:T(8,128)(2,1)}, u32[]{:S(2)}, u32[]{:S(2)}) collective-permute-start(bf16[256,1152]{1,0:T(8,128)(2,1)S(1)} %add_convert_fusion.1), channel_id=1, source_target_pairs={{0,1},{1,0},{2,3},{3,2},{4,5},{5,4},{6,7},{7,6},{8,9},{9,8},{10,11... | collective-permute-start | bytes 1769480 | tf_op jit(solution)/shard_map/ppermute | solution.py:51
  369.8 40.2 %collective-permute-start.7 = (bf16[256,1152]{1,0:T(8,128)(2,1)}, bf16[256,1152]{1,0:T(8,128)(2,1)}, u32[]{:S(2)}, u32[]{:S(2)}) collective-permute-start(bf16[256,1152]{1,0:T(8,128)(2,1)} %convolution_convert_fusion.8), channel_id=1, source_target_pairs={{0,1},{1,0},{2,3},{3,2},{4,5},{5,4},{6,7},{7,6},{8,9},{9,8},{10,11... | collective-permute-start | bytes 1769480 | tf_op jit(solution)/shard_map/ppermute | solution.py:51
  384.8 15.3 %collective-permute-start.9 = (bf16[256,1152]{1,0:T(8,128)(2,1)S(1)}, bf16[256,1152]{1,0:T(8,128)(2,1)S(1)}, u32[]{:S(2)}, u32[]{:S(2)}) collective-permute-start(bf16[256,1152]{1,0:T(8,128)(2,1)S(1)} %convolution_convert_fusion.12), channel_id=1, source_target_pairs={{0,1},{1,0},{2,3},{3,2},{4,5},{5,4},{6,7},{7,6},{8,9},{9,8},{10,11... | collective-permute-start | bytes 1769480 | tf_op jit(solution)/shard_map/ppermute | solution.py:51
  403.2 14.4 %collective-permute-start.10 = (bf16[256,1152]{1,0:T(8,128)(2,1)S(1)}, bf16[256,1152]{1,0:T(8,128)(2,1)S(1)}, u32[]{:S(2)}, u32[]{:S(2)}) collective-permute-start(bf16[256,1152]{1,0:T(8,128)(2,1)S(1)} %get-tuple-element.157), channel_id=1, source_target_pairs={{0,1},{1,0},{2,3},{3,2},{4,5},{5,4},{6,7},{7,6},{8,9},{9,8},{10,11... | collective-permute-start | bytes 1769480 | tf_op jit(solution)/shard_map/ppermute | solution.py:51
  439.2 13.5 %collective-permute-start.11 = (bf16[256,1152]{1,0:T(8,128)(2,1)S(1)}, bf16[256,1152]{1,0:T(8,128)(2,1)S(1)}, u32[]{:S(2)}, u32[]{:S(2)}) collective-permute-start(bf16[256,1152]{1,0:T(8,128)(2,1)S(1)} %fusion.21), channel_id=1, source_target_pairs={{0,1},{1,0},{2,3},{3,2},{4,5},{5,4},{6,7},{7,6},{8,9},{9,8},{10,11... | collective-permute-start | bytes 1769480 | tf_op jit(solution)/shard_map/ppermute | solution.py:51
  457.3 12.6 %collective-permute-start.12 = (bf16[256,1152]{1,0:T(8,128)(2,1)S(1)}, bf16[256,1152]{1,0:T(8,128)(2,1)S(1)}, u32[]{:S(2)}, u32[]{:S(2)}) collective-permute-start(bf16[256,1152]{1,0:T(8,128)(2,1)S(1)} %get-tuple-element.154), channel_id=1, source_target_pairs={{0,1},{1,0},{2,3},{3,2},{4,5},{5,4},{6,7},{7,6},{8,9},{9,8},{10,11... | collective-permute-start | bytes 1769480 | tf_op jit(solution)/shard_map/ppermute | solution.py:51
  488.1 11.6 %collective-permute-start.13 = (bf16[256,1152]{1,0:T(8,128)(2,1)S(1)}, bf16[256,1152]{1,0:T(8,128)(2,1)S(1)}, u32[]{:S(2)}, u32[]{:S(2)}) collective-permute-start(bf16[256,1152]{1,0:T(8,128)(2,1)S(1)} %convolution_convert_fusion.11), channel_id=1, source_target_pairs={{0,1},{1,0},{2,3},{3,2},{4,5},{5,4},{6,7},{7,6},{8,9},{9,8},{10,11... | collective-permute-start | bytes 1769480 | tf_op jit(solution)/shard_map/ppermute | solution.py:51
  502.8 10.6 %collective-permute-start.14 = (bf16[256,1152]{1,0:T(8,128)(2,1)S(1)}, bf16[256,1152]{1,0:T(8,128)(2,1)S(1)}, u32[]{:S(2)}, u32[]{:S(2)}) collective-permute-start(bf16[256,1152]{1,0:T(8,128)(2,1)S(1)} %get-tuple-element.151), channel_id=1, source_target_pairs={{0,1},{1,0},{2,3},{3,2},{4,5},{5,4},{6,7},{7,6},{8,9},{9,8},{10,11... | collective-permute-start | bytes 1769480 | tf_op jit(solution)/shard_map/ppermute | solution.py:51
  533.3 9.9 %collective-permute-start.15 = (bf16[256,1152]{1,0:T(8,128)(2,1)S(1)}, bf16[256,1152]{1,0:T(8,128)(2,1)S(1)}, u32[]{:S(2)}, u32[]{:S(2)}) collective-permute-start(bf16[256,1152]{1,0:T(8,128)(2,1)S(1)} %convolution_convert_fusion.10), channel_id=1, source_target_pairs={{0,1},{1,0},{2,3},{3,2},{4,5},{5,4},{6,7},{7,6},{8,9},{9,8},{10,11... | collective-permute-start | bytes 1769480 | tf_op jit(solution)/shard_map/ppermute | solution.py:51
  553.3 4.8 collective-permute-start.16
  559.1 206.3 %reduce-scatter.5.cloned.1.call-start = ((), (), s32[]{:S(2)}) async-start(), calls=%async_computation.10 | async-start | bytes 7520256 | tf_op jit(solution)/shard_map/reduce_scatter | solution.py:666
  559.9 277.9 %reduce-scatter.3.cloned.1.call-start = ((), (), s32[]{:S(2)}) async-start(), calls=%async_computation.9 | async-start | bytes 7520256 | tf_op jit(solution)/shard_map/reduce_scatter | solution.py:666
  561.3 181.9 %all-to-all-start.1 = ((bf16[16,4,72]{2,1,0:T(4,128)(2,1)}), bf16[16,4,72]{2,1,0:T(4,128)(2,1)S(1)}, u32[]{:S(2)}, u32[]{:S(2)}) async-start(bf16[16,4,72]{2,1,0:T(4,128)(2,1)} %bitcast.266), calls=%async_computation.1 | async-start | bytes 32768 | tf_op jit(solution)/shard_map/all_to_all | solution.py:801
  743.2 17.7 %all-to-all-start = ((bf16[16,4,72]{2,1,0:T(4,128)(2,1)}), bf16[16,4,72]{2,1,0:T(4,128)(2,1)S(1)}, u32[]{:S(2)}, u32[]{:S(2)}) async-start(bf16[16,4,72]{2,1,0:T(4,128)(2,1)} %bitcast.97), calls=%async_computation | async-start | bytes 32768 | tf_op jit(solution)/shard_map/all_to_all | solution.py:873
  761.0 3.7 collective-permute-start.17
  (267 other events, 2300.4 us)
Sparse Core Ops, SparseCore 0:
  10.9 92.3 all-gather.9
  106.1 45.1 all-gather.11
  154.2 49.2 all-gather.19
  205.5 37.9 all-gather.13
  246.2 65.4 all-gather.15
  314.3 45.6 all-gather.17
  559.2 56.3 all-gather.21
  619.6 125.5 reduce-scatter.4
  749.7 88.0 reduce-scatter.2

commit v3 on v2

--- a/solution.py
+++ b/solution.py
@@ -447,46 +447,69 @@
 
 
 def scatter_kernel(row_size, head_size, count, *refs):
-    ins, outs = refs[:count], refs[count : 2 * count]
-    scratch = refs[2 * count : 6 * count]
-    send, recv, load = refs[6 * count :]
+    ins, small = refs[:count], refs[count]
+    outs, smalls = refs[count + 1 : 2 * count + 1], refs[2 * count + 1]
+    refs = refs[2 * count + 2 :]
+    scratch = refs[: 4 * count]
+    send, recv, load, small_send, small_recv, small_keep = refs[4 * count :]
     place = Place(row_size, head_size)
     place.greet(False)
-    scatter_all(
-        [
-            Scatter(
-                place, ins[i], outs[i], *scratch[4 * i : 4 * i + 4], send.at[i], recv.at[i], load.at[i]
-            )
-            for i in range(count)
-        ]
-    )
-
-
-def scatter_call(row_size, head_size, grads):
+    lead = Gather(place, small, smalls, small_send, small_recv, small_keep.at[0])
+    lead.begin()
+    items = [
+        Scatter(
+            place, ins[i], outs[i], *scratch[4 * i : 4 * i + 4], send.at[i], recv.at[i], load.at[i]
+        )
+        for i in range(count)
+    ]
+    for item in items:
+        item.begin()
+    for k in range(1, place.sizes[0]):
+        lead.first(k)
+    for step in range(count + 2):
+        if step < count:
+            items[step].first()
+        if step == 0:
+            lead.second()
+        if 1 <= step <= count:
+            items[step - 1].second()
+        if step >= 2:
+            items[step - 2].finish()
+    lead.finish()
+
+
+def scatter_call(row_size, head_size, grads, small):
     count = len(grads)
     copies = scatter_count(row_size)
+    small_copies = gather_count(row_size)
     a, b = 4, row_size // 8
     scratch = []
     for grad in grads:
         chunk = grad.shape[1:]
         for lead in ((a, b), (a, b), (b - 1, a), (a - 1,)):
             scratch.append(pltpu.VMEM(lead + chunk, grad.dtype))
+    anywhere = pl.BlockSpec(memory_space=pl.ANY)
+    vmem = pl.BlockSpec(memory_space=pltpu.VMEM)
     return pl.pallas_call(
         functools.partial(scatter_kernel, row_size, head_size, count),
-        out_shape=[jax.ShapeDtypeStruct(grad.shape[1:], jnp.float32) for grad in grads],
-        in_specs=[pl.BlockSpec(memory_space=pl.ANY)] * count,
-        out_specs=[pl.BlockSpec(memory_space=pltpu.VMEM)] * count,
+        out_shape=[jax.ShapeDtypeStruct(grad.shape[1:], jnp.float32) for grad in grads]
+        + [jax.ShapeDtypeStruct((row_size,) + small.shape, small.dtype)],
+        in_specs=[anywhere] * (count + 1),
+        out_specs=[vmem] * count + [anywhere],
         scratch_shapes=scratch
         + [
             pltpu.SemaphoreType.DMA((count, copies)),
             pltpu.SemaphoreType.DMA((count, copies)),
             pltpu.SemaphoreType.DMA((count, a * b)),
+            pltpu.SemaphoreType.DMA((small_copies,)),
+            pltpu.SemaphoreType.DMA((small_copies,)),
+            pltpu.SemaphoreType.DMA((1,)),
         ],
         compiler_params=pltpu.CompilerParams(
             collective_id=2, has_side_effects=True, vmem_limit_bytes=56 * 2**20
         ),
         name="sum_rows",
-    )(*grads)
+    )(*grads, small)
 
 
 def rope_parts(coords):
@@ -779,24 +802,27 @@
     cond_act = jax.nn.silu(cond_wide).astype(jnp.bfloat16)
     pad = -image_count % 16
     bias_rows = jnp.repeat(ada_bias.astype(jnp.float32), image_count, axis=0)
-    first_qkv, first_proj, mods = start_call(
+    *first, mods = start_call(
         row_size,
         head_size,
         jnp.pad(cond_act, ((0, pad), (0, 0))),
         ada_weight,
         bias_rows,
-        [qkv_weight[0], proj_weight[0].T],
+        [qkv_weight[0], proj_weight[0].T, gu_weight[0].reshape(shard_rows, -1), down_weight[0].T],
     )
     qkv_full, gu_full, down_t, proj_t = [], [], [], []
     for b in range(block_count):
         if b == 0:
-            qkv_full.append(first_qkv.reshape(-1, first_qkv.shape[-1]))
-            proj_t.append(first_proj.reshape(-1, first_proj.shape[-1]))
+            block = [item.reshape(-1, item.shape[-1]) for item in first]
         else:
-            qkv_full.append(gathered(qkv_weight[b]))
-            proj_t.append(gathered(proj_weight[b].T))
-        gu_full.append(gathered(gu_weight[b].reshape(shard_rows, -1)))
-        down_t.append(gathered(down_weight[b].T))
+            block = [
+                gathered(qkv_weight[b]),
+                gathered(proj_weight[b].T),
+                gathered(gu_weight[b].reshape(shard_rows, -1)),
+                gathered(down_weight[b].T),
+            ]
+        for held, item in zip((qkv_full, proj_t, gu_full, down_t), block):
+            held.append(item)
     mod_all = mods.reshape(head_size, block_count, image_count, -1)
     cond_mine = lax.all_to_all(
         cond_act.reshape(image_count, row_size, -1).transpose(1, 0, 2), "rows", 0, 0
@@ -858,7 +884,16 @@
         ],
         axis=1,
     )
-    small = lax.all_gather(small, "rows", axis=0, tiled=True)
+    small_size = small.size
+    small = jnp.pad(small, ((0, 0), (0, -small_size % 2048))).reshape(16, -1)
+    parts = []
+    for b in reversed(range(block_count)):
+        parts += [block_grads[b][4], block_grads[b][2], block_grads[b][0]]
+    *sums, small = scatter_call(
+        row_size, head_size, [part.reshape(row_size, shard_rows, -1) for part in parts], small
+    )
+    sums = [sums[3 * b : 3 * b + 3] for b in reversed(range(block_count))]
+    small = small.reshape(row_size, -1)[:, :small_size]
     split = image_grads.size
     all_grads = small[:, :split].reshape((row_size,) + image_grads.shape)
     bias_all = small[:, split:].reshape((row_size, 3) + bias_sums.shape).astype(jnp.float32)
@@ -879,13 +914,6 @@
         cond_total = cond_total + head_move(cond_rows.astype(jnp.bfloat16), flip).astype(jnp.float32)
     logistic = jax.nn.sigmoid(cond_wide)
     cond_grad = cond_total * logistic * (1.0 + cond_wide * (1.0 - logistic))
-    parts = []
-    for b in reversed(range(block_count)):
-        parts += [block_grads[b][4], block_grads[b][2], block_grads[b][0]]
-    sums = scatter_call(
-        row_size, head_size, [part.reshape(row_size, shard_rows, -1) for part in parts]
-    )
-    sums = [sums[3 * b : 3 * b + 3] for b in reversed(range(block_count))]
     return (
         block_out,
         incoming,

time: 853 us -> 735 us (0.86)
  waiting for transfers between devices: 277 us -> 90.4 us
  Pallas kernels: 235 us -> 283 us
  matrix products: 154 us -> 169 us
    all_gather x6 -> x4, waiting for transfers between devices: 75 us -> 0.03 us  [gathered(): return lax.all_gather(shard, 'rows', axis=0, tiled=True)]
    reduce_scatter x2, waiting for transfers between devices: 71 us -> 0.02 us  [block_backward(): lax.psum_scatter(gu_grad, 'rows', scatter_dimension=0, tiled=True)]
    pallas_call x1, Pallas kernels: 88.9 us -> 150 us  [start_call(): pl.pallas_call(functools.partial(start_kernel, row_size, head_size, image...]
    ppermute x18, waiting for transfers between devices: 125 us -> 90.1 us  [head_move(): lax.ppermute(value, 'heads', [(index, index ^ flip) for index in range(si...]
    pallas_call x1, Pallas kernels: 147 us -> 133 us  [scatter_call(): pl.pallas_call(functools.partial(scatter_kernel, row_size, head_size, cou...]
    unnamed x546 -> x528, local copies, waits for them, and re-layouts: 25.1 us -> 31.6 us
  transfers between devices with their start and end apart: 29 -> 26, of which waited for: 22 -> 12; matrix products, arithmetic and copies ran while one was open for 21% -> 37% of each run, Pallas kernels for 28% -> 39%
where the time goes in v3:
time: 735 us; the launch traced here: 730 us
  Pallas kernels  283 us (39%)
  matrix products  169 us (23%)
  waiting for transfers between devices  90.4 us (12%)
  local copies, waits for them, and re-layouts  73.3 us (10%)
  other arithmetic  59.6 us (8%)
  starting transfers between devices  35.7 us (5%)
  between operations  18 us (2%)
    pallas_call x1, Pallas kernels, start_call(): pl.pallas_call(functools.partial(start_kernel, row_size, head_size, image...  150 us
    pallas_call x1, Pallas kernels, scatter_call(): pl.pallas_call(functools.partial(scatter_kernel, row_size, head_size, cou...  133 us
    ppermute x18, waiting for transfers between devices, head_move(): lax.ppermute(value, 'heads', [(index, index ^ flip) for index in range(si...  90.1 us
    dot_general x18, matrix products, tail_dot(): lax.dot_general(operand, other, (((1,), (1,)), ((), ())), preferred_eleme...  44.4 us
    dot_general x10, matrix products, lead_dot(): lax.dot_general(operand, other, (((0,), (0,)), ((), ())), preferred_eleme...  42.7 us
    dot_general x8, matrix products, plain_dot(): return jnp.dot(operand, other, preferred_element_type=jnp.float32)  40.7 us
    unnamed x528, local copies, waits for them, and re-layouts  31.6 us
    ppermute x18, starting transfers between devices, head_move(): lax.ppermute(value, 'heads', [(index, index ^ flip) for index in range(si...  20.1 us
  transfers between devices with their start and end apart: 26, of which 12 were waited for; matrix products, arithmetic and copies ran while one was open for 37% of the time, Pallas kernels for 39%

profile of v3, /device:TPU:0, one launch (start us, length us, event | category | flops | bytes accessed | tf_op | source)
XLA Modules:
  0.0 729.7 jit_solution(232054958006653222)
XLA Ops:
  14.4 150.0 %start.1 = (bf16[16,72,1728]{2,1,0:T(8,128)(2,1)}, bf16[16,72,576]{2,1,0:T(8,128)(2,1)S(1)}, bf16[16,72,3072]{2,1,0:T(8,128)(2,1)}, bf16[16,72,1536]{2,1,0:T(8,128)(2,1)}, f32[2,8,3456]{2,1,0:T(8,128)S(1)}) custom-call(bf16[16,1152]{1,0:T(8,128)(2,1)S(1)} %pad.8.refs_0_, bf16[2,72,3456]{2,1,0:T(8,128)(2,1)S(1)} %copy-done.2, ...), custom_call_target="tpu_custom_call" | custom-call | tf_op jit(solution)/shard_map/start/pallas_call | solution.py:418
  172.8 11.4 %collective-permute-done = bf16[256,1152]{1,0:T(8,128)(2,1)} collective-permute-done((bf16[256,1152]{1,0:T(8,128)(2,1)S(1)}, bf16[256,1152]{1,0:T(8,128)(2,1)}, u32[]{:S(2)}, u32[]{:S(2)}) %collective-permute-start) | collective-permute-done | bytes 589856 | tf_op jit(solution)/shard_map/ppermute | solution.py:51
  184.2 4.9 convolution_add_fusion
  202.2 12.7 %collective-permute-done.1 = bf16[256,1152]{1,0:T(8,128)(2,1)S(1)} collective-permute-done((bf16[256,1152]{1,0:T(8,128)(2,1)S(1)}, bf16[256,1152]{1,0:T(8,128)(2,1)S(1)}, u32[]{:S(2)}, u32[]{:S(2)}) %collective-permute-start.1) | collective-permute-done | bytes 589856 | tf_op jit(solution)/shard_map/ppermute | solution.py:51
  218.9 12.8 %collective-permute-done.2 = bf16[256,1152]{1,0:T(8,128)(2,1)S(1)} collective-permute-done((bf16[256,1152]{1,0:T(8,128)(2,1)S(1)}, bf16[256,1152]{1,0:T(8,128)(2,1)S(1)}, u32[]{:S(2)}, u32[]{:S(2)}) %collective-permute-start.2) | collective-permute-done | bytes 589856 | tf_op jit(solution)/shard_map/ppermute | solution.py:51
  231.8 4.3 fusion.76
  245.8 9.2 %collective-permute-done.3 = bf16[256,1152]{1,0:T(8,128)(2,1)S(1)} collective-permute-done((bf16[256,1152]{1,0:T(8,128)(2,1)S(1)}, bf16[256,1152]{1,0:T(8,128)(2,1)S(1)}, u32[]{:S(2)}, u32[]{:S(2)}) %collective-permute-start.3) | collective-permute-done | bytes 589856 | tf_op jit(solution)/shard_map/ppermute | solution.py:51
  260.6 11.1 %collective-permute-done.4 = bf16[256,1152]{1,0:T(8,128)(2,1)} collective-permute-done((bf16[256,1152]{1,0:T(8,128)(2,1)S(1)}, bf16[256,1152]{1,0:T(8,128)(2,1)}, u32[]{:S(2)}, u32[]{:S(2)}) %collective-permute-start.4) | collective-permute-done | bytes 589856 | tf_op jit(solution)/shard_map/ppermute | solution.py:51
  271.7 4.9 fusion.18
  310.1 5.1 collective-permute-done.8
  316.0 10.2 %collective-permute-done.6 = bf16[256,1152]{1,0:T(8,128)(2,1)} collective-permute-done((bf16[256,1152]{1,0:T(8,128)(2,1)S(1)}, bf16[256,1152]{1,0:T(8,128)(2,1)}, u32[]{:S(2)}, u32[]{:S(2)}) %collective-permute-start.6) | collective-permute-done | bytes 589856 | tf_op jit(solution)/shard_map/ppermute | solution.py:51
  326.2 10.3 %fusion.75 = f32[512,3072]{1,0:T(8,128)} fusion(bf16[1152,3072]{1,0:T(8,128)(2,1)} %all-gather.8.cloned.1.call-done, bf16[256,1152]{1,0:T(8,128)(2,1)} %collective-permute-done.6, bf16[256,1152]{1,0:T(8,128)(2,1)} %copy-done.89), kind=kOutput, calls=%fused_computation.193 | convolution fusion | flops 3626237952 | bytes 14548992 | tf_op jit(solution)/shard_map/dot_general | solution.py:596
  336.5 7.5 %multiply_convert_fusion.4 = (bf16[512,1536]{1,0:T(8,128)(2,1)S(1)}, bf16[512,1536]{1,0:T(8,128)(2,1)S(1)}, bf16[512,1536]{1,0:T(8,128)(2,1)S(1)}) fusion(f32[512,3072]{1,0:T(8,128)} %fusion.75, bf16[1152,1536]{1,0:T(8,128)(2,1)} %all-gather.10.cloned.1.call-done, bf16[256,1152]{1,0:T(8,128)(2,1)} %copy-done.239, bf16[256,1152]{1,0:T(8,128)(2,1)} %get-tuple-element.265), kind=kOutput, calls=%fused_computation.54 | convolution fusion | flops 1826881536 | bytes 15728640 | tf_op jit(solution)/shard_map/dot_general | solution.py:596
  347.5 7.4 %convolution_convert_fusion.1 = bf16[1152,3072]{1,0:T(8,128)(2,1)} fusion(bf16[512,1536]{1,0:T(8,128)(2,1)S(1)} %get-tuple-element.174, bf16[512,1536]{1,0:T(8,128)(2,1)S(1)} %get-tuple-element.175, bf16[256,1152]{1,0:T(8,128)(2,1)} %collective-permute-done.6, bf16[256,1152]{1,0:T(8,128)(2,1)S(1)} %copy-done.90), kind=kOutput, calls=%fused_computation.1 | convolution fusion | flops 3636068352 | bytes 11403264 | tf_op jit(solution)/shard_map/dot_general | solution.py:33
  354.9 5.8 convolution_convert_fusion.12
  361.9 5.2 fusion.30
  367.2 6.9 collective-permute-done.9
  384.8 5.3 collective-permute-done.10
  392.8 5.7 fusion.40
  398.5 5.8 multiply_reduce_fusion.1
  427.6 5.5 convolution_convert_fusion.3
  456.7 6.1 convolution_convert_fusion
  462.8 5.8 fusion.25
  473.8 5.5 convolution_bitcast_fusion
  480.9 6.6 copy.114
  487.6 5.3 convolution_convert_fusion.4
  496.4 4.9 fusion.43
  501.4 5.7 multiply_reduce_fusion
  520.3 5.5 convolution_convert_fusion.2
  544.9 6.5 copy.116
  552.7 133.2 %sum_rows.1 = (f32[72,1536]{1,0:T(8,128)}, f32[72,576]{1,0:T(8,128)}, f32[72,1728]{1,0:T(8,128)}, f32[72,1536]{1,0:T(8,128)}, f32[72,576]{1,0:T(8,128)}, /*index...) custom-call(bf16[16,72,1536]{2,1,0:T(8,128)(2,1)} %bitcast.307, bf16[16,72,576]{2,1,0:T(8,128)(2,1)} %bitcast.283, ...), custom_call_target="tpu_custom_call" | custom-call | tf_op jit(solution)/shard_map/sum_rows/pallas_call | solution.py:493
  695.7 10.8 %all-to-all-start = ((bf16[16,4,72]{2,1,0:T(4,128)(2,1)}), bf16[16,4,72]{2,1,0:T(4,128)(2,1)S(1)}, u32[]{:S(2)}, u32[]{:S(2)}) async-start(bf16[16,4,72]{2,1,0:T(4,128)(2,1)} %bitcast.104), calls=%async_computation | async-start | bytes 32768 | tf_op jit(solution)/shard_map/all_to_all | solution.py:908
  (760 shorter events, 213.8 us)
Async XLA Ops:
  7.2 264.5 %all-gather.12.cloned.1.call-start = ((), (), s32[]{:S(2)}) async-start(), calls=%async_computation.9 | async-start | bytes 4386816 | tf_op jit(solution)/shard_map/all_gather | solution.py:799
  9.1 277.4 %all-gather.6.cloned.1.call-start = ((), (), s32[]{:S(2)}) async-start(), calls=%async_computation.4 | async-start | bytes 1566720 | tf_op jit(solution)/shard_map/all_gather | solution.py:799
  9.9 316.3 %all-gather.8.cloned.1.call-start = ((), (), s32[]{:S(2)}) async-start(), calls=%async_computation.5 | async-start | bytes 7520256 | tf_op jit(solution)/shard_map/all_gather | solution.py:799
  12.6 323.9 %all-gather.10.cloned.1.call-start = ((), (), s32[]{:S(2)}) async-start(), calls=%async_computation.6 | async-start | bytes 3760128 | tf_op jit(solution)/shard_map/all_gather | solution.py:799
  12.8 152.6 %copy-start.214 = (f32[256]{0:T(256)}, f32[256]{0:T(256)S(1)}, u32[]{:S(2)}) copy-start(f32[256]{0:T(256)S(1)} %broadcast_multiply_fusion.13) | copy-start | bytes 3076
  13.2 158.2 %copy-start.216 = (s32[1,256]{1,0:T(1,128)}, s32[1,256]{1,0:T(1,128)S(1)}, u32[]{:S(2)}) copy-start(s32[1,256]{1,0:T(1,128)S(1)} %get-tuple-element.270) | copy-start | bytes 3076
  13.3 244.3 %copy-start.111 = (pred[256]{0:T(512)(128)(4,1)}, pred[256]{0:T(512)(128)(4,1)S(1)}, u32[]{:S(2)}) copy-start(pred[256]{0:T(512)(128)(4,1)S(1)} %get-tuple-element.273) | copy-start | bytes 772
  13.3 244.3 %copy-start.116 = (pred[256]{0:T(512)(128)(4,1)}, pred[256]{0:T(512)(128)(4,1)S(1)}, u32[]{:S(2)}) copy-start(pred[256]{0:T(512)(128)(4,1)S(1)} %get-tuple-element.274) | copy-start | bytes 772
  13.3 244.3 %copy-start.121 = (pred[256]{0:T(512)(128)(4,1)}, pred[256]{0:T(512)(128)(4,1)S(1)}, u32[]{:S(2)}) copy-start(pred[256]{0:T(512)(128)(4,1)S(1)} %get-tuple-element.275) | copy-start | bytes 772
  168.5 15.8 %collective-permute-start = (bf16[256,1152]{1,0:T(8,128)(2,1)S(1)}, bf16[256,1152]{1,0:T(8,128)(2,1)}, u32[]{:S(2)}, u32[]{:S(2)}) collective-permute-start(bf16[256,1152]{1,0:T(8,128)(2,1)S(1)} %fusion.53), channel_id=1, source_target_pairs={{0,1},{1,0},{2,3},{3,2},{4,5},{5,4},{6,7},{7,6},{8,9},{9,8},{10,11... | collective-permute-start | bytes 1769480 | tf_op jit(solution)/shard_map/ppermute | solution.py:51
  200.0 14.9 %collective-permute-start.1 = (bf16[256,1152]{1,0:T(8,128)(2,1)S(1)}, bf16[256,1152]{1,0:T(8,128)(2,1)S(1)}, u32[]{:S(2)}, u32[]{:S(2)}) collective-permute-start(bf16[256,1152]{1,0:T(8,128)(2,1)S(1)} %convolution_convert_fusion.14), channel_id=1, source_target_pairs={{0,1},{1,0},{2,3},{3,2},{4,5},{5,4},{6,7},{7,6},{8,9},{9,8},{10,11... | collective-permute-start | bytes 1769480 | tf_op jit(solution)/shard_map/ppermute | solution.py:51
  215.7 254.0 %copy-start.5 = (f32[256,1152]{1,0:T(8,128)}, f32[256,1152]{1,0:T(8,128)S(1)}, u32[]{:S(2)}) copy-start(f32[256,1152]{1,0:T(8,128)S(1)} %get-tuple-element.171) | copy-start | bytes 3538948
  217.7 14.0 %collective-permute-start.2 = (bf16[256,1152]{1,0:T(8,128)(2,1)S(1)}, bf16[256,1152]{1,0:T(8,128)(2,1)S(1)}, u32[]{:S(2)}, u32[]{:S(2)}) collective-permute-start(bf16[256,1152]{1,0:T(8,128)(2,1)S(1)} %add_convert_fusion.3), channel_id=1, source_target_pairs={{0,1},{1,0},{2,3},{3,2},{4,5},{5,4},{6,7},{7,6},{8,9},{9,8},{10,11... | collective-permute-start | bytes 1769480 | tf_op jit(solution)/shard_map/ppermute | solution.py:51
  241.9 13.1 %collective-permute-start.3 = (bf16[256,1152]{1,0:T(8,128)(2,1)S(1)}, bf16[256,1152]{1,0:T(8,128)(2,1)S(1)}, u32[]{:S(2)}, u32[]{:S(2)}) collective-permute-start(bf16[256,1152]{1,0:T(8,128)(2,1)S(1)} %convolution_convert_fusion.9), channel_id=1, source_target_pairs={{0,1},{1,0},{2,3},{3,2},{4,5},{5,4},{6,7},{7,6},{8,9},{9,8},{10,11... | collective-permute-start | bytes 1769480 | tf_op jit(solution)/shard_map/ppermute | solution.py:51
  259.4 12.3 %collective-permute-start.4 = (bf16[256,1152]{1,0:T(8,128)(2,1)S(1)}, bf16[256,1152]{1,0:T(8,128)(2,1)}, u32[]{:S(2)}, u32[]{:S(2)}) collective-permute-start(bf16[256,1152]{1,0:T(8,128)(2,1)S(1)} %add_convert_fusion.2), channel_id=1, source_target_pairs={{0,1},{1,0},{2,3},{3,2},{4,5},{5,4},{6,7},{7,6},{8,9},{9,8},{10,11... | collective-permute-start | bytes 1769480 | tf_op jit(solution)/shard_map/ppermute | solution.py:51
  289.4 13.2 %collective-permute-start.5 = (bf16[256,1152]{1,0:T(8,128)(2,1)}, bf16[256,1152]{1,0:T(8,128)(2,1)S(1)}, u32[]{:S(2)}, u32[]{:S(2)}) collective-permute-start(bf16[256,1152]{1,0:T(8,128)(2,1)} %convolution_convert_fusion.13), channel_id=1, source_target_pairs={{0,1},{1,0},{2,3},{3,2},{4,5},{5,4},{6,7},{7,6},{8,9},{9,8},{10,11... | collective-permute-start | bytes 1769480 | tf_op jit(solution)/shard_map/ppermute | solution.py:51
  291.2 404.6 %all-to-all-start.1 = ((bf16[16,4,72]{2,1,0:T(4,128)(2,1)}), bf16[16,4,72]{2,1,0:T(4,128)(2,1)}, u32[]{:S(2)}, u32[]{:S(2)}) async-start(bf16[16,4,72]{2,1,0:T(4,128)(2,1)} %bitcast.265), calls=%async_computation.1 | async-start | bytes 32768 | tf_op jit(solution)/shard_map/all_to_all | solution.py:827
  295.3 422.3 %reduce-scatter.5.cloned.1.call-start = ((), (), s32[]{:S(2)}) async-start(), calls=%async_computation.8 | async-start | bytes 7520256 | tf_op jit(solution)/shard_map/reduce_scatter | solution.py:689
  295.8 19.3 %collective-permute-start.8 = (bf16[256,1152]{1,0:T(8,128)(2,1)}, bf16[256,1152]{1,0:T(8,128)(2,1)S(1)}, u32[]{:S(2)}, u32[]{:S(2)}) collective-permute-start(bf16[256,1152]{1,0:T(8,128)(2,1)} %get-tuple-element.265), channel_id=1, source_target_pairs={{0,1},{1,0},{2,3},{3,2},{4,5},{5,4},{6,7},{7,6},{8,9},{9,8},{10,11... | collective-permute-start | bytes 1769480 | tf_op jit(solution)/shard_map/ppermute | solution.py:51
  307.6 18.5 %collective-permute-start.6 = (bf16[256,1152]{1,0:T(8,128)(2,1)S(1)}, bf16[256,1152]{1,0:T(8,128)(2,1)}, u32[]{:S(2)}, u32[]{:S(2)}) collective-permute-start(bf16[256,1152]{1,0:T(8,128)(2,1)S(1)} %add_convert_fusion.1), channel_id=1, source_target_pairs={{0,1},{1,0},{2,3},{3,2},{4,5},{5,4},{6,7},{7,6},{8,9},{9,8},{10,11... | collective-permute-start | bytes 1769480 | tf_op jit(solution)/shard_map/ppermute | solution.py:51
  346.4 38.3 %collective-permute-start.7 = (bf16[256,1152]{1,0:T(8,128)(2,1)}, bf16[256,1152]{1,0:T(8,128)(2,1)}, u32[]{:S(2)}, u32[]{:S(2)}) collective-permute-start(bf16[256,1152]{1,0:T(8,128)(2,1)} %convolution_convert_fusion.8), channel_id=1, source_target_pairs={{0,1},{1,0},{2,3},{3,2},{4,5},{5,4},{6,7},{7,6},{8,9},{9,8},{10,11... | collective-permute-start | bytes 1769480 | tf_op jit(solution)/shard_map/ppermute | solution.py:51
  360.8 13.3 %collective-permute-start.9 = (bf16[256,1152]{1,0:T(8,128)(2,1)S(1)}, bf16[256,1152]{1,0:T(8,128)(2,1)S(1)}, u32[]{:S(2)}, u32[]{:S(2)}) collective-permute-start(bf16[256,1152]{1,0:T(8,128)(2,1)S(1)} %convolution_convert_fusion.12), channel_id=1, source_target_pairs={{0,1},{1,0},{2,3},{3,2},{4,5},{5,4},{6,7},{7,6},{8,9},{9,8},{10,11... | collective-permute-start | bytes 1769480 | tf_op jit(solution)/shard_map/ppermute | solution.py:51
  377.5 12.6 %collective-permute-start.10 = (bf16[256,1152]{1,0:T(8,128)(2,1)}, bf16[256,1152]{1,0:T(8,128)(2,1)}, u32[]{:S(2)}, u32[]{:S(2)}) collective-permute-start(bf16[256,1152]{1,0:T(8,128)(2,1)} %get-tuple-element.163), channel_id=1, source_target_pairs={{0,1},{1,0},{2,3},{3,2},{4,5},{5,4},{6,7},{7,6},{8,9},{9,8},{10,11... | collective-permute-start | bytes 1769480 | tf_op jit(solution)/shard_map/ppermute | solution.py:51
  384.8 334.2 %reduce-scatter.3.cloned.1.call-start = ((), (), s32[]{:S(2)}) async-start(), calls=%async_computation.7 | async-start | bytes 7520256 | tf_op jit(solution)/shard_map/reduce_scatter | solution.py:689
  421.2 12.0 %collective-permute-start.11 = (bf16[256,1152]{1,0:T(8,128)(2,1)S(1)}, bf16[256,1152]{1,0:T(8,128)(2,1)S(1)}, u32[]{:S(2)}, u32[]{:S(2)}) collective-permute-start(bf16[256,1152]{1,0:T(8,128)(2,1)S(1)} %fusion.21), channel_id=1, source_target_pairs={{0,1},{1,0},{2,3},{3,2},{4,5},{5,4},{6,7},{7,6},{8,9},{9,8},{10,11... | collective-permute-start | bytes 1769480 | tf_op jit(solution)/shard_map/ppermute | solution.py:51
  438.3 10.6 %collective-permute-start.12 = (bf16[256,1152]{1,0:T(8,128)(2,1)S(1)}, bf16[256,1152]{1,0:T(8,128)(2,1)S(1)}, u32[]{:S(2)}, u32[]{:S(2)}) collective-permute-start(bf16[256,1152]{1,0:T(8,128)(2,1)S(1)} %get-tuple-element.160), channel_id=1, source_target_pairs={{0,1},{1,0},{2,3},{3,2},{4,5},{5,4},{6,7},{7,6},{8,9},{9,8},{10,11... | collective-permute-start | bytes 1769480 | tf_op jit(solution)/shard_map/ppermute | solution.py:51
  455.8 12.9 %collective-permute-start.13 = (bf16[256,1152]{1,0:T(8,128)(2,1)}, bf16[256,1152]{1,0:T(8,128)(2,1)S(1)}, u32[]{:S(2)}, u32[]{:S(2)}) collective-permute-start(bf16[256,1152]{1,0:T(8,128)(2,1)} %convolution_convert_fusion.11), channel_id=1, source_target_pairs={{0,1},{1,0},{2,3},{3,2},{4,5},{5,4},{6,7},{7,6},{8,9},{9,8},{10,11... | collective-permute-start | bytes 1769480 | tf_op jit(solution)/shard_map/ppermute | solution.py:51
  472.8 20.1 %collective-permute-start.14 = (bf16[256,1152]{1,0:T(8,128)(2,1)}, bf16[256,1152]{1,0:T(8,128)(2,1)}, u32[]{:S(2)}, u32[]{:S(2)}) collective-permute-start(bf16[256,1152]{1,0:T(8,128)(2,1)} %get-tuple-element.157), channel_id=1, source_target_pairs={{0,1},{1,0},{2,3},{3,2},{4,5},{5,4},{6,7},{7,6},{8,9},{9,8},{10,11... | collective-permute-start | bytes 1769480 | tf_op jit(solution)/shard_map/ppermute | solution.py:51
  519.2 11.7 %collective-permute-start.15 = (bf16[256,1152]{1,0:T(8,128)(2,1)}, bf16[256,1152]{1,0:T(8,128)(2,1)}, u32[]{:S(2)}, u32[]{:S(2)}) collective-permute-start(bf16[256,1152]{1,0:T(8,128)(2,1)} %convolution_convert_fusion.10), channel_id=1, source_target_pairs={{0,1},{1,0},{2,3},{3,2},{4,5},{5,4},{6,7},{7,6},{8,9},{9,8},{10,11... | collective-permute-start | bytes 1769480 | tf_op jit(solution)/shard_map/ppermute | solution.py:51
  541.9 9.5 %collective-permute-start.16 = (f32[2,4,3456]{2,1,0:T(4,128)S(1)}, f32[2,4,3456]{2,1,0:T(4,128)S(1)}, u32[]{:S(2)}, u32[]{:S(2)}) collective-permute-start(f32[2,4,3456]{2,1,0:T(4,128)S(1)} %fusion.111), channel_id=1, source_target_pairs={{0,1},{1,0},{2,3},{3,2},{4,5},{5,4},{6,7},{7,6},{8,9},{9,8},{10,11... | collective-permute-start | bytes 331784 | tf_op jit(solution)/shard_map/ppermute | solution.py:51
  695.7 17.2 %all-to-all-start = ((bf16[16,4,72]{2,1,0:T(4,128)(2,1)}), bf16[16,4,72]{2,1,0:T(4,128)(2,1)S(1)}, u32[]{:S(2)}, u32[]{:S(2)}) async-start(bf16[16,4,72]{2,1,0:T(4,128)(2,1)} %bitcast.104), calls=%async_computation | async-start | bytes 32768 | tf_op jit(solution)/shard_map/all_to_all | solution.py:908
  713.1 3.9 collective-permute-start.17
  (255 other events, 1904.2 us)
Sparse Core Ops, SparseCore 0:
  10.9 69.4 all-gather.11
  83.1 43.4 all-gather.5
  129.5 68.2 all-gather.7
  260.7 44.7 all-gather.9
  384.9 89.8 reduce-scatter.4
  493.0 108.0 reduce-scatter.2

commit v4 on v2

--- a/solution.py
+++ b/solution.py
@@ -341,8 +341,8 @@
     cond, ada, bias = refs[:3]
     shards = refs[3 : 3 + weights]
     outs = refs[3 + weights : 3 + 2 * weights]
-    mods = refs[3 + 2 * weights]
-    (conds, part, held, met, side, far, total, every, sends, recvs, keeps, mod_send, mod_recv, mod_load, head_send, head_recv) = refs[4 + 2 * weights :]
+    mods, mine_out = refs[3 + 2 * weights : 5 + 2 * weights]
+    (conds, part, held, met, side, far, total, every, sends, recvs, keeps, mod_send, mod_recv, mod_load, head_send, head_recv) = refs[5 + 2 * weights :]
     place = Place(row_size, head_size)
     place.greet(True)
     items = [
@@ -366,6 +366,7 @@
     mine = jnp.dot(
         conds[...].reshape(row_size * pad, width), pick, preferred_element_type=jnp.float32
     ).astype(jnp.bfloat16)
+    mine_out[...] = mine
     for b in range(blocks):
         value = jnp.dot(mine, ada[b], preferred_element_type=jnp.float32)
         part[:, b * images : (b + 1) * images, :] = value.reshape(row_size, pad, -1)[:, :images]
@@ -418,9 +419,12 @@
     return pl.pallas_call(
         functools.partial(start_kernel, row_size, head_size, images, blocks, count),
         out_shape=[jax.ShapeDtypeStruct((row_size,) + item.shape, item.dtype) for item in shards]
-        + [jax.ShapeDtypeStruct((head_size,) + chunk, f32)],
+        + [
+            jax.ShapeDtypeStruct((head_size,) + chunk, f32),
+            jax.ShapeDtypeStruct((row_size * cond.shape[0], ada.shape[1]), cond.dtype),
+        ],
         in_specs=[vmem] * 3 + [anywhere] * count,
-        out_specs=[anywhere] * count + [vmem],
+        out_specs=[anywhere] * count + [vmem] * 2,
         scratch_shapes=[
             pltpu.VMEM((row_size,) + cond.shape, cond.dtype),
             pltpu.VMEM((row_size,) + chunk, f32),
@@ -446,47 +450,439 @@
     )(cond, ada, bias, *shards)
 
 
-def scatter_kernel(row_size, head_size, count, *refs):
-    ins, outs = refs[:count], refs[count : 2 * count]
-    scratch = refs[2 * count : 6 * count]
-    send, recv, load = refs[6 * count :]
+def finish_kernel(row_size, head_size, images, blocks, count, *refs):
+    small, mine, ada, factor = refs[:4]
+    ins = refs[4 : 4 + count]
+    ada_out, ada_bias_out, qkv_bias_out, cond_out = refs[4 + count : 8 + count]
+    outs = refs[8 + count : 8 + 2 * count]
+    refs = refs[8 + 2 * count :]
+    scratch = refs[: 4 * count]
+    refs = refs[4 * count :]
+    every, part, held, met, side, far, total, landed = refs[:8]
+    send, recv, load, small_send, small_recv, small_keep = refs[8:14]
+    cond_send, cond_recv, cond_load, head_send, head_recv = refs[14:]
     place = Place(row_size, head_size)
-    place.greet(False)
-    scatter_all(
-        [
-            Scatter(
-                place, ins[i], outs[i], *scratch[4 * i : 4 * i + 4], send.at[i], recv.at[i], load.at[i]
-            )
-            for i in range(count)
-        ]
-    )
-
-
-def scatter_call(row_size, head_size, grads):
+    place.greet(True)
+    lead = Gather(place, small, every, small_send, small_recv, small_keep.at[0])
+    lead.begin()
+    items = [
+        Scatter(
+            place, ins[i], outs[i], *scratch[4 * i : 4 * i + 4], send.at[i], recv.at[i], load.at[i]
+        )
+        for i in range(count)
+    ]
+    for item in items:
+        item.begin()
+    hops = range(1, place.sizes[0])
+    for k in hops:
+        lead.first(k)
+    for item in items:
+        item.first()
+    lead.second()
+    items[0].second()
+    lead.finish()
+    rows = small.shape[0]
+    share, width = ada.shape[1], cond_out.shape[1]
+    grads = every[...].reshape(row_size * rows, -1)
+    columns = qkv_bias_out.shape[1]
+    for b in range(blocks):
+        value = dot_tn(mine[b], grads)
+        ada_out[b] = value[:share]
+        ada_bias_out[b : b + 1, :] = value[share : share + 1]
+        qkv_bias_out[b : b + 1, :] = value[share + 1 : share + 2, :columns]
+    lane = lax.broadcasted_iota(jnp.int32, (share, width), 1)
+    slot = lax.broadcasted_iota(jnp.int32, (share, width), 0)
+    pick = jnp.where(lane == lax.axis_index("rows") * share + slot, 1.0, 0.0).astype(jnp.bfloat16)
+    back = 0.0
+    for b in range(blocks):
+        value = dot_nt(grads, ada[b]).reshape(row_size, rows, share)
+        back = back + value[:, b * images : (b + 1) * images]
+    pad = part.shape[1]
+    back = back.reshape(row_size * images, share).astype(jnp.bfloat16)
+    part[...] = jnp.zeros_like(part)
+    part[:, :images, :] = dot_nn(back, pick).reshape(row_size, images, width)
+    sums = Scatter(place, part, total, held, met, side, far, cond_send, cond_recv, cond_load)
+    sums.begin()
+    sums.first()
+    for item in items[1:2]:
+        item.second()
+    sums.second()
+    for item in items[2:]:
+        item.second()
+    sums.finish()
+    across = Across(
+        place, lambda by: total, lambda by: landed.at[by - 1], head_send, head_recv, 0
+    )
+    for by in range(1, head_size):
+        across.start(by)
+    for item in items:
+        item.finish()
+    value = total[...]
+    for by in range(1, head_size):
+        across.arrived(by)
+        value = value + landed[by - 1]
+    cond_out[...] = value * factor[...]
+    across.left()
+
+
+def finish_call(row_size, head_size, images, grads, small, mine, ada, factor, columns):
     count = len(grads)
     copies = scatter_count(row_size)
+    small_copies = gather_count(row_size)
+    blocks, share, wide = ada.shape
     a, b = 4, row_size // 8
+    f32 = jnp.float32
+    shape = jax.ShapeDtypeStruct
     scratch = []
     for grad in grads:
         chunk = grad.shape[1:]
         for lead in ((a, b), (a, b), (b - 1, a), (a - 1,)):
             scratch.append(pltpu.VMEM(lead + chunk, grad.dtype))
+    chunk = factor.shape
+    anywhere = pl.BlockSpec(memory_space=pl.ANY)
+    vmem = pl.BlockSpec(memory_space=pltpu.VMEM)
     return pl.pallas_call(
-        functools.partial(scatter_kernel, row_size, head_size, count),
-        out_shape=[jax.ShapeDtypeStruct(grad.shape[1:], jnp.float32) for grad in grads],
-        in_specs=[pl.BlockSpec(memory_space=pl.ANY)] * count,
-        out_specs=[pl.BlockSpec(memory_space=pltpu.VMEM)] * count,
+        functools.partial(finish_kernel, row_size, head_size, images, blocks, count),
+        out_shape=[
+            shape(ada.shape, f32),
+            shape((blocks, wide), f32),
+            shape((blocks, columns), f32),
+            shape(factor.shape, f32),
+        ]
+        + [shape(grad.shape[1:], f32) for grad in grads],
+        in_specs=[anywhere] + [vmem] * 3 + [anywhere] * count,
+        out_specs=[vmem] * (4 + count),
         scratch_shapes=scratch
+        + [
+            pltpu.VMEM((row_size,) + small.shape, small.dtype),
+            pltpu.VMEM((row_size,) + chunk, f32),
+            pltpu.VMEM((a, b) + chunk, f32),
+            pltpu.VMEM((a, b) + chunk, f32),
+            pltpu.VMEM((b - 1, a) + chunk, f32),
+            pltpu.VMEM((a - 1,) + chunk, f32),
+            pltpu.VMEM(chunk, f32),
+            pltpu.VMEM((head_size - 1,) + chunk, f32),
+            pltpu.SemaphoreType.DMA((count, copies)),
+            pltpu.SemaphoreType.DMA((count, copies)),
+            pltpu.SemaphoreType.DMA((count, a * b)),
+            pltpu.SemaphoreType.DMA((small_copies,)),
+            pltpu.SemaphoreType.DMA((small_copies,)),
+            pltpu.SemaphoreType.DMA((1,)),
+            pltpu.SemaphoreType.DMA((copies,)),
+            pltpu.SemaphoreType.DMA((copies,)),
+            pltpu.SemaphoreType.DMA((a * b,)),
+            pltpu.SemaphoreType.DMA((head_size - 1,)),
+            pltpu.SemaphoreType.DMA((head_size - 1,)),
+        ],
+        compiler_params=pltpu.CompilerParams(
+            collective_id=2, has_side_effects=True, vmem_limit_bytes=56 * 2**20
+        ),
+        name="finish",
+    )(small, mine, ada, factor, *grads)
+
+
+def weight_grads_kernel(*refs):
+    count = len(refs) // 3
+    for i in range(count):
+        left, right, out = refs[2 * i], refs[2 * i + 1], refs[2 * count + i]
+        columns = out.shape[1]
+        for at in range(0, columns, 256):
+            size = min(256, columns - at)
+            out[:, at : at + size] = dot_tn(left[...], right[:, at : at + size]).astype(out.dtype)
+
+
+def weight_grads(*pairs):
+    vmem = pl.BlockSpec(memory_space=pltpu.VMEM)
+    flat = [item for pair in pairs for item in pair]
+    flops = sum(2 * left.size * right.shape[1] for left, right in pairs)
+    moved = sum(2 * (left.size + right.size + left.shape[1] * right.shape[1]) for left, right in pairs)
+    return pl.pallas_call(
+        weight_grads_kernel,
+        out_shape=[
+            jax.ShapeDtypeStruct((left.shape[1], right.shape[1]), jnp.bfloat16)
+            for left, right in pairs
+        ],
+        in_specs=[vmem] * len(flat),
+        out_specs=[vmem] * len(pairs),
+        compiler_params=pltpu.CompilerParams(vmem_limit_bytes=48 * 2**20),
+        cost_estimate=pl.CostEstimate(flops=flops, bytes_accessed=moved, transcendentals=0),
+        name="weight_grads",
+    )(*flat)
+
+
+def tile_of(width):
+    return next(size for size in (256, 128, width) if width % size == 0)
+
+
+def dot_nn(left, right):
+    return jnp.dot(left, right, preferred_element_type=jnp.float32)
+
+
+def dot_nt(left, right):
+    return lax.dot_general(left, right, (((1,), (1,)), ((), ())), preferred_element_type=jnp.float32)
+
+
+def dot_tn(left, right):
+    return lax.dot_general(left, right, (((0,), (0,)), ((), ())), preferred_element_type=jnp.float32)
+
+
+def tiles(width, size, body):
+    @pl.loop(0, width // size)
+    def _(step):
+        body(step, pl.multiple_of(step * size, size))
+
+
+class Across:
+    def __init__(self, place, sources, targets, send, recv, stage):
+        count = place.heads - 1
+        self.copies = [
+            pltpu.make_async_remote_copy(
+                src_ref=sources(by),
+                dst_ref=targets(by),
+                send_sem=send.at[stage * count + by - 1],
+                recv_sem=recv.at[stage * count + by - 1],
+                device_id=place.flip(by),
+                device_id_type=MESH,
+            )
+            for by in range(1, place.heads)
+        ]
+
+    def start(self, by):
+        self.copies[by - 1].start()
+
+    def arrived(self, by):
+        self.copies[by - 1].wait_recv()
+
+    def left(self):
+        for copy in self.copies:
+            copy.wait_send()
+
+
+class Streamed:
+    def __init__(self, buffer, out, sems, size):
+        self.buffer, self.out, self.sems, self.size = buffer, out, sems, size
+
+    def copy(self, step):
+        return pltpu.make_async_copy(
+            self.buffer.at[step % 2],
+            self.out.at[:, pl.ds(pl.multiple_of(step * self.size, self.size), self.size)],
+            self.sems.at[step % 2],
+        )
+
+    def put(self, step, value):
+        @pl.when(step >= 2)
+        def _():
+            self.copy(step - 2).wait()
+
+        self.buffer[step % 2] = value.astype(self.buffer.dtype)
+        self.copy(step).start()
+
+    def drain(self, steps):
+        for step in range(max(steps - 2, 0), steps):
+            self.copy(step).wait()
+
+
+def mlp_back_kernel(row_size, head_size, count, *refs):
+    (incoming, gate_mlp, scale_mlp, gate_attn, normed, inverse) = refs[:6]
+    streams = refs[6:12]
+    grads = refs[12 : 12 + count]
+    outs = refs[12 + count : 18 + 2 * count]
+    grad_in, grad_mid, branch_out, grad_att, gu_out, down_out = outs[:6]
+    sums = outs[6:]
+    refs = refs[18 + 2 * count :]
+    down, gate_up, gu, inputs, hidden, proj = refs[:6]
+    mlp_all, branch_all, ggu, parcel, landed, own_part, buffer = refs[6:13]
+    loads, sends, recvs, tile_sems, out_sem = refs[13:18]
+    scratch = refs[18 : 18 + 4 * count]
+    sum_send, sum_recv, sum_load = refs[18 + 4 * count :]
+    place = Place(row_size, head_size)
+    heads = head_size
+    own, width = incoming.shape
+    units = hidden.shape[1]
+    step_units = tile_of(units)
+    step_width = tile_of(width)
+    copies = [
+        pltpu.make_async_copy(source, target, loads.at[i])
+        for i, (source, target) in enumerate(
+            zip(streams, (down, gate_up, gu, inputs, hidden, proj))
+        )
+    ]
+    place.greet(True)
+    mlp_all[0] = (gate_mlp[...] * incoming[...]).astype(jnp.bfloat16)
+    first = Across(place, lambda by: mlp_all.at[0], lambda by: mlp_all.at[by], sends, recvs, 0)
+    for by in range(1, heads):
+        first.start(by)
+    for copy in copies:
+        copy.start()
+    items = [
+        Scatter(
+            place,
+            grads[i],
+            sums[i],
+            *scratch[4 * i : 4 * i + 4],
+            sum_send.at[i],
+            sum_recv.at[i],
+            sum_load.at[i],
+        )
+        for i in range(count)
+    ]
+    for item in items:
+        item.begin()
+
+    def hidden_back(slot):
+        rows = pl.ds(slot * own, own)
+
+        def body(step, at):
+            gate = gate_up[rows, pl.ds(at, step_units)]
+            up = gate_up[rows, pl.ds(pl.multiple_of(units + at, 128), step_units)]
+            grad = dot_nn(mlp_all[slot], down[:, pl.ds(at, step_units)])
+            logistic = jax.nn.sigmoid(gate)
+            ggu[rows, pl.ds(at, step_units)] = (
+                grad * up * logistic * (1.0 + gate * (1.0 - logistic))
+            ).astype(jnp.bfloat16)
+            ggu[rows, pl.ds(pl.multiple_of(units + at, 128), step_units)] = (
+                grad * gate * logistic
+            ).astype(jnp.bfloat16)
+
+        tiles(units, step_units, body)
+
+    copies[0].wait()
+    copies[1].wait()
+    hidden_back(0)
+    for item in items:
+        item.first()
+    for by in range(1, heads):
+        first.arrived(by)
+        hidden_back(by)
+    copies[2].wait()
+    second = Across(
+        place, lambda by: parcel.at[by - 1], lambda by: landed.at[by - 1], sends, recvs, 1
+    )
+    for by in range(1, heads):
+
+        def body(step, at):
+            parcel[by - 1, :, pl.ds(at, step_width)] = dot_nt(
+                ggu[pl.ds(by * own, own), :], gu[pl.ds(at, step_width), :]
+            ).astype(jnp.bfloat16)
+
+        tiles(width, step_width, body)
+        second.start(by)
+
+    def body(step, at):
+        own_part[:, pl.ds(at, step_width)] = dot_nt(ggu[pl.ds(0, own), :], gu[pl.ds(at, step_width), :])
+
+    tiles(width, step_width, body)
+    for item in items[:1]:
+        item.second()
+    copies[3].wait()
+    out = Streamed(buffer, gu_out, tile_sems, step_units)
+
+    def body(step, at):
+        out.put(step, dot_tn(inputs[...], ggu[:, pl.ds(at, step_units)]))
+
+    tiles(2 * units, step_units, body)
+    total = own_part[...]
+    for by in range(1, heads):
+        second.arrived(by)
+        total = total + landed[by - 1].astype(jnp.float32)
+    grad_in[...] = total
+    scaled = total * (1.0 + scale_mlp[...])
+    middle = incoming[...] + inverse[...] * (
+        scaled
+        - jnp.mean(scaled, axis=-1, keepdims=True)
+        - normed[...] * jnp.mean(scaled * normed[...], axis=-1, keepdims=True)
+    )
+    grad_mid[...] = middle
+    branch_all[0] = (gate_attn[...] * middle).astype(jnp.bfloat16)
+    third = Across(place, lambda by: branch_all.at[0], lambda by: branch_all.at[by], sends, recvs, 2)
+    for by in range(1, heads):
+        third.start(by)
+    for item in items[1:2]:
+        item.second()
+    out.drain(2 * units // step_units)
+    copies[4].wait()
+    copies[5].wait()
+    out = Streamed(buffer, down_out, tile_sems, step_units)
+
+    def body(step, at):
+        out.put(
+            step,
+            dot_tn(mlp_all[...].reshape(heads * own, width), hidden[:, pl.ds(at, step_units)]),
+        )
+
+    tiles(units, step_units, body)
+    grad_att[pl.ds(0, own), :] = dot_nn(branch_all[0], proj[...]).astype(jnp.bfloat16)
+    for item in items[2:]:
+        item.second()
+    for by in range(1, heads):
+        third.arrived(by)
+        grad_att[pl.ds(by * own, own), :] = dot_nn(branch_all[by], proj[...]).astype(jnp.bfloat16)
+    keep = pltpu.make_async_copy(branch_all, branch_out, out_sem.at[0])
+    keep.start()
+    out.drain(units // step_units)
+    for item in items:
+        item.finish()
+    for stage in (first, second, third):
+        stage.left()
+    keep.wait()
+
+
+def mlp_back_call(row_size, head_size, near, streams, grads):
+    count = len(grads)
+    own, width = near[0].shape
+    down, gate_up, gu, inputs, hidden, proj = streams
+    units = hidden.shape[1]
+    tokens = hidden.shape[0]
+    a, b = 4, row_size // 8
+    copies = scatter_count(row_size)
+    scratch = []
+    for grad in grads:
+        chunk = grad.shape[1:]
+        for lead in ((a, b), (a, b), (b - 1, a), (a - 1,)):
+            scratch.append(pltpu.VMEM(lead + chunk, grad.dtype))
+    anywhere = pl.BlockSpec(memory_space=pl.ANY)
+    vmem = pl.BlockSpec(memory_space=pltpu.VMEM)
+    shape = jax.ShapeDtypeStruct
+    f32, bf16 = jnp.float32, jnp.bfloat16
+    return pl.pallas_call(
+        functools.partial(mlp_back_kernel, row_size, head_size, count),
+        out_shape=[
+            shape((own, width), f32),
+            shape((own, width), f32),
+            shape((head_size, own, width), bf16),
+            shape((tokens, proj.shape[1]), bf16),
+            shape((width, 2 * units), bf16),
+            shape((width, units), bf16),
+        ]
+        + [shape(grad.shape[1:], f32) for grad in grads],
+        in_specs=[vmem] * 6 + [anywhere] * (6 + count),
+        out_specs=[vmem, vmem, anywhere, vmem, anywhere, anywhere] + [vmem] * count,
+        scratch_shapes=[pltpu.VMEM(item.shape, item.dtype) for item in streams]
+        + [
+            pltpu.VMEM((head_size, own, width), bf16),
+            pltpu.VMEM((head_size, own, width), bf16),
+            pltpu.VMEM((tokens, 2 * units), bf16),
+            pltpu.VMEM((head_size - 1, own, width), bf16),
+            pltpu.VMEM((head_size - 1, own, width), bf16),
+            pltpu.VMEM((own, width), f32),
+            pltpu.VMEM((2, width, tile_of(units)), bf16),
+            pltpu.SemaphoreType.DMA((6,)),
+            pltpu.SemaphoreType.DMA((3 * (head_size - 1),)),
+            pltpu.SemaphoreType.DMA((3 * (head_size - 1),)),
+            pltpu.SemaphoreType.DMA((2,)),
+            pltpu.SemaphoreType.DMA((1,)),
+        ]
+        + scratch
         + [
             pltpu.SemaphoreType.DMA((count, copies)),
             pltpu.SemaphoreType.DMA((count, copies)),
             pltpu.SemaphoreType.DMA((count, a * b)),
         ],
         compiler_params=pltpu.CompilerParams(
-            collective_id=2, has_side_effects=True, vmem_limit_bytes=56 * 2**20
+            collective_id=3, has_side_effects=True, vmem_limit_bytes=62 * 2**20
         ),
-        name="sum_rows",
-    )(*grads)
+        name="mlp_back",
+    )(*near, *streams, *grads)
 
 
 def rope_parts(coords):
@@ -582,12 +978,15 @@
     return total
 
 
-def block_forward(residual, pieces, qkv_full, qkv_b, proj_t, gu_full, down_t, image_ids, geometry):
+def block_forward(residual, ready, pieces, qkv_full, qkv_b, proj_t, gu_full, down_t, image_ids, geometry):
     shift_attn, scale_attn, gate_attn, shift_mlp, scale_mlp, gate_mlp = pieces
     own_rows = residual.shape[0]
     count_rows, row_len = image_ids.shape
-    normed_attn, inverse_attn = normalize(residual)
-    input_attn, _ = spread((normed_attn * (1.0 + scale_attn) + shift_attn).astype(jnp.bfloat16))
+    if ready is None:
+        normed_attn, inverse_attn = normalize(residual)
+        input_attn, _ = spread((normed_attn * (1.0 + scale_attn) + shift_attn).astype(jnp.bfloat16))
+    else:
+        normed_attn, inverse_attn, input_attn = ready
     packed = plain_dot(input_attn, qkv_full) + qkv_b
     heads_here = packed.shape[1] // (3 * HD)
     packed = packed.reshape(count_rows, row_len, heads_here, 3, HD)
@@ -620,15 +1019,16 @@
         normed_mlp,
         inverse_mlp,
         input_mlp,
-        gate_part,
-        up_part,
+        gate_up,
         hidden,
         mlp_out,
     )
     return (result, stored)
 
 
-def block_backward(incoming, pieces, stored, qkv_full, proj_t, gu_full, down_t, image_ids, geometry):
+def block_backward(
+    incoming, ready, later, pieces, stored, qkv_full, proj_t, gu_full, down_t, image_ids, geometry
+):
     shift_attn, scale_attn, gate_attn, shift_mlp, scale_mlp, gate_mlp = pieces
     (
         normed_attn,
@@ -643,34 +1043,49 @@
         normed_mlp,
         inverse_mlp,
         input_mlp,
-        gate_part,
-        up_part,
+        gate_up,
         hidden,
         mlp_out,
     ) = stored
     own_rows = incoming.shape[0]
     count_rows, row_len = image_ids.shape
-    grad_mlp = (gate_mlp * incoming).astype(jnp.bfloat16)
+    units = hidden.shape[1]
     grad_gate_mlp = incoming * mlp_out
-    gathered_mlp, _ = spread(grad_mlp)
-    down_grad = lead_dot(gathered_mlp, hidden).astype(jnp.bfloat16)
-    grad_hidden = plain_dot(gathered_mlp, down_t)
-    logistic = jax.nn.sigmoid(gate_part)
-    grad_gate_part = grad_hidden * up_part * logistic * (1.0 + gate_part * (1.0 - logistic))
-    grad_up_part = grad_hidden * gate_part * logistic
-    grad_gate_up = jnp.concatenate([grad_gate_part, grad_up_part], axis=1).astype(jnp.bfloat16)
-    gu_grad = lead_dot(input_mlp, grad_gate_up).astype(jnp.bfloat16)
-    grad_input_mlp, gu_grad = collect(
-        grad_gate_up, lambda rows: tail_dot(rows, gu_full), own_rows, gu_grad
-    )
+    sums = ()
+    if later:
+        grad_input_mlp, grad_middle, gathered_branch, grad_attended, gu_grad, down_grad, *sums = (
+            mlp_back_call(
+                lax.axis_size("rows"),
+                lax.axis_size("heads"),
+                (incoming, gate_mlp, scale_mlp, gate_attn, normed_mlp, inverse_mlp),
+                (down_t, gate_up, gu_full, input_mlp, hidden, proj_t),
+                later,
+            )
+        )
+        gathered_branch = gathered_branch.reshape(-1, gathered_branch.shape[-1])
+    else:
+        gathered_mlp = ready
+        down_grad = lead_dot(gathered_mlp, hidden).astype(jnp.bfloat16)
+        grad_hidden = plain_dot(gathered_mlp, down_t)
+        gate_part = gate_up[:, :units]
+        up_part = gate_up[:, units:]
+        logistic = jax.nn.sigmoid(gate_part)
+        grad_gate_part = grad_hidden * up_part * logistic * (1.0 + gate_part * (1.0 - logistic))
+        grad_up_part = grad_hidden * gate_part * logistic
+        grad_gate_up = jnp.concatenate([grad_gate_part, grad_up_part], axis=1).astype(jnp.bfloat16)
+        gu_grad = lead_dot(input_mlp, grad_gate_up).astype(jnp.bfloat16)
+        grad_input_mlp, gu_grad = collect(
+            grad_gate_up, lambda rows: tail_dot(rows, gu_full), own_rows, gu_grad
+        )
+        grad_middle = incoming + norm_back(
+            grad_input_mlp * (1.0 + scale_mlp), normed_mlp, inverse_mlp
+        )
+        grad_branch = (gate_attn * grad_middle).astype(jnp.bfloat16)
+        gathered_branch, down_grad = spread(grad_branch, down_grad)
+        grad_attended = plain_dot(gathered_branch, proj_t).astype(jnp.bfloat16)
     gu_out = lax.psum_scatter(gu_grad, "rows", scatter_dimension=0, tiled=True).astype(jnp.float32)
-    grad_middle = incoming + norm_back(grad_input_mlp * (1.0 + scale_mlp), normed_mlp, inverse_mlp)
-    grad_branch = (gate_attn * grad_middle).astype(jnp.bfloat16)
     grad_gate_attn = grad_middle * branch
     heads_here = queries.shape[2]
-    gathered_branch, down_grad = spread(grad_branch, down_grad)
-    proj_grad = lead_dot(gathered_branch, attended).astype(jnp.bfloat16)
-    grad_attended = plain_dot(gathered_branch, proj_t).astype(jnp.bfloat16)
     grad_attended = grad_attended.reshape(count_rows, row_len, heads_here, HD)
     grad_query, grad_key, grad_value = attend_back(
         queries, key_rows, value_rows, image_ids, logsum, grad_attended
@@ -683,7 +1098,7 @@
         .astype(jnp.bfloat16)
     )
     qkv_bias_grad = jnp.sum(grad_packed, axis=0, dtype=jnp.float32)
-    qkv_grad = lead_dot(input_attn, grad_packed).astype(jnp.bfloat16)
+    qkv_grad, proj_grad = weight_grads((input_attn, grad_packed), (gathered_branch, attended))
     grad_input_attn, (qkv_grad, proj_grad) = collect(
         grad_packed, lambda rows: tail_dot(rows, qkv_full), own_rows, (qkv_grad, proj_grad)
     )
@@ -701,7 +1116,7 @@
         ],
         axis=1,
     )
-    return (grad_input, grad_mods, (qkv_grad, qkv_bias_grad, proj_grad, gu_out, down_grad))
+    return (grad_input, grad_mods, (qkv_grad, qkv_bias_grad, proj_grad, gu_out, down_grad), sums)
 
 
 def heads_in_order(value):
@@ -779,28 +1194,21 @@
     cond_act = jax.nn.silu(cond_wide).astype(jnp.bfloat16)
     pad = -image_count % 16
     bias_rows = jnp.repeat(ada_bias.astype(jnp.float32), image_count, axis=0)
-    first_qkv, first_proj, mods = start_call(
+    *early, mods, cond_mine = start_call(
         row_size,
         head_size,
         jnp.pad(cond_act, ((0, pad), (0, 0))),
         ada_weight,
         bias_rows,
-        [qkv_weight[0], proj_weight[0].T],
+        [item for b in range(block_count) for item in (qkv_weight[b], proj_weight[b].T)],
     )
     qkv_full, gu_full, down_t, proj_t = [], [], [], []
     for b in range(block_count):
-        if b == 0:
-            qkv_full.append(first_qkv.reshape(-1, first_qkv.shape[-1]))
-            proj_t.append(first_proj.reshape(-1, first_proj.shape[-1]))
-        else:
-            qkv_full.append(gathered(qkv_weight[b]))
-            proj_t.append(gathered(proj_weight[b].T))
+        qkv_full.append(early[2 * b].reshape(-1, early[2 * b].shape[-1]))
+        proj_t.append(early[2 * b + 1].reshape(-1, early[2 * b + 1].shape[-1]))
         gu_full.append(gathered(gu_weight[b].reshape(shard_rows, -1)))
         down_t.append(gathered(down_weight[b].T))
     mod_all = mods.reshape(head_size, block_count, image_count, -1)
-    cond_mine = lax.all_to_all(
-        cond_act.reshape(image_count, row_size, -1).transpose(1, 0, 2), "rows", 0, 0
-    ).reshape(row_size * image_count, -1)
     modulation = [
         jnp.concatenate([mod_all[index, b] for index in range(head_size)], axis=1)
         for b in range(block_count)
@@ -809,10 +1217,26 @@
         [piece_of(modulation[b], own_images, index) for index in range(6)] for b in range(block_count)
     ]
     residual = tokens.astype(jnp.float32)
+    all_images = image_ids.reshape(-1)
+    every_token, _ = spread(tokens)
+    every_token = every_token.astype(jnp.float32)
+    normed, inverse = normalize(every_token)
+    shift, scale = [piece_of(modulation[0], all_images, index) for index in range(2)]
+    forward_ready = [None] * block_count
+    forward_ready[0] = (
+        normed[:own_rows],
+        inverse[:own_rows],
+        (normed * (1.0 + scale) + shift).astype(jnp.bfloat16),
+    )
+    every_cotangent, _ = spread(cotangent)
+    gate = piece_of(modulation[-1], all_images, 5)
+    backward_ready = [None] * block_count
+    backward_ready[-1] = (gate * every_cotangent.astype(jnp.float32)).astype(jnp.bfloat16)
     stored_all = []
     for b in range(block_count):
         residual, stored = block_forward(
             residual,
+            forward_ready[b],
             pieces[b],
             qkv_full[b],
             qkv_bias[b].astype(jnp.float32),
@@ -827,9 +1251,13 @@
     incoming = cotangent.astype(jnp.float32)
     block_grads = [None] * block_count
     image_sums = [None] * block_count
+    block_sums = [None] * block_count
+    later = []
     for b in reversed(range(block_count)):
-        incoming, grad_mods, gradients = block_backward(
+        incoming, grad_mods, gradients, sums = block_backward(
             incoming,
+            backward_ready[b],
+            later,
             pieces[b],
             stored_all[b],
             qkv_full[b],
@@ -843,60 +1271,64 @@
             picker, grad_mods, (((0,), (0,)), ((), ())), precision=highest
         )
         block_grads[b] = gradients
+        later = [
+            gradients[which].reshape(row_size, shard_rows, -1) for which in (4, 0, 2)
+        ]
+        if b + 1 < block_count:
+            block_sums[b + 1] = sums
     image_grads = heads_share(jnp.stack(image_sums)).astype(jnp.bfloat16)
     bias_sums = jnp.stack([item[1] for item in block_grads])
     bias_high = bias_sums.astype(jnp.bfloat16)
     bias_rest = bias_sums - bias_high.astype(jnp.float32)
     bias_middle = bias_rest.astype(jnp.bfloat16)
     bias_low = (bias_rest - bias_middle.astype(jnp.float32)).astype(jnp.bfloat16)
-    small = jnp.concatenate(
-        [
-            image_grads.reshape(1, -1),
-            bias_high.reshape(1, -1),
-            bias_middle.reshape(1, -1),
-            bias_low.reshape(1, -1),
-        ],
-        axis=1,
-    )
-    small = lax.all_gather(small, "rows", axis=0, tiled=True)
-    split = image_grads.size
-    all_grads = small[:, :split].reshape((row_size,) + image_grads.shape)
-    bias_all = small[:, split:].reshape((row_size, 3) + bias_sums.shape).astype(jnp.float32)
-    qkv_bias_out = jnp.sum(bias_all, axis=(0, 1))
-    ada_grads = []
-    cond_partial = 0.0
+    wide = image_grads.shape[-1]
+    bias_parts = jnp.stack([bias_high, bias_middle, bias_low], axis=1)
+    columns = bias_sums.shape[1]
+    bias_parts = jnp.pad(bias_parts, ((0, 0), (0, 0), (0, wide - columns)))
+    small = jnp.concatenate([image_grads.reshape(-1, wide), bias_parts.reshape(-1, wide)])
+    used = small.shape[0]
+    small = jnp.pad(small, ((0, -used % 16), (0, 0)))
+    cond_rows = cond_mine.reshape(row_size, -1, shard_rows)[:, :image_count]
+    row = jnp.arange(small.shape[0])
+    mine = []
     for b in range(block_count):
-        block_grads_all = all_grads[:, b].reshape(row_size * image_count, -1)
-        ada_grads.append(lead_dot(cond_mine, block_grads_all))
-        cond_partial = cond_partial + tail_dot(block_grads_all, ada_weight[b])
-    ada_bias_grads = jnp.sum(all_grads, axis=(0, 2), dtype=jnp.float32)
-    cond_parts = lax.all_to_all(
-        cond_partial.astype(jnp.bfloat16).reshape(row_size, image_count, -1), "rows", 0, 0
-    )
-    cond_rows = cond_parts.transpose(1, 0, 2).reshape(image_count, -1).astype(jnp.float32)
-    cond_total = cond_rows
-    for flip in range(1, head_size):
-        cond_total = cond_total + head_move(cond_rows.astype(jnp.bfloat16), flip).astype(jnp.float32)
+        first = b * image_count
+        lead = jnp.pad(cond_rows, ((0, 0), (first, small.shape[0] - first - image_count), (0, 0)))
+        is_image = (row >= first) & (row < first + image_count)
+        start = block_count * image_count + 3 * b
+        is_bias = (row >= start) & (row < start + 3)
+        ones = jnp.stack([is_image, is_bias], axis=1).astype(jnp.bfloat16)
+        ones = jnp.broadcast_to(ones[None], (row_size,) + ones.shape)
+        both = jnp.concatenate([lead, ones], axis=2)
+        both = jnp.pad(both, ((0, 0), (0, 0), (0, -both.shape[2] % 128)))
+        mine.append(both.reshape(-1, both.shape[2]))
     logistic = jax.nn.sigmoid(cond_wide)
-    cond_grad = cond_total * logistic * (1.0 + cond_wide * (1.0 - logistic))
-    parts = []
-    for b in reversed(range(block_count)):
-        parts += [block_grads[b][4], block_grads[b][2], block_grads[b][0]]
-    sums = scatter_call(
-        row_size, head_size, [part.reshape(row_size, shard_rows, -1) for part in parts]
-    )
-    sums = [sums[3 * b : 3 * b + 3] for b in reversed(range(block_count))]
+    factor = logistic * (1.0 + cond_wide * (1.0 - logistic))
+    factor = jnp.pad(factor, ((0, -image_count % 8), (0, 0)))
+    ada_grads, ada_bias_grads, qkv_bias_out, cond_grad, *block_sums[0] = finish_call(
+        row_size,
+        head_size,
+        image_count,
+        later,
+        small,
+        jnp.stack(mine),
+        ada_weight,
+        factor,
+        columns,
+    )
+    cond_grad = cond_grad[:image_count]
     return (
         block_out,
         incoming,
         cond_grad,
-        jnp.stack(ada_grads),
+        ada_grads,
         ada_bias_grads,
-        jnp.stack([item[2] for item in sums]),
+        jnp.stack([item[1] for item in block_sums]),
         qkv_bias_out,
-        jnp.stack([item[1].T for item in sums]),
+        jnp.stack([item[2].T for item in block_sums]),
         jnp.stack([item[3].reshape(gu_weight.shape[1:]) for item in block_grads]),
-        jnp.stack([item[0].T for item in sums]),
+        jnp.stack([item[0].T for item in block_sums]),
     )
 
 

time: 853 us -> 701 us (0.82)
  waiting for transfers between devices: 277 us -> 58.9 us
  Pallas kernels: 235 us -> 342 us
  matrix products: 154 us -> 114 us
  other arithmetic: 58.9 us -> 76.6 us
  starting transfers between devices: 35.9 us -> 18.7 us
    all_gather x6 -> x4, waiting for transfers between devices: 75 us -> 0.01 us  [gathered(): return lax.all_gather(shard, 'rows', axis=0, tiled=True)]
    reduce_scatter x2, waiting for transfers between devices: 71 us -> 0.02 us  [block_backward(): lax.psum_scatter(gu_grad, 'rows', scatter_dimension=0, tiled=True)]
    ppermute x18 -> x14, waiting for transfers between devices: 125 us -> 58.7 us  [head_move(): lax.ppermute(value, 'heads', [(index, index ^ flip) for index in range(si...]
    pallas_call x1 -> x4, Pallas kernels: 147 us -> 210 us  [the longest x1 101 us: finish_call(): pl.pallas_call(functools.partial(finish_kernel, row_size, head_size, imag...]
    pallas_call x1, Pallas kernels: 88.9 us -> 132 us  [start_call(): pl.pallas_call(functools.partial(start_kernel, row_size, head_size, image...]
    dot_general x10 -> x2, matrix products: 37.3 us -> 13.1 us  [lead_dot(): lax.dot_general(operand, other, (((0,), (0,)), ((), ())), preferred_eleme...]
    optimization_barrier x4 -> x0, local copies, waits for them, and re-layouts: 16.2 us -> none  [collect(): total, arrived, beside = lax.optimization_barrier((total, arrived, beside))]
    dot_general x18 -> x14, matrix products: 50.5 us -> 34.2 us  [tail_dot(): lax.dot_general(operand, other, (((1,), (1,)), ((), ())), preferred_eleme...]
  transfers between devices with their start and end apart: 29 -> 20, of which waited for: 22 -> 10; matrix products, arithmetic and copies ran while one was open for 21% -> 30% of each run, Pallas kernels for 28% -> 49%
where the time goes in v4:
time: 701 us; the launch traced here: 692 us
  Pallas kernels  342 us (49%)
  matrix products  114 us (16%)
  other arithmetic  76.6 us (11%)
  local copies, waits for them, and re-layouts  65.4 us (9%)
  waiting for transfers between devices  58.9 us (8%)
  starting transfers between devices  18.7 us (3%)
  between operations  17.1 us (2%)
    pallas_call x1, Pallas kernels, start_call(): pl.pallas_call(functools.partial(start_kernel, row_size, head_size, image...  132 us
    pallas_call x1, Pallas kernels, finish_call(): pl.pallas_call(functools.partial(finish_kernel, row_size, head_size, imag...  101 us
    pallas_call x1, Pallas kernels, mlp_back_call(): pl.pallas_call(functools.partial(mlp_back_kernel, row_size, head_size, co...  96.3 us
    ppermute x14, waiting for transfers between devices, head_move(): lax.ppermute(value, 'heads', [(index, index ^ flip) for index in range(si...  58.7 us
    dot_general x14, matrix products, tail_dot(): lax.dot_general(operand, other, (((1,), (1,)), ((), ())), preferred_eleme...  34.2 us
    dot_general x6, matrix products, plain_dot(): return jnp.dot(operand, other, preferred_element_type=jnp.float32)  34 us
    unnamed x446, local copies, waits for them, and re-layouts  31.4 us
    ppermute x14, starting transfers between devices, head_move(): lax.ppermute(value, 'heads', [(index, index ^ flip) for index in range(si...  18.1 us
  transfers between devices with their start and end apart: 20, of which 10 were waited for; matrix products, arithmetic and copies ran while one was open for 30% of the time, Pallas kernels for 49%

profile of v4, /device:TPU:0, one launch (start us, length us, event | category | flops | bytes accessed | tf_op | source)
XLA Modules:
  0.0 692.4 jit_solution(6185476303970550857)
XLA Ops:
  19.0 132.0 %start.1 = (bf16[16,72,1728]{2,1,0:T(8,128)(2,1)}, bf16[16,72,576]{2,1,0:T(8,128)(2,1)S(1)}, bf16[16,72,1728]{2,1,0:T(8,128)(2,1)}, bf16[16,72,576]{2,1,0:T(8,12...) custom-call(bf16[16,1152]{1,0:T(8,128)(2,1)S(1)} %pad.31.refs_0_, ...), custom_call_target="tpu_custom_call" | custom-call | tf_op jit(solution)/shard_map/start/pallas_call | solution.py:419
  158.3 7.3 %fusion.13 = (f32[512,1152]{1,0:T(8,128)}, bf16[512,1152]{1,0:T(8,128)(2,1)S(1)}) fusion(f32[512]{0:T(512)S(1)} %add_rsqrt_fusion, f32[512]{0:T(512)S(1)} %broadcast_multiply_fusion.2, bf16[256,1152]{1,0:T(8,128)(2,1)} %collective-permute-done, bf16[256,1152]{1,0:T(8,128)(2,1)} %param.13, f32[1152]{0:T(1024)S(1)} %get-tuple-element.155, ...), kind=kLoop, calls=%fused_computation.45 | loop fusion | flops 10616832 | bytes 4761600 | tf_op jit(solution)/shard_map/mul | solution.py:21
  180.6 11.7 %collective-permute-done.1 = bf16[256,1152]{1,0:T(8,128)(2,1)S(1)} collective-permute-done((bf16[256,1152]{1,0:T(8,128)(2,1)S(1)}, bf16[256,1152]{1,0:T(8,128)(2,1)S(1)}, u32[]{:S(2)}, u32[]{:S(2)}) %collective-permute-start.1) | collective-permute-done | bytes 589856 | tf_op jit(solution)/shard_map/ppermute | solution.py:51
  202.9 8.9 %collective-permute-done.2 = bf16[256,1152]{1,0:T(8,128)(2,1)} collective-permute-done((bf16[256,1152]{1,0:T(8,128)(2,1)S(1)}, bf16[256,1152]{1,0:T(8,128)(2,1)}, u32[]{:S(2)}, u32[]{:S(2)}) %collective-permute-start.2) | collective-permute-done | bytes 589856 | tf_op jit(solution)/shard_map/ppermute | solution.py:51
  211.9 6.6 fusion.106.refs_7_
  223.1 3.6 convolution_convert_fusion.3
  229.9 9.9 %collective-permute-done.3 = bf16[256,1152]{1,0:T(8,128)(2,1)S(1)} collective-permute-done((bf16[256,1152]{1,0:T(8,128)(2,1)S(1)}, bf16[256,1152]{1,0:T(8,128)(2,1)S(1)}, u32[]{:S(2)}, u32[]{:S(2)}) %collective-permute-start.3) | collective-permute-done | bytes 589856 | tf_op jit(solution)/shard_map/ppermute | solution.py:51
  248.0 8.2 %collective-permute-done.4 = bf16[256,1152]{1,0:T(8,128)(2,1)S(1)} collective-permute-done((bf16[256,1152]{1,0:T(8,128)(2,1)S(1)}, bf16[256,1152]{1,0:T(8,128)(2,1)S(1)}, u32[]{:S(2)}, u32[]{:S(2)}) %collective-permute-start.4) | collective-permute-done | bytes 589856 | tf_op jit(solution)/shard_map/ppermute | solution.py:51
  256.2 4.9 convolution_add_fusion
  278.0 6.0 collective-permute-done.5
  296.8 4.2 collective-permute-done.6
  301.0 10.3 %fusion.42 = f32[512,3072]{1,0:T(8,128)} fusion(bf16[1152,3072]{1,0:T(8,128)(2,1)} %all-gather.9.cloned.1.call-done, bf16[256,1152]{1,0:T(8,128)(2,1)} %collective-permute-done.6, bf16[256,1152]{1,0:T(8,128)(2,1)} %add_convert_fusion.2), kind=kOutput, calls=%fused_computation.142 | convolution fusion | flops 3626237952 | bytes 14548992 | tf_op jit(solution)/shard_map/dot_general | solution.py:969
  311.3 7.5 %multiply_convert_fusion.2 = (bf16[512,1536]{1,0:T(8,128)(2,1)S(1)}, bf16[512,1536]{1,0:T(8,128)(2,1)S(1)}, bf16[512,1536]{1,0:T(8,128)(2,1)S(1)}) fusion(f32[512,3072]{1,0:T(8,128)} %fusion.42, bf16[1152,1536]{1,0:T(8,128)(2,1)} %all-gather.11.cloned.1.call-done, bf16[256,1152]{1,0:T(8,128)(2,1)} %collective-permute-done.8, bf16[256,1152]{1,0:T(8,128)(2,1)} %param.25, ...), kind=kOutput, calls=%fused_computation.37 | convolution fusion | flops 1830420480 | bytes 15749120 | tf_op jit(solution)/shard_map/dot_general | solution.py:969
  322.9 7.5 %convolution_convert_fusion = bf16[1152,3072]{1,0:T(8,128)(2,1)} fusion(bf16[512,1536]{1,0:T(8,128)(2,1)S(1)} %get-tuple-element.185, bf16[512,1536]{1,0:T(8,128)(2,1)S(1)} %get-tuple-element.186, bf16[256,1152]{1,0:T(8,128)(2,1)} %collective-permute-done.6, bf16[256,1152]{1,0:T(8,128)(2,1)} %add_convert_fusion.2), kind=kOutput, calls=%fused_computation | convolution fusion | flops 3636068352 | bytes 11403264 | tf_op jit(solution)/shard_map/dot_general | solution.py:33
  330.3 5.9 convolution_convert_fusion.6
  336.7 5.3 fusion.17
  342.0 4.2 collective-permute-done.9
  347.2 3.6 multiply_convert_fusion.6
  353.6 5.6 convolution_convert_fusion.1
  363.3 5.0 multiply_reduce_fusion.1
  380.3 3.1 copy.79
  384.5 4.0 copy.80.refs_1_
  388.6 3.9 convolution_convert_fusion.5
  394.5 6.3 weight_grads.2
  408.0 96.3 %mlp_back.1 = (f32[256,1152]{1,0:T(8,128)}, f32[256,1152]{1,0:T(8,128)}, bf16[2,256,1152]{2,1,0:T(8,128)(2,1)}, bf16[512,576]{1,0:T(8,128)(2,1)}, bf16[1152,3072...) custom-call(f32[256,1152]{1,0:T(8,128)} %get-tuple-element.235.refs_, ...), custom_call_target="tpu_custom_call" | custom-call | tf_op jit(solution)/shard_map/mlp_back/pallas_call | solution.py:847
  505.6 5.0 multiply_reduce_fusion
  526.7 4.2 copy.90.refs_1_
  532.5 6.5 weight_grads.3
  543.1 3.5 fusion.33
  546.6 6.0 convolution_bitcast_fusion
  566.3 3.9 collective-permute-done.13
  570.9 100.7 %finish.1 = (f32[2,72,3456]{2,1,0:T(8,128)}, f32[2,3456]{1,0:T(2,128)}, f32[2,1728]{1,0:T(2,128)}, f32[8,1152]{1,0:T(8,128)}, f32[72,1536]{1,0:T(8,128)}, /*index=5*/f32[72,1728]{1,0:T(8,128)}, f32[72,576]{1,0:T(8,128)}) custom-call(bf16[16,3456]{1,0:T(8,128)(2,1)} %fusion.75.refs_0_, bf16[2,256,128]{2,1,0:T(8,128)(2,1)} %pad_maximum_fusion.16.refs_1_, ...), custom_call_target="tpu_custom_call" | custom-call | tf_op jit(solution)/shard_map/finish/pallas_call | solution.py:544
  (654 shorter events, 173.9 us)
Async XLA Ops:
  7.2 204.7 %all-gather.5.cloned.1.call-start = ((), (), s32[]{:S(2)}) async-start(), calls=%async_computation.2 | async-start | bytes 7520256 | tf_op jit(solution)/shard_map/all_gather | solution.py:1191
  9.9 213.2 %all-gather.7.cloned.1.call-start = ((), (), s32[]{:S(2)}) async-start(), calls=%async_computation.3 | async-start | bytes 3760128 | tf_op jit(solution)/shard_map/all_gather | solution.py:1191
  10.8 290.2 %all-gather.9.cloned.1.call-start = ((), (), s32[]{:S(2)}) async-start(), calls=%async_computation.4 | async-start | bytes 7520256 | tf_op jit(solution)/shard_map/all_gather | solution.py:1191
  11.7 299.6 %all-gather.11.cloned.1.call-start = ((), (), s32[]{:S(2)}) async-start(), calls=%async_computation.5 | async-start | bytes 3760128 | tf_op jit(solution)/shard_map/all_gather | solution.py:1191
  11.8 143.1 %collective-permute-start = (bf16[256,1152]{1,0:T(8,128)(2,1)}, bf16[256,1152]{1,0:T(8,128)(2,1)}, u32[]{:S(2)}, u32[]{:S(2)}) collective-permute-start(bf16[256,1152]{1,0:T(8,128)(2,1)} %param.13), channel_id=1, source_target_pairs={{0,1},{1,0},{2,3},{3,2},{4,5},{5,4},{6,7},{7,6},{8,9},{9,8},{10,11... | collective-permute-start | bytes 1769480 | tf_op jit(solution)/shard_map/ppermute | solution.py:51
  14.8 260.5 %collective-permute-start.8 = (bf16[256,1152]{1,0:T(8,128)(2,1)}, bf16[256,1152]{1,0:T(8,128)(2,1)}, u32[]{:S(2)}, u32[]{:S(2)}) collective-permute-start(bf16[256,1152]{1,0:T(8,128)(2,1)} %param.25), channel_id=1, source_target_pairs={{0,1},{1,0},{2,3},{3,2},{4,5},{5,4},{6,7},{7,6},{8,9},{9,8},{10,11... | collective-permute-start | bytes 1769480 | tf_op jit(solution)/shard_map/ppermute | solution.py:51
  14.9 663.0 %reduce-scatter.5.cloned.1.call-start = ((), (), s32[]{:S(2)}) async-start(), calls=%async_computation.7 | async-start | bytes 7520256 | tf_op jit(solution)/shard_map/reduce_scatter | solution.py:1086
  16.2 163.6 %copy-start.148 = (s32[1,256]{1,0:T(1,128)}, s32[1,256]{1,0:T(1,128)S(1)}, u32[]{:S(2)}) copy-start(s32[1,256]{1,0:T(1,128)S(1)} %get-tuple-element.290) | copy-start | bytes 3076
  19.0 134.8 %copy-start.173 = (bf16[2,1728]{1,0:T(2,128)(2,1)S(1)}, bf16[2,1728]{1,0:T(2,128)(2,1)}, u32[]{:S(2)}) copy-start(bf16[2,1728]{1,0:T(2,128)(2,1)} %param.21) | copy-start | bytes 20740
  178.0 14.2 %collective-permute-start.1 = (bf16[256,1152]{1,0:T(8,128)(2,1)S(1)}, bf16[256,1152]{1,0:T(8,128)(2,1)S(1)}, u32[]{:S(2)}, u32[]{:S(2)}) collective-permute-start(bf16[256,1152]{1,0:T(8,128)(2,1)S(1)} %convolution_convert_fusion.8), channel_id=1, source_target_pairs={{0,1},{1,0},{2,3},{3,2},{4,5},{5,4},{6,7},{7,6},{8,9},{9,8},{10,11... | collective-permute-start | bytes 1769480 | tf_op jit(solution)/shard_map/ppermute | solution.py:51
  179.8 62.0 %copy-start.125 = (pred[256]{0:T(512)(128)(4,1)}, pred[256]{0:T(512)(128)(4,1)S(1)}, u32[]{:S(2)}) copy-start(pred[256]{0:T(512)(128)(4,1)S(1)} %get-tuple-element.293) | copy-start | bytes 772
  179.8 62.0 %copy-start.127 = (pred[256]{0:T(512)(128)(4,1)}, pred[256]{0:T(512)(128)(4,1)S(1)}, u32[]{:S(2)}) copy-start(pred[256]{0:T(512)(128)(4,1)S(1)} %get-tuple-element.294) | copy-start | bytes 772
  179.8 62.0 %copy-start.132 = (pred[256]{0:T(512)(128)(4,1)}, pred[256]{0:T(512)(128)(4,1)S(1)}, u32[]{:S(2)}) copy-start(pred[256]{0:T(512)(128)(4,1)S(1)} %get-tuple-element.295) | copy-start | bytes 772
  198.2 13.7 %collective-permute-start.2 = (bf16[256,1152]{1,0:T(8,128)(2,1)S(1)}, bf16[256,1152]{1,0:T(8,128)(2,1)}, u32[]{:S(2)}, u32[]{:S(2)}) collective-permute-start(bf16[256,1152]{1,0:T(8,128)(2,1)S(1)} %get-tuple-element.181), channel_id=1, source_target_pairs={{0,1},{1,0},{2,3},{3,2},{4,5},{5,4},{6,7},{7,6},{8,9},{9,8},{10,11... | collective-permute-start | bytes 1769480 | tf_op jit(solution)/shard_map/ppermute | solution.py:51
  202.9 38.9 %copy-start.106 = (f32[1152]{0:T(1024)}, f32[1152]{0:T(1024)S(1)}, u32[]{:S(2)}) copy-start(f32[1152]{0:T(1024)S(1)} %get-tuple-element.136) | copy-start | bytes 13828
  202.9 38.9 %copy-start.108 = (f32[1152]{0:T(1024)}, f32[1152]{0:T(1024)S(1)}, u32[]{:S(2)}) copy-start(f32[1152]{0:T(1024)S(1)} %get-tuple-element.137) | copy-start | bytes 13828
  202.9 38.9 %copy-start.110 = (f32[1152]{0:T(1024)}, f32[1152]{0:T(1024)S(1)}, u32[]{:S(2)}) copy-start(f32[1152]{0:T(1024)S(1)} %get-tuple-element.138) | copy-start | bytes 13828
  226.8 13.1 %collective-permute-start.3 = (bf16[256,1152]{1,0:T(8,128)(2,1)S(1)}, bf16[256,1152]{1,0:T(8,128)(2,1)S(1)}, u32[]{:S(2)}, u32[]{:S(2)}) collective-permute-start(bf16[256,1152]{1,0:T(8,128)(2,1)S(1)} %convolution_convert_fusion.3), channel_id=1, source_target_pairs={{0,1},{1,0},{2,3},{3,2},{4,5},{5,4},{6,7},{7,6},{8,9},{9,8},{10,11... | collective-permute-start | bytes 1769480 | tf_op jit(solution)/shard_map/ppermute | solution.py:51
  244.0 12.2 %collective-permute-start.4 = (bf16[256,1152]{1,0:T(8,128)(2,1)S(1)}, bf16[256,1152]{1,0:T(8,128)(2,1)S(1)}, u32[]{:S(2)}, u32[]{:S(2)}) collective-permute-start(bf16[256,1152]{1,0:T(8,128)(2,1)S(1)} %add_convert_fusion.3), channel_id=1, source_target_pairs={{0,1},{1,0},{2,3},{3,2},{4,5},{5,4},{6,7},{7,6},{8,9},{9,8},{10,11... | collective-permute-start | bytes 1769480 | tf_op jit(solution)/shard_map/ppermute | solution.py:51
  247.4 39.5 %copy-start.116 = (f32[1152]{0:T(1024)}, f32[1152]{0:T(1024)S(1)}, u32[]{:S(2)}) copy-start(f32[1152]{0:T(1024)S(1)} %get-tuple-element.123) | copy-start | bytes 13828
  247.4 39.5 %copy-start.118 = (f32[1152]{0:T(1024)}, f32[1152]{0:T(1024)S(1)}, u32[]{:S(2)}) copy-start(f32[1152]{0:T(1024)S(1)} %get-tuple-element.124) | copy-start | bytes 13828
  272.6 11.4 %collective-permute-start.5 = (bf16[256,1152]{1,0:T(8,128)(2,1)}, bf16[256,1152]{1,0:T(8,128)(2,1)S(1)}, u32[]{:S(2)}, u32[]{:S(2)}) collective-permute-start(bf16[256,1152]{1,0:T(8,128)(2,1)} %convolution_convert_fusion.7), channel_id=1, source_target_pairs={{0,1},{1,0},{2,3},{3,2},{4,5},{5,4},{6,7},{7,6},{8,9},{9,8},{10,11... | collective-permute-start | bytes 1769480 | tf_op jit(solution)/shard_map/ppermute | solution.py:51
  290.5 10.6 %collective-permute-start.6 = (bf16[256,1152]{1,0:T(8,128)(2,1)}, bf16[256,1152]{1,0:T(8,128)(2,1)}, u32[]{:S(2)}, u32[]{:S(2)}) collective-permute-start(bf16[256,1152]{1,0:T(8,128)(2,1)} %add_convert_fusion.2), channel_id=1, source_target_pairs={{0,1},{1,0},{2,3},{3,2},{4,5},{5,4},{6,7},{7,6},{8,9},{9,8},{10,11... | collective-permute-start | bytes 1769480 | tf_op jit(solution)/shard_map/ppermute | solution.py:51
  321.2 37.9 %collective-permute-start.7 = (bf16[256,1152]{1,0:T(8,128)(2,1)}, bf16[256,1152]{1,0:T(8,128)(2,1)}, u32[]{:S(2)}, u32[]{:S(2)}) collective-permute-start(bf16[256,1152]{1,0:T(8,128)(2,1)} %convolution_convert_fusion.2), channel_id=1, source_target_pairs={{0,1},{1,0},{2,3},{3,2},{4,5},{5,4},{6,7},{7,6},{8,9},{9,8},{10,11... | collective-permute-start | bytes 1769480 | tf_op jit(solution)/shard_map/ppermute | solution.py:51
  336.3 9.9 %collective-permute-start.9 = (bf16[256,1152]{1,0:T(8,128)(2,1)S(1)}, bf16[256,1152]{1,0:T(8,128)(2,1)S(1)}, u32[]{:S(2)}, u32[]{:S(2)}) collective-permute-start(bf16[256,1152]{1,0:T(8,128)(2,1)S(1)} %convolution_convert_fusion.6), channel_id=1, source_target_pairs={{0,1},{1,0},{2,3},{3,2},{4,5},{5,4},{6,7},{7,6},{8,9},{9,8},{10,11... | collective-permute-start | bytes 1769480 | tf_op jit(solution)/shard_map/ppermute | solution.py:51
  350.8 10.3 %collective-permute-start.10 = (bf16[256,1152]{1,0:T(8,128)(2,1)}, bf16[256,1152]{1,0:T(8,128)(2,1)}, u32[]{:S(2)}, u32[]{:S(2)}) collective-permute-start(bf16[256,1152]{1,0:T(8,128)(2,1)} %get-tuple-element.174), channel_id=1, source_target_pairs={{0,1},{1,0},{2,3},{3,2},{4,5},{5,4},{6,7},{7,6},{8,9},{9,8},{10,11... | collective-permute-start | bytes 1769480 | tf_op jit(solution)/shard_map/ppermute | solution.py:51
  359.2 320.1 %reduce-scatter.3.cloned.1.call-start = ((), (), s32[]{:S(2)}) async-start(), calls=%async_computation.6 | async-start | bytes 7520256 | tf_op jit(solution)/shard_map/reduce_scatter | solution.py:1086
  392.5 9.9 %collective-permute-start.11 = (bf16[256,1152]{1,0:T(8,128)(2,1)S(1)}, bf16[256,1152]{1,0:T(8,128)(2,1)S(1)}, u32[]{:S(2)}, u32[]{:S(2)}) collective-permute-start(bf16[256,1152]{1,0:T(8,128)(2,1)S(1)} %convolution_convert_fusion.5), channel_id=1, source_target_pairs={{0,1},{1,0},{2,3},{3,2},{4,5},{5,4},{6,7},{7,6},{8,9},{9,8},{10,11... | collective-permute-start | bytes 1769480 | tf_op jit(solution)/shard_map/ppermute | solution.py:51
  530.9 23.2 %collective-permute-start.12 = (bf16[256,1152]{1,0:T(8,128)(2,1)}, bf16[256,1152]{1,0:T(8,128)(2,1)S(1)}, u32[]{:S(2)}, u32[]{:S(2)}) collective-permute-start(bf16[256,1152]{1,0:T(8,128)(2,1)} %convolution_convert_fusion.4), channel_id=1, source_target_pairs={{0,1},{1,0},{2,3},{3,2},{4,5},{5,4},{6,7},{7,6},{8,9},{9,8},{10,11... | collective-permute-start | bytes 1769480 | tf_op jit(solution)/shard_map/ppermute | solution.py:51
  565.4 4.8 collective-permute-start.13
  570.9 102.1 %copy-start.97 = (f32[72,576]{1,0:T(8,128)S(1)}, f32[72,576]{1,0:T(8,128)}, u32[]{:S(2)}) copy-start(f32[72,576]{1,0:T(8,128)} %get-tuple-element.107) | copy-start | bytes 497668
  570.9 103.9 %copy-start.90 = (f32[72,1536]{1,0:T(8,128)S(1)}, f32[72,1536]{1,0:T(8,128)}, u32[]{:S(2)}) copy-start(f32[72,1536]{1,0:T(8,128)} %get-tuple-element.111) | copy-start | bytes 1327108
  (207 other events, 867.4 us)
Sparse Core Ops, SparseCore 0:
  10.9 102.5 all-gather.4
  116.3 47.8 all-gather.6
  166.5 65.9 all-gather.8
  234.6 45.6 all-gather.10
  359.3 124.6 reduce-scatter.4
  525.5 123.2 reduce-scatter.2

commit v5 on v4

--- a/solution.py
+++ b/solution.py
@@ -450,137 +450,6 @@
     )(cond, ada, bias, *shards)
 
 
-def finish_kernel(row_size, head_size, images, blocks, count, *refs):
-    small, mine, ada, factor = refs[:4]
-    ins = refs[4 : 4 + count]
-    ada_out, ada_bias_out, qkv_bias_out, cond_out = refs[4 + count : 8 + count]
-    outs = refs[8 + count : 8 + 2 * count]
-    refs = refs[8 + 2 * count :]
-    scratch = refs[: 4 * count]
-    refs = refs[4 * count :]
-    every, part, held, met, side, far, total, landed = refs[:8]
-    send, recv, load, small_send, small_recv, small_keep = refs[8:14]
-    cond_send, cond_recv, cond_load, head_send, head_recv = refs[14:]
-    place = Place(row_size, head_size)
-    place.greet(True)
-    lead = Gather(place, small, every, small_send, small_recv, small_keep.at[0])
-    lead.begin()
-    items = [
-        Scatter(
-            place, ins[i], outs[i], *scratch[4 * i : 4 * i + 4], send.at[i], recv.at[i], load.at[i]
-        )
-        for i in range(count)
-    ]
-    for item in items:
-        item.begin()
-    hops = range(1, place.sizes[0])
-    for k in hops:
-        lead.first(k)
-    for item in items:
-        item.first()
-    lead.second()
-    items[0].second()
-    lead.finish()
-    rows = small.shape[0]
-    share, width = ada.shape[1], cond_out.shape[1]
-    grads = every[...].reshape(row_size * rows, -1)
-    columns = qkv_bias_out.shape[1]
-    for b in range(blocks):
-        value = dot_tn(mine[b], grads)
-        ada_out[b] = value[:share]
-        ada_bias_out[b : b + 1, :] = value[share : share + 1]
-        qkv_bias_out[b : b + 1, :] = value[share + 1 : share + 2, :columns]
-    lane = lax.broadcasted_iota(jnp.int32, (share, width), 1)
-    slot = lax.broadcasted_iota(jnp.int32, (share, width), 0)
-    pick = jnp.where(lane == lax.axis_index("rows") * share + slot, 1.0, 0.0).astype(jnp.bfloat16)
-    back = 0.0
-    for b in range(blocks):
-        value = dot_nt(grads, ada[b]).reshape(row_size, rows, share)
-        back = back + value[:, b * images : (b + 1) * images]
-    pad = part.shape[1]
-    back = back.reshape(row_size * images, share).astype(jnp.bfloat16)
-    part[...] = jnp.zeros_like(part)
-    part[:, :images, :] = dot_nn(back, pick).reshape(row_size, images, width)
-    sums = Scatter(place, part, total, held, met, side, far, cond_send, cond_recv, cond_load)
-    sums.begin()
-    sums.first()
-    for item in items[1:2]:
-        item.second()
-    sums.second()
-    for item in items[2:]:
-        item.second()
-    sums.finish()
-    across = Across(
-        place, lambda by: total, lambda by: landed.at[by - 1], head_send, head_recv, 0
-    )
-    for by in range(1, head_size):
-        across.start(by)
-    for item in items:
-        item.finish()
-    value = total[...]
-    for by in range(1, head_size):
-        across.arrived(by)
-        value = value + landed[by - 1]
-    cond_out[...] = value * factor[...]
-    across.left()
-
-
-def finish_call(row_size, head_size, images, grads, small, mine, ada, factor, columns):
-    count = len(grads)
-    copies = scatter_count(row_size)
-    small_copies = gather_count(row_size)
-    blocks, share, wide = ada.shape
-    a, b = 4, row_size // 8
-    f32 = jnp.float32
-    shape = jax.ShapeDtypeStruct
-    scratch = []
-    for grad in grads:
-        chunk = grad.shape[1:]
-        for lead in ((a, b), (a, b), (b - 1, a), (a - 1,)):
-            scratch.append(pltpu.VMEM(lead + chunk, grad.dtype))
-    chunk = factor.shape
-    anywhere = pl.BlockSpec(memory_space=pl.ANY)
-    vmem = pl.BlockSpec(memory_space=pltpu.VMEM)
-    return pl.pallas_call(
-        functools.partial(finish_kernel, row_size, head_size, images, blocks, count),
-        out_shape=[
-            shape(ada.shape, f32),
-            shape((blocks, wide), f32),
-            shape((blocks, columns), f32),
-            shape(factor.shape, f32),
-        ]
-        + [shape(grad.shape[1:], f32) for grad in grads],
-        in_specs=[anywhere] + [vmem] * 3 + [anywhere] * count,
-        out_specs=[vmem] * (4 + count),
-        scratch_shapes=scratch
-        + [
-            pltpu.VMEM((row_size,) + small.shape, small.dtype),
-            pltpu.VMEM((row_size,) + chunk, f32),
-            pltpu.VMEM((a, b) + chunk, f32),
-            pltpu.VMEM((a, b) + chunk, f32),
-            pltpu.VMEM((b - 1, a) + chunk, f32),
-            pltpu.VMEM((a - 1,) + chunk, f32),
-            pltpu.VMEM(chunk, f32),
-            pltpu.VMEM((head_size - 1,) + chunk, f32),
-            pltpu.SemaphoreType.DMA((count, copies)),
-            pltpu.SemaphoreType.DMA((count, copies)),
-            pltpu.SemaphoreType.DMA((count, a * b)),
-            pltpu.SemaphoreType.DMA((small_copies,)),
-            pltpu.SemaphoreType.DMA((small_copies,)),
-            pltpu.SemaphoreType.DMA((1,)),
-            pltpu.SemaphoreType.DMA((copies,)),
-            pltpu.SemaphoreType.DMA((copies,)),
-            pltpu.SemaphoreType.DMA((a * b,)),
-            pltpu.SemaphoreType.DMA((head_size - 1,)),
-            pltpu.SemaphoreType.DMA((head_size - 1,)),
-        ],
-        compiler_params=pltpu.CompilerParams(
-            collective_id=2, has_side_effects=True, vmem_limit_bytes=56 * 2**20
-        ),
-        name="finish",
-    )(small, mine, ada, factor, *grads)
-
-
 def weight_grads_kernel(*refs):
     count = len(refs) // 3
     for i in range(count):
@@ -659,14 +528,13 @@
 
 
 class Streamed:
-    def __init__(self, buffer, out, sems, size):
-        self.buffer, self.out, self.sems, self.size = buffer, out, sems, size
+    def __init__(self, buffer, out, sems, size, begin=0):
+        self.buffer, self.out, self.sems, self.size, self.begin = buffer, out, sems, size, begin
 
     def copy(self, step):
+        at = pl.multiple_of(self.begin + step * self.size, 128)
         return pltpu.make_async_copy(
-            self.buffer.at[step % 2],
-            self.out.at[:, pl.ds(pl.multiple_of(step * self.size, self.size), self.size)],
-            self.sems.at[step % 2],
+            self.buffer.at[step % 2], self.out.at[:, pl.ds(at, self.size)], self.sems.at[step % 2]
         )
 
     def put(self, step, value):
@@ -682,38 +550,557 @@
             self.copy(step).wait()
 
 
-def mlp_back_kernel(row_size, head_size, count, *refs):
-    (incoming, gate_mlp, scale_mlp, gate_attn, normed, inverse) = refs[:6]
-    streams = refs[6:12]
-    grads = refs[12 : 12 + count]
-    outs = refs[12 + count : 18 + 2 * count]
+def finish_kernel(row_size, head_size, images, blocks, *refs):
+    (packed, qkv, inputs, attended, branch, middle, scale, normed, inverse, owner) = refs[:10]
+    known, bias, mine, ada, factor, down = refs[10:16]
+    grad_tokens, ada_out, ada_bias_out, qkv_bias_out, cond_out = refs[16:21]
+    outs = refs[21:24]
+    parcel, landed, sheet, share_in, small, qkv_grad, proj_grad = refs[24:31]
+    head_send, head_recv = refs[31:33]
+    refs = refs[33:]
+    scratch = refs[:12]
+    every, part, held, met, side, far, total, cond_in = refs[12:20]
+    send, recv, load, small_send, small_recv, small_keep = refs[20:26]
+    cond_send, cond_recv, cond_load = refs[26:]
+    place = Place(row_size, head_size)
+    own, width = middle.shape
+    step_width = tile_of(width)
+    place.greet(True)
+    items = [
+        Scatter(
+            place, source, outs[i], *scratch[4 * i : 4 * i + 4], send.at[i], recv.at[i], load.at[i]
+        )
+        for i, source in enumerate((down, qkv_grad, proj_grad))
+    ]
+    items[0].begin()
+    first = Across(
+        place, lambda by: parcel.at[by - 1], lambda by: landed.at[by - 1], head_send, head_recv, 0
+    )
+    for by in range(1, head_size):
+
+        def body(step, at):
+            parcel[by - 1, :, pl.ds(at, step_width)] = dot_nt(
+                packed[pl.ds(by * own, own), :], qkv[pl.ds(at, step_width), :]
+            ).astype(jnp.bfloat16)
+
+        tiles(width, step_width, body)
+        first.start(by)
+    for left, right, out, item in (
+        (inputs, packed, qkv_grad, items[1]),
+        (branch, attended, proj_grad, items[2]),
+    ):
+        share = out.shape[1]
+        for at in range(0, out.shape[2], 256):
+            size = min(256, out.shape[2] - at)
+            value = dot_tn(left[...], right[:, at : at + size])
+            for row in range(row_size):
+                out[row, :, at : at + size] = value[row * share : (row + 1) * share].astype(out.dtype)
+        item.begin()
+    items[0].first()
+    value = dot_nt(packed[pl.ds(0, own), :], qkv[...])
+    for by in range(1, head_size):
+        first.arrived(by)
+        value = value + landed[by - 1].astype(jnp.float32)
+    scaled = value * (1.0 + scale[...])
+    grad_tokens[...] = middle[...] + inverse[...] * (
+        scaled
+        - jnp.mean(scaled, axis=-1, keepdims=True)
+        - normed[...] * jnp.mean(scaled * normed[...], axis=-1, keepdims=True)
+    )
+    sheet[...] = known[...]
+    wide = sheet.shape[2]
+    for image in range(images):
+        here = owner[...] == image
+        for piece, item in enumerate((value, value * normed[...])):
+            row = jnp.sum(jnp.where(here, item, 0.0), axis=0, keepdims=True)
+            begin = piece * width
+            while begin < (piece + 1) * width:
+                end = min((begin // wide + 1) * wide, (piece + 1) * width)
+                sheet[begin // wide, image : image + 1, begin % wide : begin % wide + end - begin] = (
+                    row[:, begin - piece * width : end - piece * width]
+                )
+                begin = end
+    shares = Across(
+        place,
+        lambda by: sheet.at[place.head ^ by],
+        lambda by: share_in.at[by - 1],
+        head_send,
+        head_recv,
+        1,
+    )
+    for by in range(1, head_size):
+        shares.start(by)
+    mod_grads = sheet[place.head]
+    for by in range(1, head_size):
+        shares.arrived(by)
+        mod_grads = mod_grads + share_in[by - 1]
+    known_rows = mod_grads.shape[0]
+    small[...] = jnp.concatenate([mod_grads, bias[known_rows:, :]], axis=0).astype(small.dtype)
+    lead = Gather(place, small, every, small_send, small_recv, small_keep.at[0])
+    lead.begin()
+    for k in range(1, place.sizes[0]):
+        lead.first(k)
+    items[1].first()
+    items[0].second()
+    lead.second()
+    lead.finish()
+    rows = small.shape[0]
+    share = ada.shape[1]
+    grads = every[...].reshape(row_size * rows, -1)
+    columns = qkv_bias_out.shape[1]
+    for b in range(blocks):
+        value = dot_tn(mine[b], grads)
+        ada_out[b] = value[:share]
+        ada_bias_out[b : b + 1, :] = value[share : share + 1]
+        qkv_bias_out[b : b + 1, :] = value[share + 1 : share + 2, :columns]
+    lane = lax.broadcasted_iota(jnp.int32, (share, width), 1)
+    slot = lax.broadcasted_iota(jnp.int32, (share, width), 0)
+    pick = jnp.where(lane == lax.axis_index("rows") * share + slot, 1.0, 0.0).astype(jnp.bfloat16)
+    back = 0.0
+    for b in range(blocks):
+        value = dot_nt(grads, ada[b]).reshape(row_size, rows, share)
+        back = back + value[:, b * images : (b + 1) * images]
+    back = back.reshape(row_size * images, share).astype(jnp.bfloat16)
+    part[...] = jnp.zeros_like(part)
+    part[:, :images, :] = dot_nn(back, pick).reshape(row_size, images, width)
+    sums = Scatter(place, part, total, held, met, side, far, cond_send, cond_recv, cond_load)
+    sums.begin()
+    sums.first()
+    items[2].first()
+    items[1].second()
+    sums.second()
+    items[2].second()
+    sums.finish()
+    last = Across(
+        place, lambda by: total, lambda by: cond_in.at[by - 1], head_send, head_recv, 2
+    )
+    for by in range(1, head_size):
+        last.start(by)
+    for item in items:
+        item.finish()
+    value = total[...]
+    for by in range(1, head_size):
+        last.arrived(by)
+        value = value + cond_in[by - 1]
+    cond_out[...] = value * factor[...]
+    for stage in (first, shares, last):
+        stage.left()
+
+
+def finish_call(row_size, head_size, images, near, known, bias, mine, ada, factor, down):
+    packed, qkv, inputs, attended, branch, middle = near[:6]
+    copies = scatter_count(row_size)
+    small_copies = gather_count(row_size)
+    blocks, share, wide = ada.shape
+    own, width = middle.shape
+    a, b = 4, row_size // 8
+    f32, bf16 = jnp.float32, jnp.bfloat16
+    shape = jax.ShapeDtypeStruct
+    chunks = [(share, columns) for columns in (down.shape[2], qkv.shape[1], attended.shape[1])]
+    scratch = []
+    for chunk in chunks:
+        for lead in ((a, b), (a, b), (b - 1, a), (a - 1,)):
+            scratch.append(pltpu.VMEM(lead + chunk, bf16))
+    chunk = factor.shape
+    anywhere = pl.BlockSpec(memory_space=pl.ANY)
+    vmem = pl.BlockSpec(memory_space=pltpu.VMEM)
+    others = head_size - 1
+    return pl.pallas_call(
+        functools.partial(finish_kernel, row_size, head_size, images, blocks),
+        out_shape=[
+            shape((own, width), f32),
+            shape(ada.shape, f32),
+            shape((blocks, wide), f32),
+            shape((blocks, qkv.shape[1]), f32),
+            shape(factor.shape, f32),
+        ]
+        + [shape(item, f32) for item in chunks],
+        in_specs=[vmem] * 15 + [anywhere],
+        out_specs=[vmem] * 8,
+        scratch_shapes=[
+            pltpu.VMEM((others, own, width), bf16),
+            pltpu.VMEM((others, own, width), bf16),
+            pltpu.VMEM(known.shape, f32),
+            pltpu.VMEM((others,) + known.shape[1:], f32),
+            pltpu.VMEM(bias.shape, bf16),
+            pltpu.VMEM((row_size,) + chunks[1], bf16),
+            pltpu.VMEM((row_size,) + chunks[2], bf16),
+            pltpu.SemaphoreType.DMA((3 * others,)),
+            pltpu.SemaphoreType.DMA((3 * others,)),
+        ]
+        + scratch
+        + [
+            pltpu.VMEM((row_size,) + bias.shape, bf16),
+            pltpu.VMEM((row_size,) + chunk, f32),
+            pltpu.VMEM((a, b) + chunk, f32),
+            pltpu.VMEM((a, b) + chunk, f32),
+            pltpu.VMEM((b - 1, a) + chunk, f32),
+            pltpu.VMEM((a - 1,) + chunk, f32),
+            pltpu.VMEM(chunk, f32),
+            pltpu.VMEM((others,) + chunk, f32),
+            pltpu.SemaphoreType.DMA((3, copies)),
+            pltpu.SemaphoreType.DMA((3, copies)),
+            pltpu.SemaphoreType.DMA((3, a * b)),
+            pltpu.SemaphoreType.DMA((small_copies,)),
+            pltpu.SemaphoreType.DMA((small_copies,)),
+            pltpu.SemaphoreType.DMA((1,)),
+            pltpu.SemaphoreType.DMA((copies,)),
+            pltpu.SemaphoreType.DMA((copies,)),
+            pltpu.SemaphoreType.DMA((a * b,)),
+        ],
+        compiler_params=pltpu.CompilerParams(
+            collective_id=2, has_side_effects=True, vmem_limit_bytes=60 * 2**20
+        ),
+        name="finish",
+    )(*near, known, bias, mine, ada, factor, down)
+
+
+class Pieces:
+    def __init__(self, place, pieces, source, target, send, recv, stage):
+        self.copies = {}
+        for by in range(1, place.heads):
+            for piece in range(pieces):
+                slot = (stage * (place.heads - 1) + by - 1) * pieces + piece
+                self.copies[by, piece] = pltpu.make_async_remote_copy(
+                    src_ref=source(by, piece),
+                    dst_ref=target(by, piece),
+                    send_sem=send.at[slot],
+                    recv_sem=recv.at[slot],
+                    device_id=place.flip(by),
+                    device_id_type=MESH,
+                )
+
+    def start(self, by, piece):
+        self.copies[by, piece].start()
+
+    def arrived(self, by, piece):
+        self.copies[by, piece].wait_recv()
+
+    def left(self):
+        for key in self.copies:
+            self.copies[key].wait_send()
+
+
+class Mlp:
+    def __init__(self, place, pieces, own, width, units, sends, recvs):
+        self.place, self.pieces, self.own, self.width, self.units = place, pieces, own, width, units
+        self.sends, self.recvs = sends, recvs
+        self.rows = own // pieces
+        self.others = [(by, p) for p in range(pieces) for by in range(1, place.heads)]
+
+    def at(self, piece):
+        return pl.ds(piece * self.rows, self.rows)
+
+    def flat(self, by, piece):
+        return pl.ds(by * self.own + piece * self.rows, self.rows)
+
+    def sum_stage(self, parcel, landed, stage):
+        return Pieces(
+            self.place,
+            self.pieces,
+            lambda by, p: parcel.at[by - 1, self.at(p)],
+            lambda by, p: landed.at[by - 1, self.at(p)],
+            self.sends,
+            self.recvs,
+            stage,
+        )
+
+    def spread_stage(self, every, stage):
+        return Pieces(
+            self.place,
+            self.pieces,
+            lambda by, p: every.at[0, self.at(p)],
+            lambda by, p: every.at[by, self.at(p)],
+            self.sends,
+            self.recvs,
+            stage,
+        )
+
+    def send_all(self, stage, piece):
+        for by in range(1, self.place.heads):
+            stage.start(by, piece)
+
+    def arrive_all(self, stage, piece):
+        for by in range(1, self.place.heads):
+            stage.arrived(by, piece)
+
+    def total(self, own_part, landed, piece):
+        value = own_part[self.at(piece)]
+        for by in range(1, self.place.heads):
+            value = value + landed[by - 1, self.at(piece)].astype(jnp.float32)
+        return value
+
+    def modulation(self, table, owner, index, piece):
+        here = owner[self.at(piece)]
+        total = jnp.zeros((self.rows, self.width), jnp.float32)
+        for image in range(table.shape[0]):
+            row = table[image : image + 1, index * self.width : (index + 1) * self.width]
+            total = jnp.where(here == image, row, total)
+        return total
+
+    def partial(self, out, left, rows, right):
+        size = tile_of(self.width)
+
+        def body(step, at):
+            out[:, pl.ds(at, size)] = dot_nt(left[rows, :], right[pl.ds(at, size), :]).astype(out.dtype)
+
+        tiles(self.width, size, body)
+
+    def front(self, attended, proj, residual, table, owner, parcel, landed, own_part, branch, middle, normed, inverse, inputs, tick=None):
+        first = self.sum_stage(parcel, landed, 0)
+        for by, p in self.others:
+            parcel[by - 1, self.at(p)] = dot_nt(attended[self.flat(by, p), :], proj[...]).astype(
+                jnp.bfloat16
+            )
+            first.start(by, p)
+        own_part[...] = dot_nt(attended[pl.ds(0, self.own), :], proj[...])
+        if tick:
+            tick()
+        second = self.spread_stage(inputs, 1)
+        for p in range(self.pieces):
+            at = self.at(p)
+            self.arrive_all(first, p)
+            value = self.total(own_part, landed, p)
+            branch[at] = value
+            value = residual[at] + self.modulation(table, owner, 2, p) * value
+            middle[at] = value
+            unit, scale = normalize(value)
+            normed[at] = unit
+            inverse[at] = scale
+            inputs[0, at] = (
+                unit * (1.0 + self.modulation(table, owner, 4, p))
+                + self.modulation(table, owner, 3, p)
+            ).astype(jnp.bfloat16)
+            self.send_all(second, p)
+        return first, second
+
+    def gate_up(self, inputs, gu, out, hidden, by, begin, rows):
+        flat = pl.ds(by * self.own + begin, rows)
+        size = tile_of(self.units)
+
+        def body(step, at):
+            far = pl.ds(pl.multiple_of(self.units + at, 128), size)
+            value = inputs[by, pl.ds(begin, rows)]
+            gate = dot_nn(value, gu[:, pl.ds(at, size)])
+            up = dot_nn(value, gu[:, far])
+            out[flat, pl.ds(at, size)] = gate
+            out[flat, far] = up
+            hidden[flat, pl.ds(at, size)] = (jax.nn.silu(gate) * up).astype(jnp.bfloat16)
+
+        tiles(self.units, size, body)
+
+    def hidden_back(self, grads, down, gate_up, ggu, by, begin, rows):
+        flat = pl.ds(by * self.own + begin, rows)
+        size = tile_of(self.units)
+
+        def body(step, at):
+            far = pl.ds(pl.multiple_of(self.units + at, 128), size)
+            gate = gate_up[flat, pl.ds(at, size)]
+            up = gate_up[flat, far]
+            grad = dot_nn(grads[by, pl.ds(begin, rows)], down[:, pl.ds(at, size)])
+            logistic = jax.nn.sigmoid(gate)
+            ggu[flat, pl.ds(at, size)] = (
+                grad * up * logistic * (1.0 + gate * (1.0 - logistic))
+            ).astype(jnp.bfloat16)
+            ggu[flat, far] = (grad * gate * logistic).astype(jnp.bfloat16)
+
+        tiles(self.units, size, body)
+
+
+def mlp_kernel(row_size, head_size, pieces, count, *refs):
+    attended, residual, owner, table, following = refs[:5]
+    streams, shards = refs[5:8], refs[8 : 8 + count]
+    refs = refs[8 + count :]
+    kept_out, refs = refs[:5], refs[5:]
+    inverse, mlp_out, result, next_normed, next_inverse, next_out = refs[:6]
+    gathered, refs = refs[6 : 6 + count], refs[6 + count :]
+    weights, kept = refs[:3], refs[3:8]
+    proj, gu, down = weights
+    branch, normed, inputs, gate_up, hidden = kept
+    parcel, landed, middle, own_part, next_all = refs[8:13]
+    loads, stores, sends, recvs, gather_send, gather_recv, gather_keep = refs[13:]
+    place = Place(row_size, head_size)
+    own, width = residual.shape
+    units = hidden.shape[1]
+    work = Mlp(place, pieces, own, width, units, sends, recvs)
+    copies = [
+        pltpu.make_async_copy(source, target, loads.at[i])
+        for i, (source, target) in enumerate(zip(streams, weights))
+    ]
+    out_copies = [
+        pltpu.make_async_copy(source, target, stores.at[i])
+        for i, (source, target) in enumerate(zip(kept, kept_out))
+    ]
+    items = [
+        Gather(place, shards[i], gathered[i], gather_send.at[i], gather_recv.at[i], gather_keep.at[i])
+        for i in range(count)
+    ]
+    for copy in copies:
+        copy.start()
+    place.greet(True)
+    for item in items:
+        item.begin()
+
+    def hop(k):
+        for item in items:
+            item.first(k)
+
+    copies[0].wait()
+    first, second = work.front(
+        attended,
+        proj,
+        residual,
+        table,
+        owner,
+        parcel.at[0],
+        landed.at[0],
+        own_part,
+        branch,
+        middle,
+        normed,
+        inverse,
+        inputs,
+        lambda: hop(1),
+    )
+    hop(2)
+    out_copies[0].start()
+    out_copies[1].start()
+    copies[1].wait()
+    work.gate_up(inputs, gu, gate_up, hidden, 0, 0, own)
+    for k in range(3, place.sizes[0]):
+        hop(k)
+    copies[2].wait()
+    third = work.sum_stage(parcel.at[1], landed.at[1], 2)
+    for by, p in work.others:
+        second.arrived(by, p)
+        work.gate_up(inputs, gu, gate_up, hidden, by, p * work.rows, work.rows)
+        work.partial(parcel.at[1, by - 1, work.at(p)], hidden, work.flat(by, p), down)
+        third.start(by, p)
+    for copy in out_copies[2:]:
+        copy.start()
+    work.partial(own_part, hidden, pl.ds(0, own), down)
+    for item in items:
+        item.second()
+    fourth = work.spread_stage(next_all, 3)
+    for p in range(pieces):
+        at = work.at(p)
+        work.arrive_all(third, p)
+        value = work.total(own_part, landed.at[1], p)
+        mlp_out[at] = value
+        value = middle[at] + work.modulation(table, owner, 5, p) * value
+        result[at] = value
+        unit, scale = normalize(value)
+        next_normed[at] = unit
+        next_inverse[at] = scale
+        next_all[0, at] = (
+            unit * (1.0 + work.modulation(following, owner, 1, p))
+            + work.modulation(following, owner, 0, p)
+        ).astype(jnp.bfloat16)
+        work.send_all(fourth, p)
+    next_out[0] = next_all[0]
+    for by, p in work.others:
+        fourth.arrived(by, p)
+        next_out[by, work.at(p)] = next_all[by, work.at(p)]
+    for item in items:
+        item.finish()
+    for stage in (first, second, third, fourth):
+        stage.left()
+    for copy in out_copies:
+        copy.wait()
+
+
+def pieces_of(own):
+    return 2 if own % 32 == 0 else 1
+
+
+def mlp_call(row_size, head_size, attended, residual, owner, table, following, weights, shards):
+    own, width = residual.shape
+    tokens = attended.shape[0]
+    units = weights[2].shape[1]
+    count = len(shards)
+    pieces = pieces_of(own)
+    others = head_size - 1
+    copies = gather_count(row_size)
+    anywhere = pl.BlockSpec(memory_space=pl.ANY)
+    vmem = pl.BlockSpec(memory_space=pltpu.VMEM)
+    shape = jax.ShapeDtypeStruct
+    f32, bf16 = jnp.float32, jnp.bfloat16
+    kept = [
+        shape((own, width), f32),
+        shape((own, width), f32),
+        shape((head_size, own, width), bf16),
+        shape((tokens, 2 * units), f32),
+        shape((tokens, units), bf16),
+    ]
+    return pl.pallas_call(
+        functools.partial(mlp_kernel, row_size, head_size, pieces, count),
+        out_shape=kept
+        + [
+            shape((own, 1), f32),
+            shape((own, width), f32),
+            shape((own, width), f32),
+            shape((own, width), f32),
+            shape((own, 1), f32),
+            shape((head_size, own, width), bf16),
+        ]
+        + [shape((row_size,) + item.shape, item.dtype) for item in shards],
+        in_specs=[vmem] * 5 + [anywhere] * (3 + count),
+        out_specs=[anywhere] * 5 + [vmem] * 6 + [anywhere] * count,
+        scratch_shapes=[pltpu.VMEM(item.shape, item.dtype) for item in weights]
+        + [pltpu.VMEM(item.shape, item.dtype) for item in kept]
+        + [
+            pltpu.VMEM((2, others, own, width), bf16),
+            pltpu.VMEM((2, others, own, width), bf16),
+            pltpu.VMEM((own, width), f32),
+            pltpu.VMEM((own, width), f32),
+            pltpu.VMEM((head_size, own, width), bf16),
+            pltpu.SemaphoreType.DMA((3,)),
+            pltpu.SemaphoreType.DMA((5,)),
+            pltpu.SemaphoreType.DMA((4 * others * pieces,)),
+            pltpu.SemaphoreType.DMA((4 * others * pieces,)),
+            pltpu.SemaphoreType.DMA((count, copies)),
+            pltpu.SemaphoreType.DMA((count, copies)),
+            pltpu.SemaphoreType.DMA((count,)),
+        ],
+        compiler_params=pltpu.CompilerParams(
+            collective_id=4, has_side_effects=True, vmem_limit_bytes=60 * 2**20
+        ),
+        name="mlp",
+    )(attended, residual, owner, table, following, *weights, *shards)
+
+
+def mlp_back_kernel(row_size, head_size, pieces, count, *refs):
+    incoming, owner, table, normed, inverse = refs[:5]
+    streams = refs[5:11]
+    grads = refs[11 : 11 + count]
+    outs = refs[11 + count : 17 + 2 * count]
     grad_in, grad_mid, branch_out, grad_att, gu_out, down_out = outs[:6]
     sums = outs[6:]
-    refs = refs[18 + 2 * count :]
+    refs = refs[17 + 2 * count :]
     down, gate_up, gu, inputs, hidden, proj = refs[:6]
     mlp_all, branch_all, ggu, parcel, landed, own_part, buffer = refs[6:13]
     loads, sends, recvs, tile_sems, out_sem = refs[13:18]
     scratch = refs[18 : 18 + 4 * count]
     sum_send, sum_recv, sum_load = refs[18 + 4 * count :]
     place = Place(row_size, head_size)
-    heads = head_size
     own, width = incoming.shape
     units = hidden.shape[1]
+    work = Mlp(place, pieces, own, width, units, sends, recvs)
     step_units = tile_of(units)
-    step_width = tile_of(width)
     copies = [
         pltpu.make_async_copy(source, target, loads.at[i])
         for i, (source, target) in enumerate(
             zip(streams, (down, gate_up, gu, inputs, hidden, proj))
         )
     ]
-    place.greet(True)
-    mlp_all[0] = (gate_mlp[...] * incoming[...]).astype(jnp.bfloat16)
-    first = Across(place, lambda by: mlp_all.at[0], lambda by: mlp_all.at[by], sends, recvs, 0)
-    for by in range(1, heads):
-        first.start(by)
     for copy in copies:
         copy.start()
+    place.greet(True)
+    first = work.spread_stage(mlp_all, 0)
+    for p in range(pieces):
+        at = work.at(p)
+        mlp_all[0, at] = (work.modulation(table, owner, 5, p) * incoming[at]).astype(jnp.bfloat16)
+        work.send_all(first, p)
     items = [
         Scatter(
             place,
@@ -728,77 +1115,44 @@
     ]
     for item in items:
         item.begin()
-
-    def hidden_back(slot):
-        rows = pl.ds(slot * own, own)
-
-        def body(step, at):
-            gate = gate_up[rows, pl.ds(at, step_units)]
-            up = gate_up[rows, pl.ds(pl.multiple_of(units + at, 128), step_units)]
-            grad = dot_nn(mlp_all[slot], down[:, pl.ds(at, step_units)])
-            logistic = jax.nn.sigmoid(gate)
-            ggu[rows, pl.ds(at, step_units)] = (
-                grad * up * logistic * (1.0 + gate * (1.0 - logistic))
-            ).astype(jnp.bfloat16)
-            ggu[rows, pl.ds(pl.multiple_of(units + at, 128), step_units)] = (
-                grad * gate * logistic
-            ).astype(jnp.bfloat16)
-
-        tiles(units, step_units, body)
-
     copies[0].wait()
     copies[1].wait()
-    hidden_back(0)
+    work.hidden_back(mlp_all, down, gate_up, ggu, 0, 0, own)
     for item in items:
         item.first()
-    for by in range(1, heads):
-        first.arrived(by)
-        hidden_back(by)
     copies[2].wait()
-    second = Across(
-        place, lambda by: parcel.at[by - 1], lambda by: landed.at[by - 1], sends, recvs, 1
-    )
-    for by in range(1, heads):
-
-        def body(step, at):
-            parcel[by - 1, :, pl.ds(at, step_width)] = dot_nt(
-                ggu[pl.ds(by * own, own), :], gu[pl.ds(at, step_width), :]
-            ).astype(jnp.bfloat16)
-
-        tiles(width, step_width, body)
-        second.start(by)
+    second = work.sum_stage(parcel, landed, 1)
+    for by, p in work.others:
+        first.arrived(by, p)
+        work.hidden_back(mlp_all, down, gate_up, ggu, by, p * work.rows, work.rows)
+        work.partial(parcel.at[by - 1, work.at(p)], ggu, work.flat(by, p), gu)
+        second.start(by, p)
+    work.partial(own_part, ggu, pl.ds(0, own), gu)
+    copies[3].wait()
+    out = Streamed(buffer, gu_out, tile_sems, step_units)
 
     def body(step, at):
-        own_part[:, pl.ds(at, step_width)] = dot_nt(ggu[pl.ds(0, own), :], gu[pl.ds(at, step_width), :])
-
-    tiles(width, step_width, body)
+        out.put(step, dot_tn(inputs[...], ggu[:, pl.ds(at, step_units)]))
+
+    tiles(2 * units, step_units, body)
     for item in items[:1]:
         item.second()
-    copies[3].wait()
-    out = Streamed(buffer, gu_out, tile_sems, step_units)
-
-    def body(step, at):
-        out.put(step, dot_tn(inputs[...], ggu[:, pl.ds(at, step_units)]))
-
-    tiles(2 * units, step_units, body)
-    total = own_part[...]
-    for by in range(1, heads):
-        second.arrived(by)
-        total = total + landed[by - 1].astype(jnp.float32)
-    grad_in[...] = total
-    scaled = total * (1.0 + scale_mlp[...])
-    middle = incoming[...] + inverse[...] * (
-        scaled
-        - jnp.mean(scaled, axis=-1, keepdims=True)
-        - normed[...] * jnp.mean(scaled * normed[...], axis=-1, keepdims=True)
-    )
-    grad_mid[...] = middle
-    branch_all[0] = (gate_attn[...] * middle).astype(jnp.bfloat16)
-    third = Across(place, lambda by: branch_all.at[0], lambda by: branch_all.at[by], sends, recvs, 2)
-    for by in range(1, heads):
-        third.start(by)
-    for item in items[1:2]:
-        item.second()
+    third = work.spread_stage(branch_all, 2)
+    for p in range(pieces):
+        at = work.at(p)
+        work.arrive_all(second, p)
+        value = work.total(own_part, landed, p)
+        grad_in[at] = value
+        unit = normed[at]
+        value = value * (1.0 + work.modulation(table, owner, 4, p))
+        value = incoming[at] + inverse[at] * (
+            value
+            - jnp.mean(value, axis=-1, keepdims=True)
+            - unit * jnp.mean(value * unit, axis=-1, keepdims=True)
+        )
+        grad_mid[at] = value
+        branch_all[0, at] = (work.modulation(table, owner, 2, p) * value).astype(jnp.bfloat16)
+        work.send_all(third, p)
     out.drain(2 * units // step_units)
     copies[4].wait()
     copies[5].wait()
@@ -807,16 +1161,18 @@
     def body(step, at):
         out.put(
             step,
-            dot_tn(mlp_all[...].reshape(heads * own, width), hidden[:, pl.ds(at, step_units)]),
+            dot_tn(mlp_all[...].reshape(head_size * own, width), hidden[:, pl.ds(at, step_units)]),
         )
 
     tiles(units, step_units, body)
+    for item in items[1:]:
+        item.second()
     grad_att[pl.ds(0, own), :] = dot_nn(branch_all[0], proj[...]).astype(jnp.bfloat16)
-    for item in items[2:]:
-        item.second()
-    for by in range(1, heads):
-        third.arrived(by)
-        grad_att[pl.ds(by * own, own), :] = dot_nn(branch_all[by], proj[...]).astype(jnp.bfloat16)
+    for by, p in work.others:
+        third.arrived(by, p)
+        grad_att[work.flat(by, p), :] = dot_nn(branch_all[by, work.at(p)], proj[...]).astype(
+            jnp.bfloat16
+        )
     keep = pltpu.make_async_copy(branch_all, branch_out, out_sem.at[0])
     keep.start()
     out.drain(units // step_units)
@@ -830,6 +1186,8 @@
 def mlp_back_call(row_size, head_size, near, streams, grads):
     count = len(grads)
     own, width = near[0].shape
+    pieces = pieces_of(own)
+    others = head_size - 1
     down, gate_up, gu, inputs, hidden, proj = streams
     units = hidden.shape[1]
     tokens = hidden.shape[0]
@@ -845,7 +1203,7 @@
     shape = jax.ShapeDtypeStruct
     f32, bf16 = jnp.float32, jnp.bfloat16
     return pl.pallas_call(
-        functools.partial(mlp_back_kernel, row_size, head_size, count),
+        functools.partial(mlp_back_kernel, row_size, head_size, pieces, count),
         out_shape=[
             shape((own, width), f32),
             shape((own, width), f32),
@@ -855,20 +1213,20 @@
             shape((width, units), bf16),
         ]
         + [shape(grad.shape[1:], f32) for grad in grads],
-        in_specs=[vmem] * 6 + [anywhere] * (6 + count),
+        in_specs=[vmem] * 5 + [anywhere] * (6 + count),
         out_specs=[vmem, vmem, anywhere, vmem, anywhere, anywhere] + [vmem] * count,
         scratch_shapes=[pltpu.VMEM(item.shape, item.dtype) for item in streams]
         + [
             pltpu.VMEM((head_size, own, width), bf16),
             pltpu.VMEM((head_size, own, width), bf16),
             pltpu.VMEM((tokens, 2 * units), bf16),
-            pltpu.VMEM((head_size - 1, own, width), bf16),
-            pltpu.VMEM((head_size - 1, own, width), bf16),
+            pltpu.VMEM((others, own, width), bf16),
+            pltpu.VMEM((others, own, width), bf16),
             pltpu.VMEM((own, width), f32),
             pltpu.VMEM((2, width, tile_of(units)), bf16),
             pltpu.SemaphoreType.DMA((6,)),
-            pltpu.SemaphoreType.DMA((3 * (head_size - 1),)),
-            pltpu.SemaphoreType.DMA((3 * (head_size - 1),)),
+            pltpu.SemaphoreType.DMA((3 * others * pieces,)),
+            pltpu.SemaphoreType.DMA((3 * others * pieces,)),
             pltpu.SemaphoreType.DMA((2,)),
             pltpu.SemaphoreType.DMA((1,)),
         ]
@@ -885,6 +1243,172 @@
     )(*near, *streams, *grads)
 
 
+def last_mlp_kernel(row_size, head_size, pieces, *refs):
+    attended, residual, owner, table, incoming, mlp_grads = refs[:6]
+    streams, refs = refs[6:9], refs[9:]
+    block_out, branch, normed, mlp_out, grad_in, grad_mid, branch_out, grad_att = refs[:8]
+    grads_out = refs[8]
+    weights, refs = refs[9:12], refs[12:]
+    proj, gu, down = weights
+    inputs, gate_up, hidden, ggu, branch_all, parcel, landed = refs[:7]
+    middle, inverse, own_part, own_mlp, buffer = refs[7:12]
+    loads, sends, recvs, tile_sems, out_sem = refs[12:]
+    place = Place(row_size, head_size)
+    own, width = residual.shape
+    units = hidden.shape[1]
+    work = Mlp(place, pieces, own, width, units, sends, recvs)
+    step_units = tile_of(units)
+    copies = [
+        pltpu.make_async_copy(source, target, loads.at[i])
+        for i, (source, target) in enumerate(zip(streams, weights))
+    ]
+    for copy in copies:
+        copy.start()
+    place.greet(True)
+    copies[0].wait()
+    first, second = work.front(
+        attended,
+        proj,
+        residual,
+        table,
+        owner,
+        parcel.at[0],
+        landed.at[0],
+        own_part,
+        branch,
+        middle,
+        normed,
+        inverse,
+        inputs,
+    )
+    copies[1].wait()
+    copies[2].wait()
+    work.gate_up(inputs, gu, gate_up, hidden, 0, 0, own)
+    work.hidden_back(mlp_grads, down, gate_up, ggu, 0, 0, own)
+    fourth = work.sum_stage(parcel.at[1], landed.at[1], 3)
+    for by, p in work.others:
+        second.arrived(by, p)
+        begin = p * work.rows
+        work.gate_up(inputs, gu, gate_up, hidden, by, begin, work.rows)
+        work.hidden_back(mlp_grads, down, gate_up, ggu, by, begin, work.rows)
+        work.partial(parcel.at[1, by - 1, work.at(p)], ggu, work.flat(by, p), gu)
+        fourth.start(by, p)
+    work.partial(own_part, ggu, pl.ds(0, own), gu)
+    out = Streamed(buffer, grads_out, tile_sems, step_units)
+
+    def body(step, at):
+        out.put(
+            step,
+            dot_tn(inputs[...].reshape(head_size * own, width), ggu[:, pl.ds(at, step_units)]),
+        )
+
+    tiles(2 * units, step_units, body)
+    fifth = work.spread_stage(branch_all, 4)
+    for p in range(pieces):
+        at = work.at(p)
+        work.arrive_all(fourth, p)
+        value = work.total(own_part, landed.at[1], p)
+        grad_in[at] = value
+        unit = normed[at]
+        value = value * (1.0 + work.modulation(table, owner, 4, p))
+        value = incoming[at].astype(jnp.float32) + inverse[at] * (
+            value
+            - jnp.mean(value, axis=-1, keepdims=True)
+            - unit * jnp.mean(value * unit, axis=-1, keepdims=True)
+        )
+        grad_mid[at] = value
+        branch_all[0, at] = (work.modulation(table, owner, 2, p) * value).astype(jnp.bfloat16)
+        work.send_all(fifth, p)
+    first.left()
+    third = work.sum_stage(parcel.at[0], landed.at[0], 2)
+    for by, p in work.others:
+        work.partial(parcel.at[0, by - 1, work.at(p)], hidden, work.flat(by, p), down)
+        third.start(by, p)
+    work.partial(own_mlp, hidden, pl.ds(0, own), down)
+    out.drain(2 * units // step_units)
+    out = Streamed(buffer, grads_out, tile_sems, step_units, 2 * units)
+
+    def body(step, at):
+        out.put(
+            step,
+            dot_tn(mlp_grads[...].reshape(head_size * own, width), hidden[:, pl.ds(at, step_units)]),
+        )
+
+    tiles(units, step_units, body)
+    grad_att[pl.ds(0, own), :] = dot_nn(branch_all[0], proj[...]).astype(jnp.bfloat16)
+    for by, p in work.others:
+        fifth.arrived(by, p)
+        grad_att[work.flat(by, p), :] = dot_nn(branch_all[by, work.at(p)], proj[...]).astype(
+            jnp.bfloat16
+        )
+    keep = pltpu.make_async_copy(branch_all, branch_out, out_sem.at[0])
+    keep.start()
+    for p in range(pieces):
+        at = work.at(p)
+        work.arrive_all(third, p)
+        value = work.total(own_mlp, landed.at[0], p)
+        mlp_out[at] = value
+        block_out[at] = (middle[at] + work.modulation(table, owner, 5, p) * value).astype(
+            jnp.bfloat16
+        )
+    out.drain(units // step_units)
+    for stage in (second, third, fourth, fifth):
+        stage.left()
+    keep.wait()
+
+
+def last_mlp_call(row_size, head_size, attended, residual, owner, table, incoming, mlp_grads, weights):
+    own, width = residual.shape
+    tokens = attended.shape[0]
+    units = weights[2].shape[1]
+    pieces = pieces_of(own)
+    others = head_size - 1
+    anywhere = pl.BlockSpec(memory_space=pl.ANY)
+    vmem = pl.BlockSpec(memory_space=pltpu.VMEM)
+    shape = jax.ShapeDtypeStruct
+    f32, bf16 = jnp.float32, jnp.bfloat16
+    return pl.pallas_call(
+        functools.partial(last_mlp_kernel, row_size, head_size, pieces),
+        out_shape=[
+            shape((own, width), bf16),
+            shape((own, width), f32),
+            shape((own, width), f32),
+            shape((own, width), f32),
+            shape((own, width), f32),
+            shape((own, width), f32),
+            shape((head_size, own, width), bf16),
+            shape(attended.shape, bf16),
+            shape((width, 3 * units), bf16),
+        ],
+        in_specs=[vmem] * 6 + [anywhere] * 3,
+        out_specs=[vmem] * 6 + [anywhere, vmem, anywhere],
+        scratch_shapes=[pltpu.VMEM(item.shape, item.dtype) for item in weights]
+        + [
+            pltpu.VMEM((head_size, own, width), bf16),
+            pltpu.VMEM((tokens, 2 * units), f32),
+            pltpu.VMEM((tokens, units), bf16),
+            pltpu.VMEM((tokens, 2 * units), bf16),
+            pltpu.VMEM((head_size, own, width), bf16),
+            pltpu.VMEM((2, others, own, width), bf16),
+            pltpu.VMEM((2, others, own, width), bf16),
+            pltpu.VMEM((own, width), f32),
+            pltpu.VMEM((own, 1), f32),
+            pltpu.VMEM((own, width), f32),
+            pltpu.VMEM((own, width), f32),
+            pltpu.VMEM((2, width, tile_of(units)), bf16),
+            pltpu.SemaphoreType.DMA((3,)),
+            pltpu.SemaphoreType.DMA((5 * others * pieces,)),
+            pltpu.SemaphoreType.DMA((5 * others * pieces,)),
+            pltpu.SemaphoreType.DMA((2,)),
+            pltpu.SemaphoreType.DMA((1,)),
+        ],
+        compiler_params=pltpu.CompilerParams(
+            collective_id=5, has_side_effects=True, vmem_limit_bytes=60 * 2**20
+        ),
+        name="last_mlp",
+    )(attended, residual, owner, table, incoming, mlp_grads, *weights)
+
+
 def rope_parts(coords):
     angle = angles(coords, HD // 4)
     return jnp.cos(angle), jnp.sin(angle)
@@ -946,14 +1470,12 @@
     return (grad_query, grad_key, grad_value)
 
 
-def spread(values, beside=()):
+def spread(values):
     arrived = [head_move(values, flip) for flip in range(1, lax.axis_size("heads"))]
-    arrived, beside = lax.optimization_barrier((arrived, beside))
-    return jnp.concatenate([values] + arrived, axis=0), beside
-
-
-def collect(operand, product, own_rows, beside=()):
-    total = None
+    return jnp.concatenate([values] + arrived, axis=0)
+
+
+def collect(operand, product, own_rows, beside):
     arrived = []
     for flip in range(1, lax.axis_size("heads")):
         partial = product(operand[flip * own_rows : (flip + 1) * own_rows])
@@ -978,15 +1500,8 @@
     return total
 
 
-def block_forward(residual, ready, pieces, qkv_full, qkv_b, proj_t, gu_full, down_t, image_ids, geometry):
-    shift_attn, scale_attn, gate_attn, shift_mlp, scale_mlp, gate_mlp = pieces
-    own_rows = residual.shape[0]
+def attention(input_attn, qkv_full, qkv_b, image_ids, geometry):
     count_rows, row_len = image_ids.shape
-    if ready is None:
-        normed_attn, inverse_attn = normalize(residual)
-        input_attn, _ = spread((normed_attn * (1.0 + scale_attn) + shift_attn).astype(jnp.bfloat16))
-    else:
-        normed_attn, inverse_attn, input_attn = ready
     packed = plain_dot(input_attn, qkv_full) + qkv_b
     heads_here = packed.shape[1] // (3 * HD)
     packed = packed.reshape(count_rows, row_len, heads_here, 3, HD)
@@ -995,96 +1510,12 @@
     value_rows = packed[:, :, :, 2].astype(jnp.bfloat16)
     attended, logsum = attend(queries, key_rows, value_rows, image_ids)
     attended = attended.reshape(count_rows * row_len, heads_here * HD)
-    branch, _ = collect(attended, lambda rows: tail_dot(rows, proj_t), own_rows)
-    middle = residual + gate_attn * branch
-    normed_mlp, inverse_mlp = normalize(middle)
-    input_mlp, _ = spread((normed_mlp * (1.0 + scale_mlp) + shift_mlp).astype(jnp.bfloat16))
-    gate_up = plain_dot(input_mlp, gu_full)
-    hidden_width = gate_up.shape[1] // 2
-    gate_part = gate_up[:, :hidden_width]
-    up_part = gate_up[:, hidden_width:]
-    hidden = (jax.nn.silu(gate_part) * up_part).astype(jnp.bfloat16)
-    mlp_out, _ = collect(hidden, lambda rows: tail_dot(rows, down_t), own_rows)
-    result = middle + gate_mlp * mlp_out
-    stored = (
-        normed_attn,
-        inverse_attn,
-        input_attn,
-        queries,
-        key_rows,
-        value_rows,
-        logsum,
-        attended,
-        branch,
-        normed_mlp,
-        inverse_mlp,
-        input_mlp,
-        gate_up,
-        hidden,
-        mlp_out,
-    )
-    return (result, stored)
-
-
-def block_backward(
-    incoming, ready, later, pieces, stored, qkv_full, proj_t, gu_full, down_t, image_ids, geometry
-):
-    shift_attn, scale_attn, gate_attn, shift_mlp, scale_mlp, gate_mlp = pieces
-    (
-        normed_attn,
-        inverse_attn,
-        input_attn,
-        queries,
-        key_rows,
-        value_rows,
-        logsum,
-        attended,
-        branch,
-        normed_mlp,
-        inverse_mlp,
-        input_mlp,
-        gate_up,
-        hidden,
-        mlp_out,
-    ) = stored
-    own_rows = incoming.shape[0]
+    return attended, (queries, key_rows, value_rows, logsum)
+
+
+def attention_back(grad_attended, stored, image_ids, geometry):
+    queries, key_rows, value_rows, logsum = stored
     count_rows, row_len = image_ids.shape
-    units = hidden.shape[1]
-    grad_gate_mlp = incoming * mlp_out
-    sums = ()
-    if later:
-        grad_input_mlp, grad_middle, gathered_branch, grad_attended, gu_grad, down_grad, *sums = (
-            mlp_back_call(
-                lax.axis_size("rows"),
-                lax.axis_size("heads"),
-                (incoming, gate_mlp, scale_mlp, gate_attn, normed_mlp, inverse_mlp),
-                (down_t, gate_up, gu_full, input_mlp, hidden, proj_t),
-                later,
-            )
-        )
-        gathered_branch = gathered_branch.reshape(-1, gathered_branch.shape[-1])
-    else:
-        gathered_mlp = ready
-        down_grad = lead_dot(gathered_mlp, hidden).astype(jnp.bfloat16)
-        grad_hidden = plain_dot(gathered_mlp, down_t)
-        gate_part = gate_up[:, :units]
-        up_part = gate_up[:, units:]
-        logistic = jax.nn.sigmoid(gate_part)
-        grad_gate_part = grad_hidden * up_part * logistic * (1.0 + gate_part * (1.0 - logistic))
-        grad_up_part = grad_hidden * gate_part * logistic
-        grad_gate_up = jnp.concatenate([grad_gate_part, grad_up_part], axis=1).astype(jnp.bfloat16)
-        gu_grad = lead_dot(input_mlp, grad_gate_up).astype(jnp.bfloat16)
-        grad_input_mlp, gu_grad = collect(
-            grad_gate_up, lambda rows: tail_dot(rows, gu_full), own_rows, gu_grad
-        )
-        grad_middle = incoming + norm_back(
-            grad_input_mlp * (1.0 + scale_mlp), normed_mlp, inverse_mlp
-        )
-        grad_branch = (gate_attn * grad_middle).astype(jnp.bfloat16)
-        gathered_branch, down_grad = spread(grad_branch, down_grad)
-        grad_attended = plain_dot(gathered_branch, proj_t).astype(jnp.bfloat16)
-    gu_out = lax.psum_scatter(gu_grad, "rows", scatter_dimension=0, tiled=True).astype(jnp.float32)
-    grad_gate_attn = grad_middle * branch
     heads_here = queries.shape[2]
     grad_attended = grad_attended.reshape(count_rows, row_len, heads_here, HD)
     grad_query, grad_key, grad_value = attend_back(
@@ -1097,54 +1528,11 @@
         .reshape(count_rows * row_len, heads_here * 3 * HD)
         .astype(jnp.bfloat16)
     )
-    qkv_bias_grad = jnp.sum(grad_packed, axis=0, dtype=jnp.float32)
-    qkv_grad, proj_grad = weight_grads((input_attn, grad_packed), (gathered_branch, attended))
-    grad_input_attn, (qkv_grad, proj_grad) = collect(
-        grad_packed, lambda rows: tail_dot(rows, qkv_full), own_rows, (qkv_grad, proj_grad)
-    )
-    grad_input = grad_middle + norm_back(
-        grad_input_attn * (1.0 + scale_attn), normed_attn, inverse_attn
-    )
-    grad_mods = jnp.concatenate(
-        [
-            grad_input_attn,
-            grad_input_attn * normed_attn,
-            grad_gate_attn,
-            grad_input_mlp,
-            grad_input_mlp * normed_mlp,
-            grad_gate_mlp,
-        ],
-        axis=1,
-    )
-    return (grad_input, grad_mods, (qkv_grad, qkv_bias_grad, proj_grad, gu_out, down_grad), sums)
-
-
-def heads_in_order(value):
-    index = lax.axis_index("heads")
-    count = lax.axis_size("heads")
-    chunks = [value] + [head_move(value, flip) for flip in range(1, count)]
-    placed = []
-    for slot in range(count):
-        item = chunks[0]
-        for flip in range(1, count):
-            item = jnp.where(index == slot ^ flip, chunks[flip], item)
-        placed.append(item)
-    return jnp.stack(placed)
-
-
-def heads_share(value):
-    index = lax.axis_index("heads")
-    count = lax.axis_size("heads")
-    width = value.shape[-1] // count
-
-    def part(flip):
-        return lax.dynamic_slice_in_dim(value, (index ^ flip) * width, width, value.ndim - 1)
-
-    arrived = [head_move(part(flip), flip) for flip in range(1, count)]
-    total = part(0)
-    for item in arrived:
-        total = total + item
-    return total
+    return grad_packed, jnp.sum(grad_packed, axis=0, dtype=jnp.float32)
+
+
+def image_sum(picker, values):
+    return lax.dot_general(picker, values, (((0,), (0,)), ((), ())), precision=lax.Precision.HIGH)
 
 
 def shards(
@@ -1200,101 +1588,189 @@
         jnp.pad(cond_act, ((0, pad), (0, 0))),
         ada_weight,
         bias_rows,
-        [item for b in range(block_count) for item in (qkv_weight[b], proj_weight[b].T)],
-    )
-    qkv_full, gu_full, down_t, proj_t = [], [], [], []
-    for b in range(block_count):
-        qkv_full.append(early[2 * b].reshape(-1, early[2 * b].shape[-1]))
-        proj_t.append(early[2 * b + 1].reshape(-1, early[2 * b + 1].shape[-1]))
-        gu_full.append(gathered(gu_weight[b].reshape(shard_rows, -1)))
+        [qkv_weight[0], proj_weight[0].T, down_weight[0].T],
+    )
+    qkv_full, proj_t, down_t = [[item.reshape(-1, item.shape[-1])] for item in early]
+    gu_full = [gathered(item.reshape(shard_rows, -1)) for item in gu_weight]
+    for b in range(1, block_count):
         down_t.append(gathered(down_weight[b].T))
     mod_all = mods.reshape(head_size, block_count, image_count, -1)
     modulation = [
         jnp.concatenate([mod_all[index, b] for index in range(head_size)], axis=1)
         for b in range(block_count)
     ]
-    pieces = [
-        [piece_of(modulation[b], own_images, index) for index in range(6)] for b in range(block_count)
-    ]
-    residual = tokens.astype(jnp.float32)
+    last = block_count - 1
     all_images = image_ids.reshape(-1)
-    every_token, _ = spread(tokens)
-    every_token = every_token.astype(jnp.float32)
+    owner = own_images[:, None]
+    every_token = spread(tokens).astype(jnp.float32)
     normed, inverse = normalize(every_token)
     shift, scale = [piece_of(modulation[0], all_images, index) for index in range(2)]
-    forward_ready = [None] * block_count
-    forward_ready[0] = (
-        normed[:own_rows],
-        inverse[:own_rows],
-        (normed * (1.0 + scale) + shift).astype(jnp.bfloat16),
-    )
-    every_cotangent, _ = spread(cotangent)
-    gate = piece_of(modulation[-1], all_images, 5)
-    backward_ready = [None] * block_count
-    backward_ready[-1] = (gate * every_cotangent.astype(jnp.float32)).astype(jnp.bfloat16)
-    stored_all = []
+    input_attn = (normed * (1.0 + scale) + shift).astype(jnp.bfloat16)
+    normed_attn, inverse_attn = [normed[:own_rows]], [inverse[:own_rows]]
+    inputs_attn = [input_attn]
+    gate = piece_of(modulation[last], all_images, 5)
+    mlp_grads = (gate * spread(cotangent).astype(jnp.float32)).astype(jnp.bfloat16)
+    mlp_grads = mlp_grads.reshape(head_size, own_rows, -1)
+    residual = tokens.astype(jnp.float32)
+    attentions, attended = [], []
     for b in range(block_count):
-        residual, stored = block_forward(
-            residual,
-            forward_ready[b],
-            pieces[b],
-            qkv_full[b],
-            qkv_bias[b].astype(jnp.float32),
-            proj_t[b],
-            gu_full[b],
-            down_t[b],
-            image_ids,
-            geometry,
-        )
-        stored_all.append(stored)
-    block_out = residual.astype(jnp.bfloat16)
-    incoming = cotangent.astype(jnp.float32)
-    block_grads = [None] * block_count
-    image_sums = [None] * block_count
-    block_sums = [None] * block_count
-    later = []
-    for b in reversed(range(block_count)):
-        incoming, grad_mods, gradients, sums = block_backward(
+        item, kept = attention(
+            inputs_attn[b], qkv_full[b], qkv_bias[b].astype(jnp.float32), image_ids, geometry
+        )
+        attended.append(item)
+        attentions.append(kept)
+        weights = (proj_t[b], gu_full[b], down_t[b])
+        if b < last:
+            (
+                branch,
+                normed_mlp,
+                input_mlp,
+                gate_up,
+                hidden,
+                inverse_mlp,
+                mlp_out,
+                residual,
+                next_normed,
+                next_inverse,
+                next_input,
+                next_qkv,
+                next_proj,
+            ) = mlp_call(
+                row_size,
+                head_size,
+                item,
+                residual,
+                owner,
+                modulation[b],
+                modulation[b + 1],
+                weights,
+                [qkv_weight[b + 1], proj_weight[b + 1].T],
+            )
+            normed_attn.append(next_normed)
+            inverse_attn.append(next_inverse)
+            inputs_attn.append(next_input.reshape(inputs_attn[0].shape))
+            qkv_full.append(next_qkv.reshape(qkv_full[0].shape))
+            proj_t.append(next_proj.reshape(proj_t[0].shape))
+            stored = (branch, normed_mlp, input_mlp, gate_up, hidden, inverse_mlp, mlp_out)
+    (
+        block_out,
+        last_branch,
+        last_normed,
+        last_out,
+        grad_input_mlp,
+        grad_middle,
+        gathered_branch,
+        grad_attended,
+        mlp_grad,
+    ) = last_mlp_call(
+        row_size,
+        head_size,
+        attended[last],
+        residual,
+        owner,
+        modulation[last],
+        cotangent,
+        mlp_grads,
+        weights,
+    )
+
+    def scattered(grad):
+        return lax.psum_scatter(grad, "rows", scatter_dimension=0, tiled=True).astype(jnp.float32)
+
+    def late_sums(middle, branch, incoming, normed, grad, out):
+        return [
+            image_sum(picker, item)
+            for item in (middle * branch, grad, grad * normed, incoming * out)
+        ]
+
+    gu_outs, bias_sums, image_sums = [None] * 2, [None] * 2, [None] * 2
+    mlp_sum = scattered(mlp_grad)
+    units = mlp_sum.shape[1] // 3
+    gathered_branch = gathered_branch.reshape(-1, gathered_branch.shape[-1])
+    grad_packed, bias_sums[1] = attention_back(grad_attended, attentions[1], image_ids, geometry)
+    qkv_grad, proj_grad = weight_grads(
+        (inputs_attn[1], grad_packed), (gathered_branch, attended[1])
+    )
+    late = late_sums(
+        grad_middle,
+        last_branch,
+        cotangent.astype(jnp.float32),
+        last_normed,
+        grad_input_mlp,
+        last_out,
+    )
+    grad_input_attn, (qkv_grad, proj_grad, late) = collect(
+        grad_packed, lambda rows: tail_dot(rows, qkv_full[1]), own_rows, (qkv_grad, proj_grad, late)
+    )
+    scale = piece_of(modulation[1], own_images, 1)
+    incoming = grad_middle + norm_back(
+        grad_input_attn * (1.0 + scale), normed_attn[1], inverse_attn[1]
+    )
+    image_sums[1] = jnp.concatenate(
+        [
+            image_sum(picker, grad_input_attn),
+            image_sum(picker, grad_input_attn * normed_attn[1]),
+        ]
+        + late,
+        axis=1,
+    )
+    branch, normed_mlp, input_mlp, gate_up, hidden, inverse_mlp, mlp_out = stored
+    block_sums = [None] * 2
+    (
+        grad_input_mlp,
+        grad_middle,
+        gathered_branch,
+        grad_attended,
+        gu_grad,
+        down_grad,
+        *block_sums[1],
+    ) = mlp_back_call(
+        row_size,
+        head_size,
+        (
             incoming,
-            backward_ready[b],
-            later,
-            pieces[b],
-            stored_all[b],
-            qkv_full[b],
-            proj_t[b],
-            gu_full[b],
-            down_t[b],
-            image_ids,
-            geometry,
-        )
-        image_sums[b] = lax.dot_general(
-            picker, grad_mods, (((0,), (0,)), ((), ())), precision=highest
-        )
-        block_grads[b] = gradients
-        later = [
-            gradients[which].reshape(row_size, shard_rows, -1) for which in (4, 0, 2)
-        ]
-        if b + 1 < block_count:
-            block_sums[b + 1] = sums
-    image_grads = heads_share(jnp.stack(image_sums)).astype(jnp.bfloat16)
-    bias_sums = jnp.stack([item[1] for item in block_grads])
-    bias_high = bias_sums.astype(jnp.bfloat16)
-    bias_rest = bias_sums - bias_high.astype(jnp.float32)
-    bias_middle = bias_rest.astype(jnp.bfloat16)
-    bias_low = (bias_rest - bias_middle.astype(jnp.float32)).astype(jnp.bfloat16)
-    wide = image_grads.shape[-1]
-    bias_parts = jnp.stack([bias_high, bias_middle, bias_low], axis=1)
-    columns = bias_sums.shape[1]
-    bias_parts = jnp.pad(bias_parts, ((0, 0), (0, 0), (0, wide - columns)))
-    small = jnp.concatenate([image_grads.reshape(-1, wide), bias_parts.reshape(-1, wide)])
-    used = small.shape[0]
-    small = jnp.pad(small, ((0, -used % 16), (0, 0)))
+            owner,
+            modulation[0],
+            normed_mlp,
+            inverse_mlp,
+        ),
+        (
+            down_t[0],
+            gate_up,
+            gu_full[0],
+            input_mlp.reshape(-1, input_mlp.shape[-1]),
+            hidden,
+            proj_t[0],
+        ),
+        [item.reshape(row_size, shard_rows, -1) for item in (qkv_grad, proj_grad)],
+    )
+    gu_grad, mlp_sum = lax.optimization_barrier((gu_grad, mlp_sum))
+    gu_outs[0] = scattered(gu_grad)
+    gathered_branch = gathered_branch.reshape(-1, gathered_branch.shape[-1])
+    grad_packed, bias_sums[0] = attention_back(grad_attended, attentions[0], image_ids, geometry)
+    late = late_sums(grad_middle, branch, incoming, normed_mlp, grad_input_mlp, mlp_out)
+    image_sums[0] = jnp.concatenate([jnp.zeros_like(late[0])] * 2 + late, axis=1)
+    gu_outs[1] = mlp_sum[:, : 2 * units]
+    block_sums[1] = [mlp_sum[:, 2 * units :]] + block_sums[1]
+    sheets = jnp.stack(image_sums).reshape(block_count * image_count, head_size, -1)
+    sheets = sheets.transpose(1, 0, 2)
+    wide = sheets.shape[-1]
+    bias_sums = jnp.stack(bias_sums)
+    bias_high = bias_sums.astype(jnp.bfloat16).astype(jnp.float32)
+    bias_rest = bias_sums - bias_high
+    bias_middle = bias_rest.astype(jnp.bfloat16).astype(jnp.float32)
+    bias_parts = jnp.stack([bias_high, bias_middle, bias_rest - bias_middle], axis=1)
+    bias_parts = jnp.pad(bias_parts, ((0, 0), (0, 0), (0, wide - bias_sums.shape[1])))
+    bias_parts = bias_parts.reshape(-1, wide)
+    used = sheets.shape[1] + bias_parts.shape[0]
+    small_rows = used + -used % 16
+    bias_parts = jnp.pad(bias_parts, ((sheets.shape[1], small_rows - used), (0, 0)))
     cond_rows = cond_mine.reshape(row_size, -1, shard_rows)[:, :image_count]
-    row = jnp.arange(small.shape[0])
+    row = jnp.arange(small_rows)
     mine = []
     for b in range(block_count):
         first = b * image_count
-        lead = jnp.pad(cond_rows, ((0, 0), (first, small.shape[0] - first - image_count), (0, 0)))
+        lead = jnp.pad(cond_rows, ((0, 0), (first, small_rows - first - image_count), (0, 0)))
         is_image = (row >= first) & (row < first + image_count)
         start = block_count * image_count + 3 * b
         is_bias = (row >= start) & (row < start + 3)
@@ -1306,28 +1782,40 @@
     logistic = jax.nn.sigmoid(cond_wide)
     factor = logistic * (1.0 + cond_wide * (1.0 - logistic))
     factor = jnp.pad(factor, ((0, -image_count % 8), (0, 0)))
-    ada_grads, ada_bias_grads, qkv_bias_out, cond_grad, *block_sums[0] = finish_call(
+    tokens_grad, ada_grads, ada_bias_grads, qkv_bias_out, cond_grad, *block_sums[0] = finish_call(
         row_size,
         head_size,
         image_count,
-        later,
-        small,
+        (
+            grad_packed,
+            qkv_full[0],
+            inputs_attn[0],
+            attended[0],
+            gathered_branch,
+            grad_middle,
+            piece_of(modulation[0], own_images, 1),
+            normed_attn[0],
+            inverse_attn[0],
+            owner,
+        ),
+        sheets,
+        bias_parts,
         jnp.stack(mine),
         ada_weight,
         factor,
-        columns,
+        down_grad.reshape(row_size, shard_rows, -1),
     )
     cond_grad = cond_grad[:image_count]
     return (
         block_out,
-        incoming,
+        tokens_grad,
         cond_grad,
         ada_grads,
         ada_bias_grads,
         jnp.stack([item[1] for item in block_sums]),
         qkv_bias_out,
         jnp.stack([item[2].T for item in block_sums]),
-        jnp.stack([item[3].reshape(gu_weight.shape[1:]) for item in block_grads]),
+        jnp.stack([item.reshape(gu_weight.shape[1:]) for item in gu_outs]),
         jnp.stack([item[0].T for item in block_sums]),
     )
 

time: 701 us -> 666 us (0.950)
  Pallas kernels: 342 us -> 458 us
  matrix products: 114 us -> 46.2 us
  waiting for transfers between devices: 58.9 us -> 24.4 us
  other arithmetic: 76.6 us -> 47.3 us
  starting transfers between devices: 18.7 us -> 4.28 us
    pallas_call x1 -> x3, Pallas kernels: 96.3 us -> 228 us  [the longest x1 82.9 us: mlp_call(): pl.pallas_call(functools.partial(mlp_kernel, row_size, head_size, pieces,...]
    ppermute x14 -> x3, waiting for transfers between devices: 58.7 us -> 0.01 us  [head_move(): lax.ppermute(value, 'heads', [(index, index ^ flip) for index in range(si...]
    dot_general x14 -> x2, matrix products: 34.2 us -> 6.71 us  [tail_dot(): lax.dot_general(operand, other, (((1,), (1,)), ((), ())), preferred_eleme...]
    dot_general x6 -> x2, matrix products: 34 us -> 7.65 us  [plain_dot(): return jnp.dot(operand, other, preferred_element_type=jnp.float32)]
    reduce_scatter x2, waiting for transfers between devices: 0.02 us -> 24.3 us  [scattered(): lax.psum_scatter(grad, 'rows', scatter_dimension=0, tiled=True)]
    pallas_call x1, Pallas kernels: 132 us -> 113 us  [start_call(): pl.pallas_call(functools.partial(start_kernel, row_size, head_size, image...]
    dot_general x4 -> x10, matrix products: 21.8 us -> 6.86 us  [image_sum(): lax.dot_general(picker, values, (((0,), (0,)), ((), ())), precision=lax.P...]
    ppermute x14 -> x3, starting transfers between devices: 18.1 us -> 4.08 us  [head_move(): lax.ppermute(value, 'heads', [(index, index ^ flip) for index in range(si...]
  transfers between devices with their start and end apart: 20 -> 8, of which waited for: 10 -> 1; matrix products, arithmetic and copies ran while one was open for 30% -> 18% of each run, Pallas kernels for 49% -> 58%
where the time goes in v5:
time: 666 us; the launch traced here: 658 us
  Pallas kernels  458 us (69%)
  local copies, waits for them, and re-layouts  62 us (9%)
  other arithmetic  47.3 us (7%)
  matrix products  46.2 us (7%)
  waiting for transfers between devices  24.4 us (4%)
  between operations  15.7 us (2%)
    pallas_call x1, Pallas kernels, start_call(): pl.pallas_call(functools.partial(start_kernel, row_size, head_size, image...  113 us
    pallas_call x1, Pallas kernels, finish_call(): pl.pallas_call(functools.partial(finish_kernel, row_size, head_size, imag...  111 us
    pallas_call x1, Pallas kernels, mlp_call(): pl.pallas_call(functools.partial(mlp_kernel, row_size, head_size, pieces,...  82.9 us
    pallas_call x1, Pallas kernels, last_mlp_call(): pl.pallas_call(functools.partial(last_mlp_kernel, row_size, head_size, pi...  79 us
    pallas_call x1, Pallas kernels, mlp_back_call(): pl.pallas_call(functools.partial(mlp_back_kernel, row_size, head_size, pi...  66.1 us
    unnamed x223, local copies, waits for them, and re-layouts  27.2 us
    reduce_scatter x2, waiting for transfers between devices, scattered(): lax.psum_scatter(grad, 'rows', scatter_dimension=0, tiled=True)  24.3 us
  transfers between devices with their start and end apart: 8, of which 1 were waited for; matrix products, arithmetic and copies ran while one was open for 18% of the time, Pallas kernels for 58%

profile of v5, /device:TPU:0, one launch (start us, length us, event | category | flops | bytes accessed | tf_op | source)
XLA Modules:
  0.0 658.1 jit_solution(1183283639038141601)
XLA Ops:
  7.2 1.8 fusion.97
  10.8 3.0 collective-permute-start.1
  22.2 1.8 slice_bitcast_fusion.1
  25.6 113.2 %start.1 = (bf16[16,72,1728]{2,1,0:T(8,128)(2,1)}, bf16[16,72,576]{2,1,0:T(8,128)(2,1)S(1)}, bf16[16,72,1536]{2,1,0:T(8,128)(2,1)}, f32[2,8,3456]{2,1,0:T(8,128)S(1)}, bf16[256,72]{1,0:T(8,128)(2,1)S(1)}) custom-call(bf16[16,1152]{1,0:T(8,128)(2,1)S(1)} %pad.31.refs_0_, bf16[2,72,3456]{2,1,0:T(8,128)(2,1)S(1)} %copy-done.1, ...), custom_call_target="tpu_custom_call" | custom-call | tf_op jit(solution)/shard_map/start/pallas_call | solution.py:419
  143.3 6.3 fusion.12
  149.7 2.6 convolution_add_fusion.1
  154.6 1.9 fusion.98
  157.8 2.1 copy-done.6
  163.7 2.4 fusion.15.refs_5_
  166.1 82.9 %mlp.1 = (f32[256,1152]{1,0:T(8,128)}, f32[256,1152]{1,0:T(8,128)}, bf16[2,256,1152]{2,1,0:T(8,128)(2,1)}, f32[512,3072]{1,0:T(8,128)}, bf16[512,1536]{1,0:T(8,1...) custom-call(bf16[512,576]{1,0:T(8,128)(2,1)} %copy.78.refs_0_.refs_3, ...), custom_call_target="tpu_custom_call" | custom-call | tf_op jit(solution)/shard_map/mlp/pallas_call | solution.py:1035
  249.0 5.1 convolution_add_fusion
  255.1 1.9 fusion.99
  258.3 2.2 copy-done.7
  263.1 79.0 %last_mlp.1 = (bf16[256,1152]{1,0:T(8,128)(2,1)}, f32[256,1152]{1,0:T(8,128)}, f32[256,1152]{1,0:T(8,128)}, f32[256,1152]{1,0:T(8,128)}, f32[256,1152]{1,0:T(8,1...) custom-call(bf16[512,576]{1,0:T(8,128)(2,1)} %copy.84.refs_0_.refs_3, ...), custom_call_target="tpu_custom_call" | custom-call | tf_op jit(solution)/shard_map/last_mlp/pallas_call | solution.py:1370
  345.4 5.0 multiply_reduce_fusion.1
  351.7 2.5 multiply_convert_fusion.1
  361.3 2.8 copy.93.refs_1_
  364.1 5.3 convolution_convert_fusion
  373.3 6.2 weight_grads.1
  386.3 3.3 fusion.93
  390.9 66.1 %mlp_back.1 = (f32[256,1152]{1,0:T(8,128)}, f32[256,1152]{1,0:T(8,128)}, bf16[2,256,1152]{2,1,0:T(8,128)(2,1)}, bf16[512,576]{1,0:T(8,128)(2,1)}, bf16[1152,3072...) custom-call(f32[256,1152]{1,0:T(8,128)} %multiply_add_fusion.refs_0_, ...), custom_call_target="tpu_custom_call" | custom-call | tf_op jit(solution)/shard_map/mlp_back/pallas_call | solution.py:1205
  457.0 24.3 %reduce-scatter.3.cloned.1.call-done = bf16[72,4608]{1,0:T(8,128)(2,1)} async-done(((bf16[1152,4608]{1,0:T(8,128)(2,1)}), bf16[72,4608]{1,0:T(8,128)(2,1)}) %reduce-scatter.3.cloned.1.call-update) | async-done | bytes 663568 | tf_op jit(solution)/shard_map/reduce_scatter | solution.py:1678
  481.3 2.3 convert_element_type.306
  486.8 2.5 slice.396.refs_7_
  490.9 1.7 convolution_dynamic-update-slice_fusion
  498.5 5.8 multiply_reduce_fusion
  506.2 2.8 multiply_convert_fusion
  519.1 2.4 copy.106.refs_0_
  521.5 110.8 %finish.1 = (f32[256,1152]{1,0:T(8,128)}, f32[2,72,3456]{2,1,0:T(8,128)}, f32[2,3456]{1,0:T(2,128)}, f32[2,1728]{1,0:T(2,128)}, f32[8,1152]{1,0:T(8,128)}, /*ind...) custom-call(bf16[512,1728]{1,0:T(8,128)(2,1)} %copy.106.refs_0_, bf16[1152,1728]{1,0:T(8,128)(2,1)} %bitcast.235, ...), custom_call_target="tpu_custom_call" | custom-call | tf_op jit(solution)/shard_map/finish/pallas_call | solution.py:708
  635.3 2.1 pad_maximum_fusion.3
  641.3 1.9 reshape.1189
  643.2 2.0 pad_maximum_fusion
  (376 shorter events, 86.6 us)
Async XLA Ops:
  7.2 158.9 %all-gather.4.cloned.1.call-start = ((), (), s32[]{:S(2)}) async-start(), calls=%async_computation.2 | async-start | bytes 7520256 | tf_op jit(solution)/shard_map/all_gather | solution.py:1579
  9.0 4.7 copy-start.12
  9.9 253.2 %all-gather.8.cloned.1.call-start = ((), (), s32[]{:S(2)}) async-start(), calls=%async_computation.4 | async-start | bytes 3760128 | tf_op jit(solution)/shard_map/all_gather | solution.py:1579
  10.7 252.4 %all-gather.6.cloned.1.call-start = ((), (), s32[]{:S(2)}) async-start(), calls=%async_computation.3 | async-start | bytes 7520256 | tf_op jit(solution)/shard_map/all_gather | solution.py:1579
  10.8 151.7 %collective-permute-start.1 = (bf16[256,1152]{1,0:T(8,128)(2,1)S(1)}, bf16[256,1152]{1,0:T(8,128)(2,1)}, u32[]{:S(2)}, u32[]{:S(2)}) collective-permute-start(bf16[256,1152]{1,0:T(8,128)(2,1)S(1)} %copy-done.14), channel_id=1, source_target_pairs={{0,1},{1,0},{2,3},{3,2},{4,5},{5,4},{6,7},{7,6},{8,9},{9,8},{10,11... | collective-permute-start | bytes 1769480 | tf_op jit(solution)/shard_map/ppermute | solution.py:51
  13.8 128.8 %collective-permute-start = (bf16[256,1152]{1,0:T(8,128)(2,1)S(1)}, bf16[256,1152]{1,0:T(8,128)(2,1)S(1)}, u32[]{:S(2)}, u32[]{:S(2)}) collective-permute-start(bf16[256,1152]{1,0:T(8,128)(2,1)S(1)} %copy-done.12), channel_id=1, source_target_pairs={{0,1},{1,0},{2,3},{3,2},{4,5},{5,4},{6,7},{7,6},{8,9},{9,8},{10,11... | collective-permute-start | bytes 1769480 | tf_op jit(solution)/shard_map/ppermute | solution.py:51
  14.7 5.7 copy-start.83
  14.7 6.4 copy-start.81
  14.7 466.6 %reduce-scatter.3.cloned.1.call-start = ((), (), s32[]{:S(2)}) async-start(), calls=%async_computation.5 | async-start | bytes 11280384 | tf_op jit(solution)/shard_map/reduce_scatter | solution.py:1678
  15.9 9.8 %copy-start.1 = (bf16[2,72,3456]{2,1,0:T(8,128)(2,1)S(1)}, bf16[2,72,3456]{2,1,0:T(8,128)(2,1)}, u32[]{:S(2)}) copy-start(bf16[2,72,3456]{2,1,0:T(8,128)(2,1)} %refs_13_.1) | copy-start | bytes 2985988
  25.6 114.5 %copy-start.78 = (bf16[2,1728]{1,0:T(2,128)(2,1)S(1)}, bf16[2,1728]{1,0:T(2,128)(2,1)}, u32[]{:S(2)}) copy-start(bf16[2,1728]{1,0:T(2,128)(2,1)} %param.21) | copy-start | bytes 20740
  143.2 6.4 copy-start.82
  143.3 6.4 copy-start.22
  152.2 5.5 copy-start.23
  166.1 82.9 %copy-start.84 = (f32[1728]{0:T(1024)S(1)}, f32[1728]{0:T(1024)}, u32[]{:S(2)}) copy-start(f32[1728]{0:T(1024)} %get-tuple-element.146) | copy-start | bytes 20740
  254.0 4.2 copy-start.24
  342.1 299.1 %reduce-scatter.5.cloned.1.call-start = ((), (), s32[]{:S(2)}) async-start(), calls=%async_computation.6 | async-start | bytes 7520256 | tf_op jit(solution)/shard_map/reduce_scatter | solution.py:1678
  345.1 11.9 %copy-start.28 = (f32[512,18]{0,1:T(8,128)}, f32[512,18]{0,1:T(8,128)S(1)}, u32[]{:S(2)}) copy-start(f32[512,18]{0,1:T(8,128)S(1)} %broadcast_multiply_fusion.1) | copy-start | bytes 110596
  345.1 11.9 %copy-start.30 = (f32[512,18]{0,1:T(8,128)}, f32[512,18]{0,1:T(8,128)S(1)}, u32[]{:S(2)}) copy-start(f32[512,18]{0,1:T(8,128)S(1)} %broadcast_multiply_fusion) | copy-start | bytes 110596
  345.4 5.0 slice-start.2
  345.4 6.3 slice-start.3
  364.1 7.3 %copy-start.63 = (f32[256,1]{1,0:T(8,128)S(1)}, f32[256,1]{1,0:T(8,128)}, u32[]{:S(2)}) copy-start(f32[256,1]{1,0:T(8,128)} %get-tuple-element.83) | copy-start | bytes 3076
  369.4 16.8 %collective-permute-start.2 = (bf16[256,1152]{1,0:T(8,128)(2,1)}, bf16[256,1152]{1,0:T(8,128)(2,1)}, u32[]{:S(2)}, u32[]{:S(2)}) collective-permute-start(bf16[256,1152]{1,0:T(8,128)(2,1)} %convolution_convert_fusion), channel_id=1, source_target_pairs={{0,1},{1,0},{2,3},{3,2},{4,5},{5,4},{6,7},{7,6},{8,9},{9,8},{10,11... | collective-permute-start | bytes 1769480 | tf_op jit(solution)/shard_map/ppermute | solution.py:51
  373.2 6.2 copy-start.15
  373.2 6.2 copy-start.37
  373.3 7.3 %copy-start.35 = (f32[256,1152]{1,0:T(8,128)S(1)}, f32[256,1152]{1,0:T(8,128)}, u32[]{:S(2)}) copy-start(f32[256,1152]{1,0:T(8,128)} %get-tuple-element.88) | copy-start | bytes 3538948
  373.3 10.6 %copy-start.97 = (bf16[16,72,1728]{2,1,0:T(8,128)(2,1)S(1)}, bf16[16,72,1728]{2,1,0:T(8,128)(2,1)}, u32[]{:S(2)}) copy-start(bf16[16,72,1728]{2,1,0:T(8,128)(2,1)} %get-tuple-element.78) | copy-start | bytes 11943940
  386.2 3.4 copy-start.10
  498.4 6.2 slice-start
  498.5 7.8 %slice-start.1 = ((s8[8388608]{0:T(1024)(128)(4,1)}), s8[4194304]{0:T(1024)(128)(4,1)S(1)}, s32[]{:S(2)}) async-start(s8[8388608]{0:T(1024)(128)(4,1)} %bitcast.220), calls=%async_computation.8 | async-start | bytes 8388608
  521.5 112.1 %copy-start.62 = (f32[72,576]{1,0:T(8,128)S(1)}, f32[72,576]{1,0:T(8,128)}, u32[]{:S(2)}) copy-start(f32[72,576]{1,0:T(8,128)} %get-tuple-element.122) | copy-start | bytes 497668
  521.5 113.8 %copy-start.58 = (f32[72,1728]{1,0:T(8,128)S(1)}, f32[72,1728]{1,0:T(8,128)}, u32[]{:S(2)}) copy-start(f32[72,1728]{1,0:T(8,128)} %get-tuple-element.119) | copy-start | bytes 1492996
  (82 other events, 149.9 us)
Sparse Core Ops, SparseCore 0:
  10.9 101.4 all-gather.3
  114.7 47.9 all-gather.7
  165.5 80.6 all-gather.5
  342.3 138.9 reduce-scatter.2
  485.1 107.4 reduce-scatter.4

commit v6 on v5

--- a/solution.py
+++ b/solution.py
@@ -338,19 +338,33 @@
 
 
 def start_kernel(row_size, head_size, images, blocks, weights, *refs):
-    cond, ada, bias = refs[:3]
-    shards = refs[3 : 3 + weights]
-    outs = refs[3 + weights : 3 + 2 * weights]
-    mods, mine_out = refs[3 + 2 * weights : 5 + 2 * weights]
-    (conds, part, held, met, side, far, total, every, sends, recvs, keeps, mod_send, mod_recv, mod_load, head_send, head_recv) = refs[5 + 2 * weights :]
+    cond, ada, bias, tokens, cotangent, owner = refs[:6]
+    shards = [ref.at[0] for ref in refs[6 : 6 + weights]]
+    outs = refs[6 + weights : 6 + 2 * weights]
+    refs = refs[6 + 2 * weights :]
+    table, mine_out, inputs_out, normed_out, inverse_out, grads_out = refs[:6]
+    every_token, every_cotangent, token_send, token_recv = refs[6:10]
+    refs = refs[10:]
+    (conds, part, held, met, side, far, total, every, sends, recvs, keeps) = refs[:11]
+    (mod_send, mod_recv, mod_load, head_send, head_recv) = refs[11:]
     place = Place(row_size, head_size)
     place.greet(True)
     items = [
         Gather(place, shard, out, sends.at[i], recvs.at[i], keeps.at[i])
-        for i, (shard, out) in enumerate(zip((cond,) + shards, (conds,) + outs))
+        for i, (shard, out) in enumerate(zip((cond,) + tuple(shards), (conds,) + outs))
     ]
     lead, bulk = items[0], items[1:]
     lead.begin()
+    own = tokens.shape[0]
+    every_token[0] = tokens[...]
+    every_cotangent[0] = cotangent[...]
+    raws = [
+        Across(place, lambda by: ref.at[0], lambda by: ref.at[by], token_send, token_recv, stage)
+        for stage, ref in enumerate((every_token, every_cotangent))
+    ]
+    for raw in raws:
+        for by in range(1, head_size):
+            raw.start(by)
     bulk[0].begin()
     hops = range(1, place.sizes[0])
     for k in hops:
@@ -401,12 +415,49 @@
         item.second()
     for copy in across:
         copy.wait()
-    mods[...] = every[...]
+    wide = every.shape[2]
+    for head in range(head_size):
+        table[:, head * wide : (head + 1) * wide] = every[head]
+    for raw in raws:
+        for by in range(1, head_size):
+            raw.arrived(by)
+    columns = tokens.shape[1]
+    half = own // pieces_of(own)
+
+    def modulation(here, first, index):
+        value = jnp.zeros((half, columns), jnp.float32)
+        for image in range(images):
+            row = table[first + image : first + image + 1, index * columns : (index + 1) * columns]
+            value = jnp.where(here == image, row, value)
+        return value
+
+    last = (blocks - 1) * images
+
+    @pl.loop(0, head_size * (own // half))
+    def _(step):
+        slot = step // (own // half)
+        rows = pl.ds(pl.multiple_of(step % (own // half) * half, 8), half)
+        here = owner[pl.ds(pl.multiple_of(step * half, 8), half), :]
+        unit, scale = normalize(every_token[slot, rows].astype(jnp.float32))
+        inputs_out[slot, rows] = (
+            unit * (1.0 + modulation(here, 0, 1)) + modulation(here, 0, 0)
+        ).astype(jnp.bfloat16)
+        grads_out[slot, rows] = (
+            modulation(here, last, 5) * every_cotangent[slot, rows].astype(jnp.float32)
+        ).astype(jnp.bfloat16)
+
+        @pl.when(slot == 0)
+        def _():
+            normed_out[rows] = unit
+            inverse_out[rows] = scale
+
+    for raw in raws:
+        raw.left()
     for item in bulk:
         item.finish()
 
 
-def start_call(row_size, head_size, cond, ada, bias, shards):
+def start_call(row_size, head_size, cond, ada, bias, tokens, cotangent, owner, shards):
     images = bias.shape[0] // ada.shape[0]
     blocks = ada.shape[0]
     count = len(shards)
@@ -415,17 +466,27 @@
     copies = gather_count(row_size)
     anywhere = pl.BlockSpec(memory_space=pl.ANY)
     vmem = pl.BlockSpec(memory_space=pltpu.VMEM)
-    f32 = jnp.float32
+    f32, bf16 = jnp.float32, jnp.bfloat16
+    own, width = tokens.shape
+    shape = jax.ShapeDtypeStruct
     return pl.pallas_call(
         functools.partial(start_kernel, row_size, head_size, images, blocks, count),
-        out_shape=[jax.ShapeDtypeStruct((row_size,) + item.shape, item.dtype) for item in shards]
+        out_shape=[jax.ShapeDtypeStruct((row_size,) + item.shape[1:], item.dtype) for item in shards]
         + [
-            jax.ShapeDtypeStruct((head_size,) + chunk, f32),
-            jax.ShapeDtypeStruct((row_size * cond.shape[0], ada.shape[1]), cond.dtype),
+            shape((chunk[0], head_size * chunk[1]), f32),
+            shape((row_size * cond.shape[0], ada.shape[1]), cond.dtype),
+            shape((head_size, own, width), bf16),
+            shape((own, width), f32),
+            shape((own, 1), f32),
+            shape((head_size, own, width), bf16),
         ],
-        in_specs=[vmem] * 3 + [anywhere] * count,
-        out_specs=[anywhere] * count + [vmem] * 2,
+        in_specs=[vmem] * 6 + [anywhere] * count,
+        out_specs=[anywhere] * count + [vmem] * 6,
         scratch_shapes=[
+            pltpu.VMEM((head_size, own, width), bf16),
+            pltpu.VMEM((head_size, own, width), bf16),
+            pltpu.SemaphoreType.DMA((2 * (head_size - 1),)),
+            pltpu.SemaphoreType.DMA((2 * (head_size - 1),)),
             pltpu.VMEM((row_size,) + cond.shape, cond.dtype),
             pltpu.VMEM((row_size,) + chunk, f32),
             pltpu.VMEM((a, b) + chunk, f32),
@@ -447,7 +508,7 @@
             collective_id=1, has_side_effects=True, vmem_limit_bytes=48 * 2**20
         ),
         name="start",
-    )(cond, ada, bias, *shards)
+    )(cond, ada, bias, tokens, cotangent, owner, *shards)
 
 
 def weight_grads_kernel(*refs):
@@ -552,9 +613,12 @@
 
 def finish_kernel(row_size, head_size, images, blocks, *refs):
     (packed, qkv, inputs, attended, branch, middle, scale, normed, inverse, owner) = refs[:10]
-    known, bias, mine, ada, factor, down = refs[10:16]
-    grad_tokens, ada_out, ada_bias_out, qkv_bias_out, cond_out = refs[16:21]
-    outs = refs[21:24]
+    known, bias, mine, ada, factor = refs[10:15]
+    done, down = refs[15:18], refs[18]
+    grad_tokens, ada_out, ada_bias_out, qkv_bias_out, cond_out = refs[19:24]
+    stacks = refs[24:27]
+    outs = [ref.at[0] for ref in stacks]
+    refs = refs[3:]
     parcel, landed, sheet, share_in, small, qkv_grad, proj_grad = refs[24:31]
     head_send, head_recv = refs[31:33]
     refs = refs[33:]
@@ -566,6 +630,8 @@
     own, width = middle.shape
     step_width = tile_of(width)
     place.greet(True)
+    for stack, item in zip(stacks, done):
+        stack[1] = item[...]
     items = [
         Scatter(
             place, source, outs[i], *scratch[4 * i : 4 * i + 4], send.at[i], recv.at[i], load.at[i]
@@ -687,7 +753,7 @@
         stage.left()
 
 
-def finish_call(row_size, head_size, images, near, known, bias, mine, ada, factor, down):
+def finish_call(row_size, head_size, images, near, known, bias, mine, ada, factor, done, down):
     packed, qkv, inputs, attended, branch, middle = near[:6]
     copies = scatter_count(row_size)
     small_copies = gather_count(row_size)
@@ -714,8 +780,8 @@
             shape((blocks, qkv.shape[1]), f32),
             shape(factor.shape, f32),
         ]
-        + [shape(item, f32) for item in chunks],
-        in_specs=[vmem] * 15 + [anywhere],
+        + [shape((2,) + item, f32) for item in chunks],
+        in_specs=[vmem] * 18 + [anywhere],
         out_specs=[vmem] * 8,
         scratch_shapes=[
             pltpu.VMEM((others, own, width), bf16),
@@ -752,7 +818,7 @@
             collective_id=2, has_side_effects=True, vmem_limit_bytes=60 * 2**20
         ),
         name="finish",
-    )(*near, known, bias, mine, ada, factor, down)
+    )(*near, known, bias, mine, ada, factor, *done, down)
 
 
 class Pieces:
@@ -907,9 +973,9 @@
         tiles(self.units, size, body)
 
 
-def mlp_kernel(row_size, head_size, pieces, count, *refs):
+def mlp_kernel(row_size, head_size, pieces, count, which, *refs):
     attended, residual, owner, table, following = refs[:5]
-    streams, shards = refs[5:8], refs[8 : 8 + count]
+    streams, shards = refs[5:8], [ref.at[which] for ref in refs[8 : 8 + count]]
     refs = refs[8 + count :]
     kept_out, refs = refs[:5], refs[5:]
     inverse, mlp_out, result, next_normed, next_inverse, next_out = refs[:6]
@@ -1013,7 +1079,7 @@
     return 2 if own % 32 == 0 else 1
 
 
-def mlp_call(row_size, head_size, attended, residual, owner, table, following, weights, shards):
+def mlp_call(row_size, head_size, attended, residual, owner, table, following, weights, which, shards):
     own, width = residual.shape
     tokens = attended.shape[0]
     units = weights[2].shape[1]
@@ -1033,7 +1099,7 @@
         shape((tokens, units), bf16),
     ]
     return pl.pallas_call(
-        functools.partial(mlp_kernel, row_size, head_size, pieces, count),
+        functools.partial(mlp_kernel, row_size, head_size, pieces, count, which),
         out_shape=kept
         + [
             shape((own, 1), f32),
@@ -1043,7 +1109,7 @@
             shape((own, 1), f32),
             shape((head_size, own, width), bf16),
         ]
-        + [shape((row_size,) + item.shape, item.dtype) for item in shards],
+        + [shape((row_size,) + item.shape[1:], item.dtype) for item in shards],
         in_specs=[vmem] * 5 + [anywhere] * (3 + count),
         out_specs=[anywhere] * 5 + [vmem] * 6 + [anywhere] * count,
         scratch_shapes=[pltpu.VMEM(item.shape, item.dtype) for item in weights]
@@ -1582,35 +1648,28 @@
     cond_act = jax.nn.silu(cond_wide).astype(jnp.bfloat16)
     pad = -image_count % 16
     bias_rows = jnp.repeat(ada_bias.astype(jnp.float32), image_count, axis=0)
-    *early, mods, cond_mine = start_call(
+    proj_flat, down_flat = proj_weight.transpose(0, 2, 1), down_weight.transpose(0, 2, 1)
+    *early, table, cond_mine, input_attn, normed, inverse, mlp_grads = start_call(
         row_size,
         head_size,
         jnp.pad(cond_act, ((0, pad), (0, 0))),
         ada_weight,
         bias_rows,
-        [qkv_weight[0], proj_weight[0].T, down_weight[0].T],
+        tokens,
+        cotangent,
+        image_ids.reshape(-1, 1),
+        [qkv_weight, proj_flat, down_flat],
     )
     qkv_full, proj_t, down_t = [[item.reshape(-1, item.shape[-1])] for item in early]
     gu_full = [gathered(item.reshape(shard_rows, -1)) for item in gu_weight]
     for b in range(1, block_count):
-        down_t.append(gathered(down_weight[b].T))
-    mod_all = mods.reshape(head_size, block_count, image_count, -1)
-    modulation = [
-        jnp.concatenate([mod_all[index, b] for index in range(head_size)], axis=1)
-        for b in range(block_count)
-    ]
+        down_t.append(gathered(down_flat[b]))
+    modulation = [table[b * image_count : (b + 1) * image_count] for b in range(block_count)]
     last = block_count - 1
-    all_images = image_ids.reshape(-1)
     owner = own_images[:, None]
-    every_token = spread(tokens).astype(jnp.float32)
-    normed, inverse = normalize(every_token)
-    shift, scale = [piece_of(modulation[0], all_images, index) for index in range(2)]
-    input_attn = (normed * (1.0 + scale) + shift).astype(jnp.bfloat16)
-    normed_attn, inverse_attn = [normed[:own_rows]], [inverse[:own_rows]]
+    input_attn = input_attn.reshape(-1, input_attn.shape[-1])
+    normed_attn, inverse_attn = [normed], [inverse]
     inputs_attn = [input_attn]
-    gate = piece_of(modulation[last], all_images, 5)
-    mlp_grads = (gate * spread(cotangent).astype(jnp.float32)).astype(jnp.bfloat16)
-    mlp_grads = mlp_grads.reshape(head_size, own_rows, -1)
     residual = tokens.astype(jnp.float32)
     attentions, attended = [], []
     for b in range(block_count):
@@ -1644,7 +1703,8 @@
                 modulation[b],
                 modulation[b + 1],
                 weights,
-                [qkv_weight[b + 1], proj_weight[b + 1].T],
+                b + 1,
+                [qkv_weight, proj_flat],
             )
             normed_attn.append(next_normed)
             inverse_attn.append(next_inverse)
@@ -1744,14 +1804,13 @@
         ),
         [item.reshape(row_size, shard_rows, -1) for item in (qkv_grad, proj_grad)],
     )
-    gu_grad, mlp_sum = lax.optimization_barrier((gu_grad, mlp_sum))
-    gu_outs[0] = scattered(gu_grad)
     gathered_branch = gathered_branch.reshape(-1, gathered_branch.shape[-1])
     grad_packed, bias_sums[0] = attention_back(grad_attended, attentions[0], image_ids, geometry)
+    grad_packed, mlp_sum, gu_grad = lax.optimization_barrier((grad_packed, mlp_sum, gu_grad))
+    gu_outs[0] = scattered(gu_grad)
     late = late_sums(grad_middle, branch, incoming, normed_mlp, grad_input_mlp, mlp_out)
     image_sums[0] = jnp.concatenate([jnp.zeros_like(late[0])] * 2 + late, axis=1)
     gu_outs[1] = mlp_sum[:, : 2 * units]
-    block_sums[1] = [mlp_sum[:, 2 * units :]] + block_sums[1]
     sheets = jnp.stack(image_sums).reshape(block_count * image_count, head_size, -1)
     sheets = sheets.transpose(1, 0, 2)
     wide = sheets.shape[-1]
@@ -1782,7 +1841,7 @@
     logistic = jax.nn.sigmoid(cond_wide)
     factor = logistic * (1.0 + cond_wide * (1.0 - logistic))
     factor = jnp.pad(factor, ((0, -image_count % 8), (0, 0)))
-    tokens_grad, ada_grads, ada_bias_grads, qkv_bias_out, cond_grad, *block_sums[0] = finish_call(
+    tokens_grad, ada_grads, ada_bias_grads, qkv_bias_out, cond_grad, *stacked = finish_call(
         row_size,
         head_size,
         image_count,
@@ -1803,6 +1862,7 @@
         jnp.stack(mine),
         ada_weight,
         factor,
+        [mlp_sum[:, 2 * units :]] + block_sums[1],
         down_grad.reshape(row_size, shard_rows, -1),
     )
     cond_grad = cond_grad[:image_count]
@@ -1812,11 +1872,11 @@
         cond_grad,
         ada_grads,
         ada_bias_grads,
-        jnp.stack([item[1] for item in block_sums]),
+        stacked[1],
         qkv_bias_out,
-        jnp.stack([item[2].T for item in block_sums]),
+        stacked[2].transpose(0, 2, 1),
         jnp.stack([item.reshape(gu_weight.shape[1:]) for item in gu_outs]),
-        jnp.stack([item[0].T for item in block_sums]),
+        stacked[0].transpose(0, 2, 1),
     )
 
 

time: 666 us -> 637 us (0.956)
  Pallas kernels: 458 us -> 483 us
  waiting for transfers between devices: 24.4 us -> 2.59 us
  other arithmetic: 47.3 us -> 26.7 us
    reduce_scatter x2, waiting for transfers between devices: 24.3 us -> 2.5 us  [scattered(): lax.psum_scatter(grad, 'rows', scatter_dimension=0, tiled=True)]
    pallas_call x1, Pallas kernels: 111 us -> 130 us  [finish_call(): pl.pallas_call(functools.partial(finish_kernel, row_size, head_size, imag...]
    pallas_call x1, Pallas kernels: 113 us -> 127 us  [start_call(): pl.pallas_call(functools.partial(start_kernel, row_size, head_size, image...]
    pallas_call x1, Pallas kernels: 82.9 us -> 74.7 us  [mlp_call(): pl.pallas_call(functools.partial(mlp_kernel, row_size, head_size, pieces,...]
    unnamed x223 -> x198, local copies, waits for them, and re-layouts: 27.2 us -> 28.7 us
  transfers between devices with their start and end apart: 8 -> 6, of which waited for: 1 -> 1; matrix products, arithmetic and copies ran while one was open for 18% -> 15% of each run, Pallas kernels for 58% -> 64%
where the time goes in v6:
time: 637 us; the launch traced here: 631 us
  Pallas kernels  483 us (76%)
  local copies, waits for them, and re-layouts  55.6 us (9%)
  matrix products  47.2 us (7%)
  other arithmetic  26.7 us (4%)
  between operations  15.4 us (2%)
    pallas_call x1, Pallas kernels, finish_call(): pl.pallas_call(functools.partial(finish_kernel, row_size, head_size, imag...  130 us
    pallas_call x1, Pallas kernels, start_call(): pl.pallas_call(functools.partial(start_kernel, row_size, head_size, image...  127 us
    pallas_call x1, Pallas kernels, last_mlp_call(): pl.pallas_call(functools.partial(last_mlp_kernel, row_size, head_size, pi...  79.8 us
    pallas_call x1, Pallas kernels, mlp_call(): pl.pallas_call(functools.partial(mlp_kernel, row_size, head_size, pieces,...  74.7 us
    pallas_call x1, Pallas kernels, mlp_back_call(): pl.pallas_call(functools.partial(mlp_back_kernel, row_size, head_size, pi...  65.6 us
    unnamed x198, local copies, waits for them, and re-layouts  28.7 us
  transfers between devices with their start and end apart: 6, of which 1 were waited for; matrix products, arithmetic and copies ran while one was open for 15% of the time, Pallas kernels for 64%

profile of v6, /device:TPU:0, one launch (start us, length us, event | category | flops | bytes accessed | tf_op | source)
XLA Modules:
  0.0 631.4 jit_solution(18062748551537468220)
XLA Ops:
  7.2 1.8 fusion.93
  18.5 126.8 %start.1 = (bf16[16,72,1728]{2,1,0:T(8,128)(2,1)}, bf16[16,72,576]{2,1,0:T(8,128)(2,1)}, bf16[16,72,1536]{2,1,0:T(8,128)(2,1)}, f32[8,6912]{1,0:T(8,128)S(1)}, b...) custom-call(bf16[16,1152]{1,0:T(8,128)(2,1)S(1)} %pad.31.refs_0_, ...), custom_call_target="tpu_custom_call" | custom-call | tf_op jit(solution)/shard_map/start/pallas_call | solution.py:472
  145.7 5.0 convolution_add_fusion.1
  153.2 1.9 fusion.95
  156.4 2.1 copy-done.16
  158.5 1.5 fusion.23
  161.9 74.7 %mlp.1 = (f32[256,1152]{1,0:T(8,128)}, f32[256,1152]{1,0:T(8,128)}, bf16[2,256,1152]{2,1,0:T(8,128)(2,1)}, f32[512,3072]{1,0:T(8,128)}, bf16[512,1536]{1,0:T(8,1...) custom-call(bf16[512,576]{1,0:T(8,128)(2,1)} %copy.79.refs_0_.refs_3, ...), custom_call_target="tpu_custom_call" | custom-call | tf_op jit(solution)/shard_map/mlp/pallas_call | solution.py:1101
  236.5 5.2 convolution_add_fusion
  242.8 1.9 fusion.96
  246.0 2.1 copy-done.17
  248.1 1.5 fusion.22
  250.7 79.8 %last_mlp.1 = (bf16[256,1152]{1,0:T(8,128)(2,1)}, f32[256,1152]{1,0:T(8,128)}, f32[256,1152]{1,0:T(8,128)}, f32[256,1152]{1,0:T(8,128)}, f32[256,1152]{1,0:T(8,1...) custom-call(bf16[512,576]{1,0:T(8,128)(2,1)} %copy.85.refs_0_.refs_3, ...), custom_call_target="tpu_custom_call" | custom-call | tf_op jit(solution)/shard_map/last_mlp/pallas_call | solution.py:1436
  332.3 5.2 multiply_reduce_fusion.1
  337.7 1.7 slice-done.3
  339.4 2.5 multiply_convert_fusion.1
  345.2 1.5 fusion.15
  349.3 2.6 copy.94.refs_1_
  351.9 5.0 convolution_convert_fusion
  358.8 6.5 %weight_grads.1 = (bf16[1152,1728]{1,0:T(8,128)(2,1)}, bf16[1152,576]{1,0:T(8,128)(2,1)S(1)}) custom-call(bf16[512,1152]{1,0:T(8,128)(2,1)S(1)} %bitcast.182, bf16[512,1728]{1,0:T(8,128)(2,1)} %copy.94.refs_1_, bf16[512,1152]{1,0:T(8,128)(2,1)S(1)} %bitcast.183, bf16[512,576]{1,0:T(8,128)(2,1)S(1)} %copy-done.3), custom_call_target="tpu_custom_call" | custom-call | flops 2717908992 | bytes 10027008 | tf_op jit(solution)/shard_map/weight_grads/pallas_call | solution.py:529
  371.9 3.3 fusion.89
  376.5 65.6 %mlp_back.1 = (f32[256,1152]{1,0:T(8,128)}, f32[256,1152]{1,0:T(8,128)}, bf16[2,256,1152]{2,1,0:T(8,128)(2,1)}, bf16[512,576]{1,0:T(8,128)(2,1)}, bf16[1152,3072...) custom-call(f32[256,1152]{1,0:T(8,128)} %multiply_add_fusion.refs_0_, ...), custom_call_target="tpu_custom_call" | custom-call | tf_op jit(solution)/shard_map/mlp_back/pallas_call | solution.py:1271
  443.5 5.1 multiply_reduce_fusion
  449.9 2.7 multiply_convert_fusion
  457.0 1.5 fusion.12
  460.3 2.5 reduce-scatter.3.cloned.1.call-done
  462.8 2.3 convert_element_type.284
  467.1 1.5 convolution_dynamic-update-slice_fusion.1
  468.6 1.7 convolution_dynamic-update-slice_fusion
  478.0 2.4 copy.107.refs_0_
  481.1 129.6 %finish.1 = (f32[256,1152]{1,0:T(8,128)}, f32[2,72,3456]{2,1,0:T(8,128)}, f32[2,3456]{1,0:T(2,128)}, f32[2,1728]{1,0:T(2,128)}, f32[8,1152]{1,0:T(8,128)}, /*ind...) custom-call(bf16[512,1728]{1,0:T(8,128)(2,1)} %copy.107.refs_0_, bf16[1152,1728]{1,0:T(8,128)(2,1)} %bitcast.202, ...), custom_call_target="tpu_custom_call" | custom-call | tf_op jit(solution)/shard_map/finish/pallas_call | solution.py:774
  612.1 1.9 reshape.1034
  614.0 2.0 pad_maximum_fusion
  (321 shorter events, 64.8 us)
Async XLA Ops:
  7.2 154.7 %all-gather.5.cloned.1.call-start = ((), (), s32[]{:S(2)}) async-start(), calls=%async_computation.2 | async-start | bytes 7520256 | tf_op jit(solution)/shard_map/all_gather | solution.py:1645
  9.9 3.0 copy-start.83
  9.9 3.7 copy-start.75
  9.9 240.8 %all-gather.9.cloned.1.call-start = ((), (), s32[]{:S(2)}) async-start(), calls=%async_computation.6 | async-start | bytes 3760128 | tf_op jit(solution)/shard_map/all_gather | solution.py:1645
  10.7 240.0 %all-gather.7.cloned.1.call-start = ((), (), s32[]{:S(2)}) async-start(), calls=%async_computation.3 | async-start | bytes 7520256 | tf_op jit(solution)/shard_map/all_gather | solution.py:1645
  10.7 5.7 copy-start.4
  11.6 451.2 %reduce-scatter.3.cloned.1.call-start = ((), (), s32[]{:S(2)}) async-start(), calls=%async_computation.4 | async-start | bytes 11280384 | tf_op jit(solution)/shard_map/reduce_scatter | solution.py:1738
  14.3 3.2 copy-start.76
  18.5 126.9 %copy-start.72 = (bf16[2,1728]{1,0:T(2,128)(2,1)S(1)}, bf16[2,1728]{1,0:T(2,128)(2,1)}, u32[]{:S(2)}) copy-start(bf16[2,1728]{1,0:T(2,128)(2,1)} %param.21) | copy-start | bytes 20740
  145.4 5.3 copy-start.7
  145.4 5.3 copy-start.11
  145.4 5.3 copy-start.13
  150.6 5.7 copy-start.30
  155.2 3.3 copy-start.16
  241.7 4.2 copy-start.31
  244.7 3.3 copy-start.17
  330.6 281.5 %reduce-scatter.5.cloned.1.call-start = ((), (), s32[]{:S(2)}) async-start(), calls=%async_computation.5 | async-start | bytes 7520256 | tf_op jit(solution)/shard_map/reduce_scatter | solution.py:1738
  332.2 5.4 slice-start.2
  332.3 7.1 %slice-start.3 = ((s8[8388608]{0:T(1024)(128)(4,1)}), s8[4194304]{0:T(1024)(128)(4,1)S(1)}, s32[]{:S(2)}) async-start(s8[8388608]{0:T(1024)(128)(4,1)} %bitcast.186), calls=%async_computation.10 | async-start | bytes 8388608
  351.9 5.7 copy-start.32
  351.9 6.7 %copy-start.65 = (f32[256,1]{1,0:T(8,128)S(1)}, f32[256,1]{1,0:T(8,128)}, u32[]{:S(2)}) copy-start(f32[256,1]{1,0:T(8,128)} %get-tuple-element.90) | copy-start | bytes 3076
  351.9 6.8 %copy-start.15 = (bf16[2,256,1152]{2,1,0:T(8,128)(2,1)S(1)}, bf16[2,256,1152]{2,1,0:T(8,128)(2,1)}, u32[]{:S(2)}) copy-start(bf16[2,256,1152]{2,1,0:T(8,128)(2,1)} %get-tuple-element.92) | copy-start | bytes 3538948
  356.9 14.9 %collective-permute-start = (bf16[256,1152]{1,0:T(8,128)(2,1)}, bf16[256,1152]{1,0:T(8,128)(2,1)}, u32[]{:S(2)}, u32[]{:S(2)}) collective-permute-start(bf16[256,1152]{1,0:T(8,128)(2,1)} %convolution_convert_fusion), channel_id=1, source_target_pairs={{0,1},{1,0},{2,3},{3,2},{4,5},{5,4},{6,7},{7,6},{8,9},{9,8},{10,11... | collective-permute-start | bytes 1769480 | tf_op jit(solution)/shard_map/ppermute | solution.py:51
  358.7 6.5 %copy-start.1 = (bf16[256,1152]{1,0:T(8,128)(2,1)S(1)}, bf16[256,1152]{1,0:T(8,128)(2,1)}, u32[]{:S(2)}) copy-start(bf16[256,1152]{1,0:T(8,128)(2,1)} %refs_4_.3) | copy-start | bytes 1769476
  358.7 6.5 %copy-start.41 = (f32[256,1152]{1,0:T(8,128)S(1)}, f32[256,1152]{1,0:T(8,128)}, u32[]{:S(2)}) copy-start(f32[256,1152]{1,0:T(8,128)} %get-tuple-element.98) | copy-start | bytes 3538948
  358.7 6.9 %copy-start.39 = (f32[256,1152]{1,0:T(8,128)S(1)}, f32[256,1152]{1,0:T(8,128)}, u32[]{:S(2)}) copy-start(f32[256,1152]{1,0:T(8,128)} %get-tuple-element.95) | copy-start | bytes 3538948
  358.8 10.7 %copy-start.85 = (bf16[16,72,1728]{2,1,0:T(8,128)(2,1)S(1)}, bf16[16,72,1728]{2,1,0:T(8,128)(2,1)}, u32[]{:S(2)}) copy-start(bf16[16,72,1728]{2,1,0:T(8,128)(2,1)} %get-tuple-element.84) | copy-start | bytes 11943940
  371.8 3.4 copy-start.20
  443.5 5.1 slice-start
  443.5 6.4 %slice-start.1 = ((s8[8388608]{0:T(1024)(128)(4,1)}), s8[4194304]{0:T(1024)(128)(4,1)S(1)}, s32[]{:S(2)}) async-start(s8[8388608]{0:T(1024)(128)(4,1)} %bitcast.184), calls=%async_computation.8 | async-start | bytes 8388608
  449.9 2.8 copy-start.59
  449.9 2.8 copy-start.61
  (65 other events, 109.5 us)
Sparse Core Ops, SparseCore 0:
  10.9 103.3 all-gather.4
  117.1 48.5 all-gather.8
  168.5 73.0 all-gather.6
  330.7 132.0 reduce-scatter.2
  466.6 137.2 reduce-scatter.4

commit v7 on v6

--- a/solution.py
+++ b/solution.py
@@ -365,7 +365,6 @@
     for raw in raws:
         for by in range(1, head_size):
             raw.start(by)
-    bulk[0].begin()
     hops = range(1, place.sizes[0])
     for k in hops:
         lead.first(k)
@@ -386,13 +385,14 @@
         part[:, b * images : (b + 1) * images, :] = value.reshape(row_size, pad, -1)[:, :images]
     sums = Scatter(place, part, total, held, met, side, far, mod_send, mod_recv, mod_load)
     sums.begin()
+    sums.first()
+    bulk[0].begin()
+    sums.second()
     bulk[0].first(1)
     for item in bulk[1:]:
         item.begin()
-    sums.first()
     for k in hops[1:]:
         bulk[0].first(k)
-    sums.second()
     for item in bulk[1:]:
         for k in hops:
             item.first(k)
@@ -706,7 +706,6 @@
     lead.begin()
     for k in range(1, place.sizes[0]):
         lead.first(k)
-    items[1].first()
     items[0].second()
     lead.second()
     lead.finish()
@@ -732,16 +731,17 @@
     sums = Scatter(place, part, total, held, met, side, far, cond_send, cond_recv, cond_load)
     sums.begin()
     sums.first()
+    items[1].first()
     items[2].first()
+    sums.second()
     items[1].second()
-    sums.second()
-    items[2].second()
     sums.finish()
     last = Across(
         place, lambda by: total, lambda by: cond_in.at[by - 1], head_send, head_recv, 2
     )
     for by in range(1, head_size):
         last.start(by)
+    items[2].second()
     for item in items:
         item.finish()
     value = total[...]

time: 637 us -> 629 us (0.987)
  Pallas kernels: 483 us -> 474 us
    pallas_call x1, Pallas kernels: 127 us -> 115 us  [start_call(): pl.pallas_call(functools.partial(start_kernel, row_size, head_size, image...]
  transfers between devices with their start and end apart: 6 -> 6, of which waited for: 1 -> 1; matrix products, arithmetic and copies ran while one was open for 15% -> 15% of each run, Pallas kernels for 64% -> 63%
where the time goes in v7:
time: 629 us; the launch traced here: 623 us
  Pallas kernels  474 us (75%)
  local copies, waits for them, and re-layouts  55.6 us (9%)
  matrix products  47.1 us (7%)
  other arithmetic  26.7 us (4%)
  between operations  15.4 us (2%)
    pallas_call x1, Pallas kernels, finish_call(): pl.pallas_call(functools.partial(finish_kernel, row_size, head_size, imag...  132 us
    pallas_call x1, Pallas kernels, start_call(): pl.pallas_call(functools.partial(start_kernel, row_size, head_size, image...  115 us
    pallas_call x1, Pallas kernels, last_mlp_call(): pl.pallas_call(functools.partial(last_mlp_kernel, row_size, head_size, pi...  79.1 us
    pallas_call x1, Pallas kernels, mlp_call(): pl.pallas_call(functools.partial(mlp_kernel, row_size, head_size, pieces,...  74.7 us
    pallas_call x1, Pallas kernels, mlp_back_call(): pl.pallas_call(functools.partial(mlp_back_kernel, row_size, head_size, pi...  66.2 us
    unnamed x198, local copies, waits for them, and re-layouts  28.7 us
  transfers between devices with their start and end apart: 6, of which 1 were waited for; matrix products, arithmetic and copies ran while one was open for 15% of the time, Pallas kernels for 63%

profile of v7, /device:TPU:0, one launch (start us, length us, event | category | flops | bytes accessed | tf_op | source)
XLA Modules:
  0.0 623.3 jit_solution(8097150094241284595)
XLA Ops:
  7.2 1.8 fusion.93
  18.5 115.5 %start.1 = (bf16[16,72,1728]{2,1,0:T(8,128)(2,1)}, bf16[16,72,576]{2,1,0:T(8,128)(2,1)}, bf16[16,72,1536]{2,1,0:T(8,128)(2,1)}, f32[8,6912]{1,0:T(8,128)S(1)}, b...) custom-call(bf16[16,1152]{1,0:T(8,128)(2,1)S(1)} %pad.31.refs_0_, ...), custom_call_target="tpu_custom_call" | custom-call | tf_op jit(solution)/shard_map/start/pallas_call | solution.py:472
  134.3 5.0 convolution_add_fusion.1
  141.8 1.9 fusion.95
  145.0 2.1 copy-done.16
  147.1 1.5 fusion.23
  150.5 74.7 %mlp.1 = (f32[256,1152]{1,0:T(8,128)}, f32[256,1152]{1,0:T(8,128)}, bf16[2,256,1152]{2,1,0:T(8,128)(2,1)}, f32[512,3072]{1,0:T(8,128)}, bf16[512,1536]{1,0:T(8,1...) custom-call(bf16[512,576]{1,0:T(8,128)(2,1)} %copy.79.refs_0_.refs_3, ...), custom_call_target="tpu_custom_call" | custom-call | tf_op jit(solution)/shard_map/mlp/pallas_call | solution.py:1101
  225.2 5.2 convolution_add_fusion
  231.5 1.9 fusion.96
  234.6 2.1 copy-done.17
  236.8 1.5 fusion.22
  239.4 79.1 %last_mlp.1 = (bf16[256,1152]{1,0:T(8,128)(2,1)}, f32[256,1152]{1,0:T(8,128)}, f32[256,1152]{1,0:T(8,128)}, f32[256,1152]{1,0:T(8,128)}, f32[256,1152]{1,0:T(8,1...) custom-call(bf16[512,576]{1,0:T(8,128)(2,1)} %copy.85.refs_0_.refs_3, ...), custom_call_target="tpu_custom_call" | custom-call | tf_op jit(solution)/shard_map/last_mlp/pallas_call | solution.py:1436
  320.2 5.0 multiply_reduce_fusion.1
  325.6 1.5 slice-done.3
  327.1 2.5 multiply_convert_fusion.1
  333.0 1.5 fusion.15
  337.1 2.6 copy.94.refs_1_
  339.7 5.1 convolution_convert_fusion
  344.7 2.1 collective-permute-start
  348.0 6.2 %weight_grads.1 = (bf16[1152,1728]{1,0:T(8,128)(2,1)}, bf16[1152,576]{1,0:T(8,128)(2,1)S(1)}) custom-call(bf16[512,1152]{1,0:T(8,128)(2,1)S(1)} %bitcast.182, bf16[512,1728]{1,0:T(8,128)(2,1)} %copy.94.refs_1_, bf16[512,1152]{1,0:T(8,128)(2,1)S(1)} %bitcast.183, bf16[512,576]{1,0:T(8,128)(2,1)S(1)} %copy-done.3), custom_call_target="tpu_custom_call" | custom-call | flops 2717908992 | bytes 10027008 | tf_op jit(solution)/shard_map/weight_grads/pallas_call | solution.py:529
  360.8 3.3 fusion.89
  365.4 66.2 %mlp_back.1 = (f32[256,1152]{1,0:T(8,128)}, f32[256,1152]{1,0:T(8,128)}, bf16[2,256,1152]{2,1,0:T(8,128)(2,1)}, bf16[512,576]{1,0:T(8,128)(2,1)}, bf16[1152,3072...) custom-call(f32[256,1152]{1,0:T(8,128)} %multiply_add_fusion.refs_0_, ...), custom_call_target="tpu_custom_call" | custom-call | tf_op jit(solution)/shard_map/mlp_back/pallas_call | solution.py:1271
  433.0 5.0 multiply_reduce_fusion
  439.4 2.7 multiply_convert_fusion
  449.8 2.6 reduce-scatter.3.cloned.1.call-done
  452.4 2.3 convert_element_type.284
  456.8 1.5 convolution_dynamic-update-slice_fusion.1
  458.2 1.7 convolution_dynamic-update-slice_fusion
  467.6 2.4 copy.107.refs_0_
  470.7 131.9 %finish.1 = (f32[256,1152]{1,0:T(8,128)}, f32[2,72,3456]{2,1,0:T(8,128)}, f32[2,3456]{1,0:T(2,128)}, f32[2,1728]{1,0:T(2,128)}, f32[8,1152]{1,0:T(8,128)}, /*ind...) custom-call(bf16[512,1728]{1,0:T(8,128)(2,1)} %copy.107.refs_0_, bf16[1152,1728]{1,0:T(8,128)(2,1)} %bitcast.202, ...), custom_call_target="tpu_custom_call" | custom-call | tf_op jit(solution)/shard_map/finish/pallas_call | solution.py:774
  604.0 1.9 reshape.1034
  605.9 2.0 pad_maximum_fusion
  (321 shorter events, 65.7 us)
Async XLA Ops:
  7.2 143.3 %all-gather.5.cloned.1.call-start = ((), (), s32[]{:S(2)}) async-start(), calls=%async_computation.2 | async-start | bytes 7520256 | tf_op jit(solution)/shard_map/all_gather | solution.py:1645
  9.9 3.0 copy-start.83
  9.9 3.7 copy-start.75
  9.9 229.5 %all-gather.9.cloned.1.call-start = ((), (), s32[]{:S(2)}) async-start(), calls=%async_computation.6 | async-start | bytes 3760128 | tf_op jit(solution)/shard_map/all_gather | solution.py:1645
  10.7 228.7 %all-gather.7.cloned.1.call-start = ((), (), s32[]{:S(2)}) async-start(), calls=%async_computation.3 | async-start | bytes 7520256 | tf_op jit(solution)/shard_map/all_gather | solution.py:1645
  10.7 5.7 copy-start.4
  11.6 440.8 %reduce-scatter.3.cloned.1.call-start = ((), (), s32[]{:S(2)}) async-start(), calls=%async_computation.4 | async-start | bytes 11280384 | tf_op jit(solution)/shard_map/reduce_scatter | solution.py:1738
  14.3 3.2 copy-start.76
  18.5 115.5 %copy-start.72 = (bf16[2,1728]{1,0:T(2,128)(2,1)S(1)}, bf16[2,1728]{1,0:T(2,128)(2,1)}, u32[]{:S(2)}) copy-start(bf16[2,1728]{1,0:T(2,128)(2,1)} %param.21) | copy-start | bytes 20740
  134.0 5.3 copy-start.7
  134.0 5.3 copy-start.11
  134.0 5.3 copy-start.13
  139.3 5.7 copy-start.30
  143.8 3.3 copy-start.16
  230.4 4.2 copy-start.31
  233.4 3.3 copy-start.17
  318.5 285.5 %reduce-scatter.5.cloned.1.call-start = ((), (), s32[]{:S(2)}) async-start(), calls=%async_computation.5 | async-start | bytes 7520256 | tf_op jit(solution)/shard_map/reduce_scatter | solution.py:1738
  320.2 5.4 slice-start.2
  320.2 6.9 %slice-start.3 = ((s8[8388608]{0:T(1024)(128)(4,1)}), s8[4194304]{0:T(1024)(128)(4,1)S(1)}, s32[]{:S(2)}) async-start(s8[8388608]{0:T(1024)(128)(4,1)} %bitcast.186), calls=%async_computation.10 | async-start | bytes 8388608
  339.6 7.2 %copy-start.32 = (bf16[1,256,8,3,72]{1,4,2,3,0:T(8,128)(2,1)S(1)}, bf16[1,256,8,3,72]{1,4,2,3,0:T(8,128)(2,1)}, u32[]{:S(2)}) copy-start(bf16[1,256,8,3,72]{1,4,2,3,0:T(8,128)(2,1)} %get-tuple-element.160) | copy-start | bytes 2654212
  339.6 8.1 %copy-start.65 = (f32[256,1]{1,0:T(8,128)S(1)}, f32[256,1]{1,0:T(8,128)}, u32[]{:S(2)}) copy-start(f32[256,1]{1,0:T(8,128)} %get-tuple-element.90) | copy-start | bytes 3076
  339.7 8.2 %copy-start.15 = (bf16[2,256,1152]{2,1,0:T(8,128)(2,1)S(1)}, bf16[2,256,1152]{2,1,0:T(8,128)(2,1)}, u32[]{:S(2)}) copy-start(bf16[2,256,1152]{2,1,0:T(8,128)(2,1)} %get-tuple-element.92) | copy-start | bytes 3538948
  344.7 3.2 copy-start.3
  344.7 3.2 copy-start.14
  344.7 16.0 %collective-permute-start = (bf16[256,1152]{1,0:T(8,128)(2,1)}, bf16[256,1152]{1,0:T(8,128)(2,1)}, u32[]{:S(2)}, u32[]{:S(2)}) collective-permute-start(bf16[256,1152]{1,0:T(8,128)(2,1)} %convolution_convert_fusion), channel_id=1, source_target_pairs={{0,1},{1,0},{2,3},{3,2},{4,5},{5,4},{6,7},{7,6},{8,9},{9,8},{10,11... | collective-permute-start | bytes 1769480 | tf_op jit(solution)/shard_map/ppermute | solution.py:51
  347.9 6.3 %copy-start.1 = (bf16[256,1152]{1,0:T(8,128)(2,1)S(1)}, bf16[256,1152]{1,0:T(8,128)(2,1)}, u32[]{:S(2)}) copy-start(bf16[256,1152]{1,0:T(8,128)(2,1)} %refs_4_.3) | copy-start | bytes 1769476
  347.9 6.3 %copy-start.41 = (f32[256,1152]{1,0:T(8,128)S(1)}, f32[256,1152]{1,0:T(8,128)}, u32[]{:S(2)}) copy-start(f32[256,1152]{1,0:T(8,128)} %get-tuple-element.98) | copy-start | bytes 3538948
  347.9 6.7 %copy-start.39 = (f32[256,1152]{1,0:T(8,128)S(1)}, f32[256,1152]{1,0:T(8,128)}, u32[]{:S(2)}) copy-start(f32[256,1152]{1,0:T(8,128)} %get-tuple-element.95) | copy-start | bytes 3538948
  347.9 10.4 %copy-start.85 = (bf16[16,72,1728]{2,1,0:T(8,128)(2,1)S(1)}, bf16[16,72,1728]{2,1,0:T(8,128)(2,1)}, u32[]{:S(2)}) copy-start(bf16[16,72,1728]{2,1,0:T(8,128)(2,1)} %get-tuple-element.84) | copy-start | bytes 11943940
  360.7 3.4 copy-start.20
  433.0 5.1 slice-start
  433.0 6.4 %slice-start.1 = ((s8[8388608]{0:T(1024)(128)(4,1)}), s8[4194304]{0:T(1024)(128)(4,1)S(1)}, s32[]{:S(2)}) async-start(s8[8388608]{0:T(1024)(128)(4,1)} %bitcast.184), calls=%async_computation.8 | async-start | bytes 8388608
  (65 other events, 111.4 us)
Sparse Core Ops, SparseCore 0:
  10.9 95.0 all-gather.4
  108.8 49.4 all-gather.8
  161.2 71.4 all-gather.6
  318.6 133.7 reduce-scatter.2
  456.3 136.5 reduce-scatter.4

commit v8 on v7

--- a/solution.py
+++ b/solution.py
@@ -511,6 +511,36 @@
     )(cond, ada, bias, tokens, cotangent, owner, *shards)
 
 
+def head_part_kernel(begin, packed, weight, out):
+    rows, width = out.shape
+    size = tile_of(width)
+
+    def body(step, at):
+        out[:, pl.ds(at, size)] = dot_nt(
+            packed[pl.ds(begin, rows), :], weight[pl.ds(at, size), :]
+        ).astype(out.dtype)
+
+    tiles(width, size, body)
+
+
+def head_part(packed, weight, rows, slot, dtype):
+    vmem = pl.BlockSpec(memory_space=pltpu.VMEM)
+    width, depth = weight.shape
+    return pl.pallas_call(
+        functools.partial(head_part_kernel, slot * rows),
+        out_shape=jax.ShapeDtypeStruct((rows, width), dtype),
+        in_specs=[vmem] * 2,
+        out_specs=vmem,
+        compiler_params=pltpu.CompilerParams(vmem_limit_bytes=32 * 2**20),
+        cost_estimate=pl.CostEstimate(
+            flops=2 * rows * width * depth,
+            bytes_accessed=2 * (packed.size + weight.size) + 4 * rows * width,
+            transcendentals=0,
+        ),
+        name="head_part",
+    )(packed, weight)
+
+
 def weight_grads_kernel(*refs):
     count = len(refs) // 3
     for i in range(count):
@@ -631,7 +661,7 @@
     step_width = tile_of(width)
     place.greet(True)
     for stack, item in zip(stacks, done):
-        stack[1] = item[...]
+        stack[1] = item[...].astype(jnp.float32)
     items = [
         Scatter(
             place, source, outs[i], *scratch[4 * i : 4 * i + 4], send.at[i], recv.at[i], load.at[i]
@@ -928,7 +958,7 @@
             self.arrive_all(first, p)
             value = self.total(own_part, landed, p)
             branch[at] = value
-            value = residual[at] + self.modulation(table, owner, 2, p) * value
+            value = residual[at].astype(jnp.float32) + self.modulation(table, owner, 2, p) * value
             middle[at] = value
             unit, scale = normalize(value)
             normed[at] = unit
@@ -1541,12 +1571,11 @@
     return jnp.concatenate([values] + arrived, axis=0)
 
 
-def collect(operand, product, own_rows, beside):
-    arrived = []
-    for flip in range(1, lax.axis_size("heads")):
-        partial = product(operand[flip * own_rows : (flip + 1) * own_rows])
-        arrived.append(head_move(partial.astype(jnp.bfloat16), flip))
-    total = product(operand[:own_rows])
+def collect(part, beside):
+    arrived = [
+        head_move(part(flip, jnp.bfloat16), flip) for flip in range(1, lax.axis_size("heads"))
+    ]
+    total = part(0, jnp.float32)
     total, arrived, beside = lax.optimization_barrier((total, arrived, beside))
     for item in arrived:
         total = total + item.astype(jnp.float32)
@@ -1670,7 +1699,7 @@
     input_attn = input_attn.reshape(-1, input_attn.shape[-1])
     normed_attn, inverse_attn = [normed], [inverse]
     inputs_attn = [input_attn]
-    residual = tokens.astype(jnp.float32)
+    residual = tokens
     attentions, attended = [], []
     for b in range(block_count):
         item, kept = attention(
@@ -1735,7 +1764,7 @@
     )
 
     def scattered(grad):
-        return lax.psum_scatter(grad, "rows", scatter_dimension=0, tiled=True).astype(jnp.float32)
+        return lax.psum_scatter(grad, "rows", scatter_dimension=0, tiled=True)
 
     def late_sums(middle, branch, incoming, normed, grad, out):
         return [
@@ -1760,7 +1789,8 @@
         last_out,
     )
     grad_input_attn, (qkv_grad, proj_grad, late) = collect(
-        grad_packed, lambda rows: tail_dot(rows, qkv_full[1]), own_rows, (qkv_grad, proj_grad, late)
+        lambda slot, dtype: head_part(grad_packed, qkv_full[1], own_rows, slot, dtype),
+        (qkv_grad, proj_grad, late),
     )
     scale = piece_of(modulation[1], own_images, 1)
     incoming = grad_middle + norm_back(
@@ -1875,7 +1905,7 @@
         stacked[1],
         qkv_bias_out,
         stacked[2].transpose(0, 2, 1),
-        jnp.stack([item.reshape(gu_weight.shape[1:]) for item in gu_outs]),
+        jnp.stack([item.reshape(gu_weight.shape[1:]).astype(jnp.float32) for item in gu_outs]),
         stacked[0].transpose(0, 2, 1),
     )
 

time: 629 us -> 632 us (level)
  Pallas kernels: 474 us -> 486 us
    pallas_call x0 -> x2, Pallas kernels: none -> 7.39 us  [head_part(): pl.pallas_call(functools.partial(head_part_kernel, slot * rows), out_shap...]
    dot_general x2 -> x0, matrix products: 6.48 us -> none  [tail_dot(): lax.dot_general(operand, other, (((1,), (1,)), ((), ())), preferred_eleme...]
    unnamed x198 -> x208, local copies, waits for them, and re-layouts: 28.7 us -> 28.2 us
  transfers between devices with their start and end apart: 6 -> 6, of which waited for: 1 -> 0; matrix products, arithmetic and copies ran while one was open for 15% -> 14% of each run, Pallas kernels for 63% -> 65%
where the time goes in v8:
time: 632 us; the launch traced here: 622 us
  Pallas kernels  486 us (77%)
  local copies, waits for them, and re-layouts  52.5 us (8%)
  matrix products  42.7 us (7%)
  other arithmetic  22.8 us (4%)
  between operations  15.6 us (2%)
    pallas_call x1, Pallas kernels, finish_call(): pl.pallas_call(functools.partial(finish_kernel, row_size, head_size, imag...  135 us
    pallas_call x1, Pallas kernels, start_call(): pl.pallas_call(functools.partial(start_kernel, row_size, head_size, image...  115 us
    pallas_call x1, Pallas kernels, last_mlp_call(): pl.pallas_call(functools.partial(last_mlp_kernel, row_size, head_size, pi...  80.5 us
    pallas_call x1, Pallas kernels, mlp_back_call(): pl.pallas_call(functools.partial(mlp_back_kernel, row_size, head_size, pi...  72.3 us
    pallas_call x1, Pallas kernels, mlp_call(): pl.pallas_call(functools.partial(mlp_kernel, row_size, head_size, pieces,...  69.8 us
    unnamed x208, local copies, waits for them, and re-layouts  28.2 us
  transfers between devices with their start and end apart: 6, of which 0 were waited for; matrix products, arithmetic and copies ran while one was open for 14% of the time, Pallas kernels for 65%

profile of v8, /device:TPU:0, one launch (start us, length us, event | category | flops | bytes accessed | tf_op | source)
XLA Modules:
  0.0 622.1 jit_solution(17347541455455358763)
XLA Ops:
  7.2 1.8 fusion.92
  17.5 114.9 %start.1 = (bf16[16,72,1728]{2,1,0:T(8,128)(2,1)}, bf16[16,72,576]{2,1,0:T(8,128)(2,1)}, bf16[16,72,1536]{2,1,0:T(8,128)(2,1)}, f32[8,6912]{1,0:T(8,128)S(1)}, b...) custom-call(bf16[16,1152]{1,0:T(8,128)(2,1)S(1)} %pad.31.refs_0_, ...), custom_call_target="tpu_custom_call" | custom-call | tf_op jit(solution)/shard_map/start/pallas_call | solution.py:472
  132.7 4.9 convolution_add_fusion.1
  140.1 2.0 fusion.94
  143.3 2.0 copy-done.20
  145.3 1.5 fusion.23
  148.7 69.8 %mlp.1 = (f32[256,1152]{1,0:T(8,128)}, f32[256,1152]{1,0:T(8,128)}, bf16[2,256,1152]{2,1,0:T(8,128)(2,1)}, f32[512,3072]{1,0:T(8,128)}, bf16[512,1536]{1,0:T(8,1...) custom-call(bf16[512,576]{1,0:T(8,128)(2,1)} %copy.79.refs_0_.refs_3, ...), custom_call_target="tpu_custom_call" | custom-call | tf_op jit(solution)/shard_map/mlp/pallas_call | solution.py:1131
  218.5 5.4 convolution_add_fusion
  225.0 1.9 fusion.95
  228.1 2.1 copy-done.21
  230.3 1.5 fusion.22
  232.9 80.5 %last_mlp.1 = (bf16[256,1152]{1,0:T(8,128)(2,1)}, f32[256,1152]{1,0:T(8,128)}, f32[256,1152]{1,0:T(8,128)}, f32[256,1152]{1,0:T(8,128)}, f32[256,1152]{1,0:T(8,1...) custom-call(bf16[512,576]{1,0:T(8,128)(2,1)} %copy.85.refs_0_.refs_3, ...), custom_call_target="tpu_custom_call" | custom-call | tf_op jit(solution)/shard_map/last_mlp/pallas_call | solution.py:1466
  315.1 5.5 multiply_reduce_fusion.1
  321.9 2.5 multiply_convert_fusion.1
  324.4 1.4 fusion.20
  327.7 1.5 fusion.15
  331.0 2.9 copy.92.packed.refs_1_
  333.9 2.7 copy-done
  336.6 3.6 head_part.3
  340.2 2.4 collective-permute-start
  343.6 6.2 %weight_grads.1 = (bf16[1152,1728]{1,0:T(8,128)(2,1)}, bf16[1152,576]{1,0:T(8,128)(2,1)S(1)}) custom-call(bf16[512,1152]{1,0:T(8,128)(2,1)S(1)} %bitcast.179, bf16[512,1728]{1,0:T(8,128)(2,1)} %copy-done.2, bf16[512,1152]{1,0:T(8,128)(2,1)S(1)} %bitcast.180, bf16[512,576]{1,0:T(8,128)(2,1)S(1)} %copy-done.7), custom_call_target="tpu_custom_call" | custom-call | flops 2717908992 | bytes 10027008 | tf_op jit(solution)/shard_map/weight_grads/pallas_call | solution.py:559
  351.0 3.8 head_part.2
  354.9 2.2 fusion.31
  358.6 1.8 fusion.89
  361.8 72.3 %mlp_back.1 = (f32[256,1152]{1,0:T(8,128)}, f32[256,1152]{1,0:T(8,128)}, bf16[2,256,1152]{2,1,0:T(8,128)(2,1)}, bf16[512,576]{1,0:T(8,128)(2,1)}, bf16[1152,3072...) custom-call(f32[256,1152]{1,0:T(8,128)} %multiply_add_fusion.refs_0_, ...), custom_call_target="tpu_custom_call" | custom-call | tf_op jit(solution)/shard_map/mlp_back/pallas_call | solution.py:1301
  435.5 5.0 multiply_reduce_fusion
  441.9 2.8 multiply_convert_fusion
  444.7 1.4 fusion.18
  449.0 1.5 fusion.12
  464.0 2.4 copy.107.refs_0_
  466.7 134.7 %finish.1 = (f32[256,1152]{1,0:T(8,128)}, f32[2,72,3456]{2,1,0:T(8,128)}, f32[2,3456]{1,0:T(2,128)}, f32[2,1728]{1,0:T(2,128)}, f32[8,1152]{1,0:T(8,128)}, /*ind...) custom-call(bf16[512,1728]{1,0:T(8,128)(2,1)} %copy.107.refs_0_, bf16[1152,1728]{1,0:T(8,128)(2,1)} %bitcast.198, ...), custom_call_target="tpu_custom_call" | custom-call | tf_op jit(solution)/shard_map/finish/pallas_call | solution.py:804
  604.2 2.3 maximum_convert_fusion.2
  (326 shorter events, 59.3 us)
Async XLA Ops:
  7.2 141.5 %all-gather.5.cloned.1.call-start = ((), (), s32[]{:S(2)}) async-start(), calls=%async_computation.2 | async-start | bytes 7520256 | tf_op jit(solution)/shard_map/all_gather | solution.py:1674
  9.9 223.0 %all-gather.9.cloned.1.call-start = ((), (), s32[]{:S(2)}) async-start(), calls=%async_computation.6 | async-start | bytes 3760128 | tf_op jit(solution)/shard_map/all_gather | solution.py:1674
  9.9 6.5 %copy-start.14 = (bf16[2,576,72]{1,2,0:T(8,128)(2,1)S(1)}, bf16[2,576,72]{1,2,0:T(8,128)(2,1)}, u32[]{:S(2)}) copy-start(bf16[2,576,72]{1,2,0:T(8,128)(2,1)} %param.22) | copy-start | bytes 497668
  10.7 5.8 copy-start.9
  10.7 222.2 %all-gather.7.cloned.1.call-start = ((), (), s32[]{:S(2)}) async-start(), calls=%async_computation.3 | async-start | bytes 7520256 | tf_op jit(solution)/shard_map/all_gather | solution.py:1674
  10.7 5.0 copy-start.83
  10.7 5.7 copy-start.4
  10.8 5.7 copy-start.6
  10.8 5.7 copy-start.8
  11.6 440.7 %reduce-scatter.3.cloned.1.call-start = ((), (), s32[]{:S(2)}) async-start(), calls=%async_computation.4 | async-start | bytes 11280384 | tf_op jit(solution)/shard_map/reduce_scatter | solution.py:1767
  17.5 114.9 %copy-start.79 = (bf16[2,1728]{1,0:T(2,128)(2,1)S(1)}, bf16[2,1728]{1,0:T(2,128)(2,1)}, u32[]{:S(2)}) copy-start(bf16[2,1728]{1,0:T(2,128)(2,1)} %param.21) | copy-start | bytes 20740
  132.4 5.2 copy-start.11
  132.4 5.2 copy-start.15
  132.4 5.2 copy-start.16
  137.6 5.7 copy-start.32
  223.9 4.2 copy-start.33
  313.4 289.4 %reduce-scatter.5.cloned.1.call-start = ((), (), s32[]{:S(2)}) async-start(), calls=%async_computation.5 | async-start | bytes 7520256 | tf_op jit(solution)/shard_map/reduce_scatter | solution.py:1767
  314.8 12.4 %copy-start.38 = (f32[512,18]{0,1:T(8,128)}, f32[512,18]{0,1:T(8,128)S(1)}, u32[]{:S(2)}) copy-start(f32[512,18]{0,1:T(8,128)S(1)} %broadcast_multiply_fusion.1) | copy-start | bytes 110596
  315.1 5.5 slice-start.2
  315.1 6.8 %slice-start.3 = ((s8[8388608]{0:T(1024)(128)(4,1)}), s8[4194304]{0:T(1024)(128)(4,1)S(1)}, s32[]{:S(2)}) async-start(s8[8388608]{0:T(1024)(128)(4,1)} %bitcast.183), calls=%async_computation.10 | async-start | bytes 8388608
  336.6 6.1 copy-start.29
  336.6 7.0 %copy-start.18 = (bf16[2,256,1152]{2,1,0:T(8,128)(2,1)S(1)}, bf16[2,256,1152]{2,1,0:T(8,128)(2,1)}, u32[]{:S(2)}) copy-start(bf16[2,256,1152]{2,1,0:T(8,128)(2,1)} %get-tuple-element.83) | copy-start | bytes 3538948
  336.6 7.0 %copy-start.19 = (bf16[2,256,1152]{2,1,0:T(8,128)(2,1)S(1)}, bf16[2,256,1152]{2,1,0:T(8,128)(2,1)}, u32[]{:S(2)}) copy-start(bf16[2,256,1152]{2,1,0:T(8,128)(2,1)} %get-tuple-element.92) | copy-start | bytes 3538948
  340.2 18.2 %collective-permute-start = (bf16[256,1152]{1,0:T(8,128)(2,1)S(1)}, bf16[256,1152]{1,0:T(8,128)(2,1)S(1)}, u32[]{:S(2)}, u32[]{:S(2)}) collective-permute-start(bf16[256,1152]{1,0:T(8,128)(2,1)S(1)} %head_part.3), channel_id=1, source_target_pairs={{0,1},{1,0},{2,3},{3,2},{4,5},{5,4},{6,7},{7,6},{8,9},{9,8},{10,11... | collective-permute-start | bytes 1769480 | tf_op jit(solution)/shard_map/ppermute | solution.py:51
  343.6 6.3 %copy-start.5 = (bf16[256,1152]{1,0:T(8,128)(2,1)S(1)}, bf16[256,1152]{1,0:T(8,128)(2,1)}, u32[]{:S(2)}) copy-start(bf16[256,1152]{1,0:T(8,128)(2,1)} %refs_4_.3) | copy-start | bytes 1769476
  343.6 6.3 %copy-start.44 = (f32[256,1152]{1,0:T(8,128)S(1)}, f32[256,1152]{1,0:T(8,128)}, u32[]{:S(2)}) copy-start(f32[256,1152]{1,0:T(8,128)} %get-tuple-element.98) | copy-start | bytes 3538948
  343.6 7.4 %copy-start.1 = (bf16[16,72,1728]{2,1,0:T(8,128)(2,1)S(1)}, bf16[16,72,1728]{2,1,0:T(8,128)(2,1)}, u32[]{:S(2)}) copy-start(bf16[16,72,1728]{2,1,0:T(8,128)(2,1)} %get-tuple-element.84) | copy-start | bytes 11943940
  343.6 7.3 %copy-start.3 = (bf16[512,1728]{1,0:T(8,128)(2,1)S(1)}, bf16[512,1728]{1,0:T(8,128)(2,1)}, u32[]{:S(2)}) copy-start(bf16[512,1728]{1,0:T(8,128)(2,1)} %copy-done.2) | copy-start | bytes 5308420
  349.9 4.9 copy-start.10
  351.0 3.8 copy-start.66
  435.4 5.1 slice-start
  435.4 6.4 %slice-start.1 = ((s8[8388608]{0:T(1024)(128)(4,1)}), s8[4194304]{0:T(1024)(128)(4,1)S(1)}, s32[]{:S(2)}) async-start(s8[8388608]{0:T(1024)(128)(4,1)} %bitcast.181), calls=%async_computation.8 | async-start | bytes 8388608
  (70 other events, 122.1 us)
Sparse Core Ops, SparseCore 0:
  10.9 95.9 all-gather.4
  109.7 50.1 all-gather.8
  162.7 69.9 all-gather.6
  313.6 136.4 reduce-scatter.2
  453.9 141.1 reduce-scatter.4
